TPU v7x, 32 devices: a whole 2x2x4 slice. The times are simulated.
32 devices in a mesh: grp: 4 (over x, core), ctx: 8 (over z, y).
Axes of the slice: x: 2, y: 2, z: 4, core: 2. Of those that a mesh axis runs over, the one named last changes fastest.
Arguments:
- inputs: bfloat16 [4, 4096, 2048], P('grp', 'ctx'), may hold values from -6 to 6
- queries: bfloat16 [4, 4096, 1024], P('grp', 'ctx'), may hold values from -6 to 6
- key_heads: bfloat16 [4, 4096, 1024], P('grp', 'ctx'), may hold values from -6 to 6
- value_heads: bfloat16 [4, 4096, 1024], P('grp', 'ctx'), may hold values from -6 to 6
- out_grad: bfloat16 [4, 4096, 1024], P('grp', 'ctx'), may hold values from -6 to 6
- qkv_weight: bfloat16 [2048, 3072], P('ctx'), may hold values from -0.125 to 0.125
- gate_weight: bfloat16 [32, 2048, 768], P(('grp', 'ctx')), may hold values from -0.125 to 0.125
- up_weight: bfloat16 [32, 2048, 768], P(('grp', 'ctx')), may hold values from -0.125 to 0.125
- down_weight: bfloat16 [32, 768, 2048], P(('grp', 'ctx')), may hold values from -0.21875 to 0.21875
- chosen: int32 [4, 8, 32, 2], P('grp', 'ctx'), may hold values from 0 to 511, as said below
- pad_counts: int32 [4, 8, 32], P('grp', 'ctx'), may hold values from 0 to 2, as said below
- combine: float32 [4, 8, 32, 2], P('grp', 'ctx'), may hold values from 0.05 to 1
Outputs:
- input_grad: bfloat16 [4, 4096, 2048], P('grp', 'ctx')
Inputs may be any that keep to these rules, and one draw needn't show every extreme that they name: `chosen`: local rows of the listing device; the 2 entries of one list are distinct, and its last pad_counts entries are padding. `pad_counts`: counts of padding entries at the end of the matching list of chosen.
All inputs are finite; a program needn't handle non-finite values.
Results may differ from a plain program's by a relative error of at most 0.015.
Values may be sent and summed in bfloat16 or wider, within the bound.
No kernel may reach another device: no remote copies, remote signals or barrier semaphores. Data moves between devices by JAX's collectives and lax.ppermute only.
A program may use at most 192 MiB of HBM per device.

v0:
```python
import math

import jax
import jax.numpy as jnp
from jax import lax
from jax.sharding import PartitionSpec as P

HEADS = 8
DH = 128
BLK = 512


def silu_parts(gate):
    sigma = jax.nn.sigmoid(gate)
    return (gate * sigma, sigma * (1.0 + gate * (1.0 - sigma)))


def expert_front(rows_in, gate_mat, up_mat):
    gate = jnp.dot(rows_in, gate_mat, preferred_element_type=jnp.float32)
    up_proj = jnp.dot(rows_in, up_mat, preferred_element_type=jnp.float32)
    active, slope = silu_parts(gate)
    return (active, up_proj * slope)


def expert_back(rows_grad, weights, active, up_slope, gate_mat, up_mat, down_mat):
    contract = (((1,), (1,)), ((), ()))
    back = lax.dot_general(rows_grad, down_mat, contract, preferred_element_type=jnp.float32)
    hidden_grad = weights[:, None] * back
    up_grad = (hidden_grad * active).astype(jnp.bfloat16)
    gate_grad = (hidden_grad * up_slope).astype(jnp.bfloat16)
    total = lax.dot_general(gate_grad, gate_mat, contract, preferred_element_type=jnp.float32)
    total = total + lax.dot_general(up_grad, up_mat, contract, preferred_element_type=jnp.float32)
    return total.astype(jnp.bfloat16)


def exclusive_sums(states, reverse):
    if reverse:
        states = states[::-1]
    running = jnp.cumsum(states, axis=0)
    shifted = jnp.concatenate([jnp.zeros_like(states), running[:-1]], axis=0)
    if reverse:
        shifted = shifted[::-1]
    return shifted


def split_state(state):
    upper = state.astype(jnp.bfloat16)
    lower = (state - upper.astype(jnp.float32)).astype(jnp.bfloat16)
    return (upper, lower)


def state_product(form, rows, parts):
    first = jnp.einsum(form, rows, parts[0], preferred_element_type=jnp.float32)
    return first + jnp.einsum(form, rows, parts[1], preferred_element_type=jnp.float32)


def block_grads(query_blk, key_blk, value_blk, grad_blk, prefix, suffix, scaling):
    block_rows = query_blk.shape[0]
    causal = lax.broadcasted_iota(jnp.int32, (block_rows, block_rows), 0) >= lax.broadcasted_iota(
        jnp.int32, (block_rows, block_rows), 1
    )
    grad_scores = jnp.einsum(
        "thd,shd->hts", grad_blk, value_blk, preferred_element_type=jnp.float32
    )
    query_scores = jnp.einsum(
        "thd,shd->hts", query_blk, key_blk, preferred_element_type=jnp.float32
    )
    near_grad = jnp.where(causal, scaling * grad_scores, 0.0).astype(jnp.bfloat16)
    near_query = jnp.where(causal, scaling * query_scores, 0.0).astype(jnp.bfloat16)
    prefix_parts = split_state(prefix)
    suffix_parts = split_state(suffix)
    query_grad = jnp.einsum("hts,shd->thd", near_grad, key_blk, preferred_element_type=jnp.float32)
    query_grad = query_grad + scaling * state_product("thd,hde->the", grad_blk, prefix_parts)
    key_grad = jnp.einsum("hts,thd->shd", near_grad, query_blk, preferred_element_type=jnp.float32)
    key_grad = key_grad + scaling * state_product("shd,hde->she", value_blk, suffix_parts)
    value_grad = jnp.einsum(
        "hts,the->she", near_query, grad_blk, preferred_element_type=jnp.float32
    )
    value_grad = value_grad + scaling * state_product("she,hde->shd", key_blk, suffix_parts)
    return (
        query_grad.astype(jnp.bfloat16),
        key_grad.astype(jnp.bfloat16),
        value_grad.astype(jnp.bfloat16),
    )


def local(
    inputs,
    queries,
    key_heads,
    value_heads,
    out_grad,
    qkv_weight,
    gate_weight,
    up_weight,
    down_weight,
    chosen,
    pad_counts,
    combine,
):
    local_rows = inputs.shape[1]
    width = inputs.shape[2]
    block_count = local_rows // BLK
    scaling = 1.0 / math.sqrt(lax.axis_size("ctx") * local_rows * DH)
    gate_mat = gate_weight[0]
    up_mat = up_weight[0]
    down_mat = down_weight[0]
    chosen_rows = chosen[0, 0]
    expert_count = chosen_rows.shape[0]
    slot_count = chosen_rows.shape[1]
    live = (
        lax.broadcasted_iota(jnp.int32, (expert_count, slot_count), 1)
        < (slot_count - pad_counts[0, 0])[:, None]
    )
    slot_weight = jnp.where(live, combine[0, 0], 0.0)
    input_rows = jnp.take(inputs[0], chosen_rows, axis=0)

    def blocks(array):
        return array[0].reshape(block_count, BLK, HEADS, DH)

    query_b = blocks(queries)
    key_b = blocks(key_heads)
    value_b = blocks(value_heads)
    grad_b = blocks(out_grad)
    outer_values = jnp.einsum("bthd,bthe->bhde", value_b, key_b, preferred_element_type=jnp.float32)
    outer_grads = jnp.einsum("bthd,bthe->bhde", grad_b, query_b, preferred_element_type=jnp.float32)
    values_total = jnp.sum(outer_values, axis=0)
    grads_total = jnp.sum(outer_grads, axis=0)
    own_index = lax.axis_index("ctx")
    stacked = jnp.stack([values_total, grads_total])[None]
    empty = jnp.zeros_like(values_total)
    piece = lax.all_gather(stacked.astype(jnp.bfloat16), "ctx", axis=0, tiled=True).astype(
        jnp.float32
    )
    index_rows = lax.broadcasted_iota(jnp.int32, (piece.shape[0], 1, 1, 1), 0)
    lower = jnp.where(index_rows < own_index, piece[:, 0], 0.0)
    higher = jnp.where(index_rows > own_index, piece[:, 1], 0.0)
    before = empty + jnp.sum(lower, axis=0)
    after = empty + jnp.sum(higher, axis=0)
    block_before = before[None] + exclusive_sums(outer_values, False)
    block_after = after[None] + exclusive_sums(outer_grads, True)

    def one_block(packed):
        return block_grads(*packed, scaling)

    query_grad, key_grad, value_grad = lax.map(
        one_block, (query_b, key_b, value_b, grad_b, block_before, block_after)
    )
    qkv_grad = jnp.concatenate(
        [
            query_grad.reshape(local_rows, HEADS * DH),
            key_grad.reshape(local_rows, HEADS * DH),
            value_grad.reshape(local_rows, HEADS * DH),
        ],
        axis=1,
    )
    token_grad = jnp.einsum(
        "tc,rc->tr",
        qkv_grad,
        lax.all_gather(qkv_weight, "ctx", axis=0, tiled=True),
        preferred_element_type=jnp.float32,
    ).astype(jnp.bfloat16)
    grad_rows = jnp.take(token_grad, chosen_rows, axis=0)
    rows_in = lax.all_to_all(input_rows, ("grp", "ctx"), split_axis=0, concat_axis=0, tiled=True)
    rows_grad = lax.all_to_all(grad_rows, ("grp", "ctx"), split_axis=0, concat_axis=0, tiled=True)
    weights_in = lax.all_to_all(
        slot_weight.astype(jnp.bfloat16), ("grp", "ctx"), split_axis=0, concat_axis=0, tiled=True
    ).astype(slot_weight.dtype)
    sources = rows_in.shape[0]
    items = rows_in.shape[1]
    active, up_slope = expert_front(rows_in.reshape(sources * items, width), gate_mat, up_mat)
    result = expert_back(
        rows_grad.reshape(sources * items, width),
        weights_in.reshape(sources * items),
        active,
        up_slope,
        gate_mat,
        up_mat,
        down_mat,
    )
    returned = lax.all_to_all(
        result.reshape(sources, items, width),
        ("grp", "ctx"),
        split_axis=0,
        concat_axis=0,
        tiled=True,
    )
    added = jnp.where(live[:, :, None], returned.astype(jnp.float32), 0.0)
    scattered = (
        jnp.zeros((local_rows, width), jnp.float32)
        .at[chosen_rows.reshape(-1)]
        .add(added.reshape(expert_count * slot_count, width))
    )
    total = token_grad.astype(jnp.float32) + scattered
    return total.astype(jnp.bfloat16)[None]


def solution(mesh):
    return jax.shard_map(
        local,
        mesh=mesh,
        in_specs=(
            P("grp", "ctx", None),
            P("grp", "ctx", None),
            P("grp", "ctx", None),
            P("grp", "ctx", None),
            P("grp", "ctx", None),
            P("ctx", None),
            P(("grp", "ctx"), None, None),
            P(("grp", "ctx"), None, None),
            P(("grp", "ctx"), None, None),
            P("grp", "ctx", None, None),
            P("grp", "ctx", None),
            P("grp", "ctx", None, None),
        ),
        out_specs=P("grp", "ctx", None),
        check_vma=False,
    )
```

profile of v0, /device:TPU:0, one launch (start us, length us, event | category | flops | bytes accessed | tf_op | source)
XLA Modules:
  0.0 367.7 jit_solution(17977370888268982109)
XLA Ops:
  6.5 2.6 copy.96
  9.2 2.6 copy.95
  13.1 2.4 copy.66
  17.1 2.5 fusion.38
  22.6 7.5 %all-to-all-start = ((bf16[32,1,2]{2,1,0:T(2,128)(2,1)}), bf16[32,1,2]{2,1,0:T(2,128)(2,1)S(1)}, u32[]{:S(2)}, u32[]{:S(2)}) async-start(bf16[32,1,2]{2,1,0:T(2,128)(2,1)} %copy.84), calls=%async_computation | async-start | bytes 32768 | tf_op jit(solution)/shard_map/all_to_all | solution.py:166
  30.3 3.0 gather_fusion.1
  34.4 5.0 %select_convert_fusion.1 = bf16[8,512,512]{2,1,0:T(8,128)(2,1)} fusion(pred[512,512]{1,0:T(8,128)(4,1)S(1)} %iota_compare_fusion, bf16[512,8,128]{2,1,0:T(8,128)(2,1)} %bitcast.107, bf16[512,8,128]{2,1,0:T(8,128)(2,1)} %bitcast.111), kind=kOutput, calls=%fused_computation.4 | convolution fusion | flops 543162368 | bytes 6553600 | tf_op jit(solution)/shard_map/while/body/eval_jaxpr/thd,shd->hts/dot_general | solution.py:62
  39.4 58.0 %all-gather.3.cloned.1.call-done = bf16[8,2,8,128,128]{4,3,2,1,0:T(8,128)(2,1)} async-done(((bf16[1,2,8,128,128]{4,3,2,1,0:T(8,128)(2,1)}), bf16[8,2,8,128,128]{4,3,2,1,0:T(8,128)(2,1)}) %all-gather.3.cloned.1.call-update) | async-done | bytes 4194320 | tf_op jit(solution)/shard_map/all_gather | solution.py:132
  97.3 3.2 convert_element_type.98
  112.0 2.5 fusion.37
  114.5 6.2 %fusion.35 = bf16[512,8,128]{0,2,1:T(8,128)(2,1)} fusion(f32[8,128,512]{2,1,0:T(8,128)} %fusion.72, f32[8,128,512]{2,1,0:T(8,128)} %fusion.70, bf16[512,8,128]{0,2,1:T(8,128)(2,1)} %copy.66, pred[512,512]{1,0:T(8,128)(4,1)S(1)} %iota_compare_fusion, bf16[512,8,128]{2,1,0:T(8,128)(2,1)} %bitcast.115, bf16[512,8,128]{2,1,0:T(8,128)(2,1)} %bitcast.102), kind=kOutput, calls=%fused_computation.36 | convolution fusion | flops 1082130432 | bytes 8650752 | tf_op jit(solution)/shard_map/while/body/eval_jaxpr/hts,the->she/dot_general | solution.py:76
  120.7 153.5 %all-gather.5.cloned.1.call-done = bf16[2048,3072]{1,0:T(8,128)(2,1)} async-done(((bf16[256,3072]{1,0:T(8,128)(2,1)}), bf16[2048,3072]{1,0:T(8,128)(2,1)}) %all-gather.5.cloned.1.call-update) | async-done | bytes 12582928 | tf_op jit(solution)/shard_map/all_gather | solution.py:160
  274.2 13.7 %fusion.94 = (f32[512,2048]{1,0:T(8,128)}, bf16[512,2048]{1,0:T(8,128)(2,1)}) fusion(bf16[2048,3072]{1,0:T(8,128)(2,1)} %all-gather.5.cloned.1.call-done, bf16[512,1024]{0,1:T(8,128)(2,1)} %bitcast.124, bf16[512,1024]{0,1:T(8,128)(2,1)} %bitcast.118, bf16[512,1024]{0,1:T(8,128)(2,1)} %bitcast.119), kind=kOutput, calls=%fused_computation.107 | convolution fusion | flops 6453985280 | bytes 22020096 | tf_op jit(solution)/shard_map/tc,rc->tr/dot_general | solution.py:157
  288.0 2.8 gather_fusion
  294.0 13.3 %all_to_all.21 = bf16[32,2,2048]{2,1,0:T(2,128)(2,1)} all-to-all(bf16[32,2,2048]{2,1,0:T(2,128)(2,1)S(1)} %get-tuple-element.26), channel_id=1, replica_groups=mesh['grp'=4,'ctx'=8] {'grp','ctx'}, dimensions={0} | all-to-all | bytes 524288 | tf_op jit(solution)/shard_map/all_to_all | solution.py:164
  307.3 3.3 all-to-all-start.1
  311.9 3.2 fusion.18
  315.1 6.2 %all-to-all-done.1 = bf16[32,2,2048]{2,1,0:T(2,128)(2,1)} async-done(((bf16[32,2,2048]{2,1,0:T(2,128)(2,1)}), bf16[32,2,2048]{2,1,0:T(2,128)(2,1)}, u32[]{:S(2)}, u32[]{:S(2)}) %all-to-all-start.1) | async-done | bytes 262176 | tf_op jit(solution)/shard_map/all_to_all | solution.py:165
  323.0 3.7 %fusion.40 = f32[64,768]{1,0:T(8,128)} fusion(bf16[64,2048]{1,0:T(8,128)(2,1)} %reshape.201, bf16[1,768,2048]{2,1,0:T(8,128)(2,1)} %param.22, f32[64]{0:T(128)S(1)} %reshape.205), kind=kOutput, calls=%fused_computation.46 | convolution fusion | flops 201375744 | bytes 3604736 | tf_op jit(solution)/shard_map/dot_general | solution.py:27
  326.8 4.6 %fusion.16 = f32[64,2048]{1,0:T(8,128)} fusion(bf16[1,2048,768]{2,1,0:T(8,128)(2,1)} %param.20, f32[64,768]{1,0:T(8,128)} %fusion.40, bf16[64,2048]{1,0:T(8,128)(2,1)S(1)} %reshape.202, bf16[1,2048,768]{2,1,0:T(8,128)(2,1)S(1)} %copy-done, f32[64,768]{1,0:T(8,128)} %fusion.18), kind=kOutput, calls=%fused_computation.22 | convolution fusion | flops 403144704 | bytes 7471104 | tf_op jit(solution)/shard_map/dot_general | solution.py:31
  334.6 2.6 all-to-all-start.3
  337.4 10.4 %all-to-all-done.3 = bf16[32,2,2048]{2,1,0:T(2,128)(2,1)S(1)} async-done(((bf16[32,2,2048]{2,1,0:T(2,128)(2,1)}), bf16[32,2,2048]{2,1,0:T(2,128)(2,1)S(1)}, u32[]{:S(2)}, u32[]{:S(2)}) %all-to-all-start.3) | async-done | bytes 262176 | tf_op jit(solution)/shard_map/all_to_all | solution.py:181
  351.1 5.9 %scatter_fusion = f32[512,2048]{1,0:T(8,128)} fusion(f32[512,2048]{1,0:T(8,128)} %get-tuple-element.28, s32[64]{0:T(128)S(1)} %fusion.86, f32[64,2048]{1,0:T(8,128)} %reshape.226), kind=kCustom, calls=%fused_computation.2 | custom fusion | flops 131072 | bytes 1573120 | tf_op jit(solution)/shard_map/scatter-add | solution.py:192
  357.0 3.8 %convert_bitcast_fusion = bf16[1,512,2048]{2,1,0:T(8,128)(2,1)} fusion(f32[512,2048]{1,0:T(8,128)} %scatter_fusion), kind=kLoop, calls=%fused_computation.41 | loop fusion | flops 1048576 | bytes 6291456 | tf_op jit(solution)/shard_map/broadcast_in_dim | solution.py:195
  (67 shorter events, 31.3 us)
Async XLA Ops:
  6.5 320.2 %copy-start = (bf16[1,2048,768]{2,1,0:T(8,128)(2,1)S(1)}, bf16[1,2048,768]{2,1,0:T(8,128)(2,1)}, u32[]{:S(2)}) copy-start(bf16[1,2048,768]{2,1,0:T(8,128)(2,1)} %param.21) | copy-start | bytes 9437188
  6.5 90.8 %all-gather.3.cloned.1.call-start = ((), (), s32[]{:S(2)}) async-start(), calls=%async_computation.4 | async-start | bytes 4718592 | tf_op jit(solution)/shard_map/all_gather | solution.py:132
  6.5 5.2 %copy-start.7 = (bf16[1,512,1024]{2,1,0:T(8,128)(2,1)S(1)}, bf16[1,512,1024]{2,1,0:T(8,128)(2,1)}, u32[]{:S(2)}) copy-start(bf16[1,512,1024]{2,1,0:T(8,128)(2,1)} %param.18) | copy-start | bytes 3145732
  15.5 4.2 %copy-start.8 = (bf16[512,8,128]{0,2,1:T(8,128)(2,1)S(1)}, bf16[512,8,128]{0,2,1:T(8,128)(2,1)}, u32[]{:S(2)}) copy-start(bf16[512,8,128]{0,2,1:T(8,128)(2,1)} %copy.66) | copy-start | bytes 3145732
  17.1 2.6 copy-start.5
  19.7 2.2 copy-start.11
  19.7 2.2 copy-start.10
  19.7 10.4 %copy-start.9 = (s32[1,1,32,2]{2,3,1,0:T(2,128)S(1)}, s32[1,1,32,2]{2,3,1,0:T(2,128)}, u32[]{:S(2)}) copy-start(s32[1,1,32,2]{2,3,1,0:T(2,128)} %param.23) | copy-start | bytes 772
  21.1 253.2 %all-gather.5.cloned.1.call-start = ((), (), s32[]{:S(2)}) async-start(), calls=%async_computation.5 | async-start | bytes 14155776 | tf_op jit(solution)/shard_map/all_gather | solution.py:160
  22.6 271.4 %all-to-all-start = ((bf16[32,1,2]{2,1,0:T(2,128)(2,1)}), bf16[32,1,2]{2,1,0:T(2,128)(2,1)S(1)}, u32[]{:S(2)}, u32[]{:S(2)}) async-start(bf16[32,1,2]{2,1,0:T(2,128)(2,1)} %copy.84), calls=%async_computation | async-start | bytes 32768 | tf_op jit(solution)/shard_map/all_to_all | solution.py:166
  100.6 1.2 copy-start.1
  101.8 3.6 copy-start.4
  105.4 1.4 copy-start.2
  106.8 2.7 copy-start.3
  106.8 3.1 copy-start.6
  307.3 13.9 %all-to-all-start.1 = ((bf16[32,2,2048]{2,1,0:T(2,128)(2,1)}), bf16[32,2,2048]{2,1,0:T(2,128)(2,1)}, u32[]{:S(2)}, u32[]{:S(2)}) async-start(bf16[32,2,2048]{2,1,0:T(2,128)(2,1)} %get-tuple-element.27), calls=%async_computation.1 | async-start | bytes 524288 | tf_op jit(solution)/shard_map/all_to_all | solution.py:165
  334.6 13.2 %all-to-all-start.3 = ((bf16[32,2,2048]{2,1,0:T(2,128)(2,1)}), bf16[32,2,2048]{2,1,0:T(2,128)(2,1)S(1)}, u32[]{:S(2)}, u32[]{:S(2)}) async-start(bf16[32,2,2048]{2,1,0:T(2,128)(2,1)} %reshape.203), calls=%async_computation.3 | async-start | bytes 524288 | tf_op jit(solution)/shard_map/all_to_all | solution.py:181
Sparse Core Ops, SparseCore 0:
  21.2 76.0 all-gather.2
  99.5 174.6 all-gather.4
where the time goes:
time: 369 us; the launch traced here: 368 us
  waiting for transfers between devices  229 us (62%)
  matrix products  52 us (14%)
  local copies, waits for them, and re-layouts  27.9 us (8%)
  other arithmetic  18.6 us (5%)
  between operations  13.7 us (4%)
  starting transfers between devices  13.4 us (4%)
  blocking collectives  13.3 us (4%)
    all_gather x1, waiting for transfers between devices, local(): lax.all_gather(qkv_weight, 'ctx', axis=0, tiled=True)  154 us
    all_gather x1, waiting for transfers between devices, local(): lax.all_gather(stacked.astype(jnp.bfloat16), 'ctx', axis=0, tiled=True)  58 us
    dot_general x1, matrix products, local(): jnp.einsum('tc,rc->tr', qkv_grad, lax.all_gather(qkv_weight, 'ctx', axis=...  13.7 us
    all_to_all x1, blocking collectives, local(): lax.all_to_all(input_rows, ('grp', 'ctx'), split_axis=0, concat_axis=0, t...  13.3 us
    unnamed x29, local copies, waits for them, and re-layouts  10.8 us
    all_to_all x1, waiting for transfers between devices, local(): lax.all_to_all(result.reshape(sources, items, width), ('grp', 'ctx'), spl...  10.4 us
    all_to_all x1, starting transfers between devices, local(): lax.all_to_all(slot_weight.astype(jnp.bfloat16), ('grp', 'ctx'), split_ax...  7.48 us
  transfers between devices with their start and end apart: 5, of which 4 were waited for; matrix products, arithmetic and copies ran while one was open for 15% of the time, Pallas kernels for 0%

commit v1 on v0

v1 whole, which is shorter than its diff:
```python
import functools
import math

import jax
import jax.numpy as jnp
from jax import lax
from jax.experimental import pallas as pl
from jax.experimental.pallas import tpu as pltpu
from jax.sharding import PartitionSpec as P

DH = 128
VMEM_BYTES = 56 * 1024 * 1024
F32 = jnp.float32
BF16 = jnp.bfloat16
LAST = (((1,), (1,)), ((), ()))
FIRST = (((0,), (0,)), ((), ()))
PLAIN = (((1,), (0,)), ((), ()))


def dot(left, right, contract):
    return lax.dot_general(left, right, contract, preferred_element_type=F32)


def in_vmem():
    return pl.BlockSpec(memory_space=pltpu.VMEM)


def in_smem():
    return pl.BlockSpec(memory_space=pltpu.SMEM)


def anywhere():
    return pl.BlockSpec(memory_space=pl.ANY)


def params():
    return pltpu.CompilerParams(vmem_limit_bytes=VMEM_BYTES)


def cost(flops, moved):
    return pl.CostEstimate(flops=int(flops), bytes_accessed=int(moved), transcendentals=0)


def lane_slice(start, size):
    return pl.ds(pl.multiple_of(start, DH), size)


class Plan:
    def __init__(self):
        self.grp = lax.axis_size("grp")
        self.ctx = lax.axis_size("ctx")
        self.cores = 2 if self.grp % 2 == 0 else 1
        self.cross = self.grp // self.cores
        inner = 1
        while inner * inner * 4 <= self.ctx and self.ctx % (inner * 2) == 0:
            inner *= 2
        self.inner = inner
        self.outer = self.ctx // inner

    def outer_turn(self, k):
        a, b = self.outer, self.inner
        return [(z * b + y, ((z + k) % a) * b + y) for z in range(a) for y in range(b)]

    def inner_turn(self, k):
        a, b = self.outer, self.inner
        return [(z * b + y, z * b + (y + k) % b) for z in range(a) for y in range(b)]

    def cross_turn(self, k):
        m, n = self.cross, self.cores
        return [(x * n + c, ((x + k) % m) * n + c) for x in range(m) for c in range(n)]

    def core_swap(self):
        return [(g, g ^ 1) for g in range(self.grp)]

    def mixed_turn(self, dx, dy):
        pairs = []
        for g in range(self.grp):
            x, c = divmod(g, self.cores)
            for s in range(self.ctx):
                z, y = divmod(s, self.inner)
                if c == 0:
                    to = (((x + dx) % self.cross) * self.cores + c, s)
                else:
                    to = (g, z * self.inner + (y + dy) % self.inner)
                pairs.append((g * self.ctx + s, to[0] * self.ctx + to[1]))
        return pairs


def state_kernel(inner, heads, pos_ref, q_ref, k_ref, v_ref, g_ref, *out_refs):
    each = heads // inner
    for i, out_ref in enumerate(out_refs):
        base = lax.rem(pos_ref[3] + i, inner) * (each * DH)
        for h in range(each):
            lanes = lane_slice(base + h * DH, DH)
            rows = slice(h * DH, (h + 1) * DH)
            out_ref[0, rows, :] = dot(v_ref[:, lanes], k_ref[:, lanes], FIRST).astype(BF16)
            out_ref[1, rows, :] = dot(g_ref[:, lanes], q_ref[:, lanes], FIRST).astype(BF16)


def total_kernel(inner, outer, pos_ref, *refs):
    ins, outs = refs[:inner], refs[inner:]
    total = ins[0][...].astype(F32)
    for ref in ins[1:]:
        total = total + ref[...].astype(F32)
    values, grads = total[0].astype(BF16), total[1].astype(BF16)
    for k, out in enumerate(outs, 1):
        out[...] = jnp.where(pos_ref[2] + k < outer, values, grads)


def spread_kernel(inner, outer, pos_ref, *refs):
    own, far, outs = refs[:inner], refs[inner : inner + outer - 1], refs[inner + outer - 1 :]
    z, y = pos_ref[2], pos_ref[3]
    shape = own[0].shape[1:]
    before = jnp.zeros(shape, F32)
    after = jnp.zeros(shape, F32)
    for k, ref in enumerate(far, 1):
        piece = ref[...].astype(F32)
        before = before + jnp.where(z >= k, piece, 0.0)
        after = after + jnp.where(z < k, piece, 0.0)
    for i, out in enumerate(outs):
        goal = lax.rem(y + i, inner)
        low, high = before, after
        for k, ref in enumerate(own):
            source = lax.rem(y + inner - k, inner)
            low = low + jnp.where(source < goal, ref[0].astype(F32), 0.0)
            high = high + jnp.where(source > goal, ref[1].astype(F32), 0.0)
        out[0] = low.astype(BF16)
        out[1] = high.astype(BF16)


def near_kernel(scaling, q_ref, k_ref, v_ref, g_ref, out_ref):
    rows = q_ref.shape[0]
    q, k, v, g = q_ref[...], k_ref[...], v_ref[...], g_ref[...]
    causal = lax.broadcasted_iota(jnp.int32, (rows, rows), 0) >= lax.broadcasted_iota(
        jnp.int32, (rows, rows), 1
    )
    near_grad = jnp.where(causal, scaling * dot(g, v, LAST), 0.0).astype(BF16)
    near_query = jnp.where(causal, scaling * dot(q, k, LAST), 0.0).astype(BF16)
    out_ref[0] = dot(near_grad, k, PLAIN).astype(BF16)
    out_ref[1] = dot(near_grad, q, FIRST).astype(BF16)
    out_ref[2] = dot(near_query, g, FIRST).astype(BF16)


def pick_matrix(pick_ref, rows):
    count = pick_ref.shape[0]
    return (lax.broadcasted_iota(jnp.int32, (count, rows), 1) == pick_ref[...]).astype(BF16)


def input_rows_kernel(pick_ref, weight_ref, x_ref, out_ref):
    rows, width = x_ref.shape
    out_ref[:, :width] = dot(pick_matrix(pick_ref, rows), x_ref[...], PLAIN).astype(BF16)
    weight = weight_ref[...]
    upper = weight.astype(BF16).astype(F32)
    lane = lax.broadcasted_iota(jnp.int32, (weight.shape[0], DH), 1)
    both = jnp.where(lane == 0, upper, jnp.where(lane == 1, weight - upper, 0.0))
    out_ref[:, width:] = both.astype(BF16)


def far_kernel(inner, heads, scaling, pos_ref, pick_ref, near_ref, k_ref, v_ref, g_ref, *refs):
    states, (qkv_ref, rows_ref) = refs[:inner], refs[inner:]
    each = heads // inner
    rows = k_ref.shape[0]
    for i, state in enumerate(states):
        base = lax.rem(pos_ref[3] + inner - i, inner) * (each * DH)
        for h in range(each):
            lanes = lane_slice(base + h * DH, DH)
            prefix = state[0, h * DH : (h + 1) * DH, :]
            suffix = state[1, h * DH : (h + 1) * DH, :]
            parts = (
                dot(g_ref[:, lanes], prefix, PLAIN),
                dot(v_ref[:, lanes], suffix, PLAIN),
                dot(k_ref[:, lanes], suffix, LAST),
            )
            for n, part in enumerate(parts):
                whole = near_ref[n, :, lanes].astype(F32) + scaling * part
                qkv_ref[:, lane_slice(base + (n * heads + h) * DH, DH)] = whole.astype(BF16)
    rows_ref[...] = dot(pick_matrix(pick_ref, rows), qkv_ref[...], PLAIN).astype(BF16)


def start_pieces(plan, keys, pos_ref, pieces, buffer, sems):
    copies = []
    x = lax.div(pos_ref[0], plan.cores)
    c = lax.rem(pos_ref[0], plan.cores)
    block = buffer.shape[0] // plan.inner
    for n, (key, piece) in enumerate(zip(keys, pieces, strict=True)):
        dx, dc, dy = key
        y = lax.rem(pos_ref[3] + plan.inner - dy, plan.inner)
        start = y * block
        if dx is not None:
            gx = lax.rem(x + plan.cross - dx, plan.cross)
            gc = c if dc == 0 else 1 - c
            start = start + (gx * plan.cores + gc) * piece.shape[0]
        size = piece.shape[0]
        start = pl.multiple_of(start, size)
        copy = pltpu.make_async_copy(piece, buffer.at[pl.ds(start, size), :], sems.at[n])
        copy.start()
        copies.append(copy)
    return copies


def project_kernel(plan, keys, pos_ref, qkv_ref, *refs):
    pieces, (out_ref, buffer, sems) = refs[: len(keys)], refs[len(keys) :]
    for copy in start_pieces(plan, keys, pos_ref, pieces, buffer, sems):
        copy.wait()
    out_ref[...] = dot(qkv_ref[...], buffer[...], LAST).astype(BF16)


def back_kernel(plan, keys, turn, pos_ref, rows_ref, so_far_ref, down_ref, *refs):
    pieces, (out_ref, buffer, down, sems) = refs[: len(keys)], refs[len(keys) :]
    copies = start_pieces(plan, keys, pos_ref, pieces, buffer, sems)
    width = buffer.shape[0]
    z = lax.rem(pos_ref[2] + plan.outer - turn, plan.outer)
    last = pltpu.make_async_copy(
        down_ref.at[:, lane_slice(z * width, width)], down, sems.at[len(keys)]
    )
    last.start()
    for copy in copies:
        copy.wait()
    last.wait()
    grad_rows = dot(rows_ref[...], buffer[...], LAST).astype(BF16)
    out_ref[...] = so_far_ref[...] + dot(grad_rows, down[...], LAST)


def front_kernel(x_ref, gate_ref, up_ref, active_ref, slope_ref, gate_acc, up_acc):
    step = pl.program_id(0)

    @pl.when(step == 0)
    def _():
        gate_acc[...] = jnp.zeros_like(gate_acc)
        up_acc[...] = jnp.zeros_like(up_acc)

    gate_acc[...] += dot(x_ref[...], gate_ref[...], PLAIN)
    up_acc[...] += dot(x_ref[...], up_ref[...], PLAIN)

    @pl.when(step == pl.num_programs(0) - 1)
    def _():
        gate = gate_acc[...]
        sigma = jax.nn.sigmoid(gate)
        active_ref[...] = gate * sigma
        slope_ref[...] = up_acc[...] * (sigma * (1.0 + gate * (1.0 - sigma)))


def slot_kernel(back_ref, weight_ref, active_ref, slope_ref, gate_ref, up_ref, out_ref):
    weight = weight_ref[:, 0:1].astype(F32) + weight_ref[:, 1:2].astype(F32)
    hidden = weight * back_ref[...]
    up_grad = (hidden * active_ref[...]).astype(BF16)
    gate_grad = (hidden * slope_ref[...]).astype(BF16)
    total = dot(gate_grad, gate_ref[...], LAST) + dot(up_grad, up_ref[...], LAST)
    out_ref[...] = total.astype(BF16)


def join_kernel(plan, pos_ref, pick_ref, returned_ref, *refs):
    parts, out_ref = refs[:-1], refs[-1]
    rows, width = parts[0].shape
    spread = pick_matrix(pick_ref, rows)
    for turn, part in enumerate(parts):
        z = lax.rem(pos_ref[2] + plan.outer - turn, plan.outer)
        lanes = lane_slice(z * width, width)
        added = dot(spread, returned_ref[:, lanes], FIRST)
        out_ref[:, lanes] = (part[...].astype(F32) + added).astype(BF16)


def gather_projection(plan, weight):
    share = weight.shape[0] // plan.grp
    core = lax.rem(lax.axis_index("grp"), plan.cores)
    own = lax.dynamic_slice_in_dim(weight, lax.axis_index("grp") * share, share, 0)
    groups = []
    held = own
    for turn in range(plan.outer):
        pieces = {}
        if turn == 0:
            for dy in range(1, plan.inner):
                pieces[0, 0, dy] = lax.ppermute(own, "ctx", plan.inner_turn(dy))
                for dx in range(1, plan.cross):
                    pieces[dx, 0, dy] = lax.ppermute(
                        pieces[0, 0, dy], "grp", plan.cross_turn(dx)
                    )
        else:
            held = lax.ppermute(held, "ctx", plan.outer_turn(1))
            pieces[0, 0, 0] = held
            for dx in range(1, plan.cross):
                pieces[dx, 0, 0] = lax.ppermute(held, "grp", plan.cross_turn(dx))
            for dy in range(1, plan.inner):
                pieces[0, 0, dy] = lax.ppermute(held, "ctx", plan.inner_turn(dy))
            for dx in range(1, plan.cross):
                for dy in range(1, plan.inner):
                    pieces[dx, 0, dy] = lax.ppermute(
                        jnp.where(core == 0, pieces[0, 0, dy], pieces[dx, 0, 0]),
                        ("grp", "ctx"),
                        plan.mixed_turn(dx, dy),
                    )
        if plan.cores == 2:
            for dx, _, dy in list(pieces):
                pieces[dx, 1, dy] = lax.ppermute(pieces[dx, 0, dy], "grp", plan.core_swap())
        if turn == 0:
            pieces[None, None, 0] = weight
        groups.append(pieces)
    return groups


def local(
    inputs,
    queries,
    key_heads,
    value_heads,
    out_grad,
    qkv_weight,
    gate_weight,
    up_weight,
    down_weight,
    chosen,
    pad_counts,
    combine,
):
    plan = Plan()
    rows, width = inputs.shape[1:]
    channels = queries.shape[2]
    heads = channels // DH
    scaling = 1.0 / math.sqrt(plan.ctx * rows * DH)
    q, k, v, g = queries[0], key_heads[0], value_heads[0], out_grad[0]
    gate_mat, up_mat, down_mat = gate_weight[0], up_weight[0], down_weight[0]
    hidden = gate_mat.shape[1]
    experts, slots = chosen.shape[2:]
    items = experts * slots
    inner, outer = plan.inner, plan.outer
    grp_at, ctx_at = lax.axis_index("grp"), lax.axis_index("ctx")
    pos = jnp.stack([grp_at, ctx_at, ctx_at // inner, ctx_at % inner]).astype(jnp.int32)
    live = (
        lax.broadcasted_iota(jnp.int32, (experts, slots), 1)
        < (slots - pad_counts[0, 0])[:, None]
    )
    pick = jnp.where(live, chosen[0, 0], -1).reshape(items, 1)
    slot_weight = jnp.where(live, combine[0, 0], 0.0).reshape(items, 1)

    groups = gather_projection(plan, qkv_weight)

    part = jax.ShapeDtypeStruct((2, channels // inner, DH), BF16)
    own = pl.pallas_call(
        functools.partial(state_kernel, inner, heads),
        out_shape=[part] * inner,
        in_specs=[in_smem()] + [in_vmem()] * 4,
        out_specs=[in_vmem()] * inner,
        compiler_params=params(),
        cost_estimate=cost(4 * rows * DH * channels, 8 * rows * channels),
        name="states",
    )(pos, q, k, v, g)
    shares = [own[0]] + [
        lax.ppermute(own[i], "ctx", plan.inner_turn(i)) for i in range(1, inner)
    ]
    totals = pl.pallas_call(
        functools.partial(total_kernel, inner, outer),
        out_shape=[jax.ShapeDtypeStruct(part.shape[1:], BF16)] * (outer - 1),
        in_specs=[in_smem()] + [in_vmem()] * inner,
        out_specs=[in_vmem()] * (outer - 1),
        compiler_params=params(),
        name="totals",
    )(pos, *shares)
    far = [lax.ppermute(totals[i - 1], "ctx", plan.outer_turn(i)) for i in range(1, outer)]
    sums = pl.pallas_call(
        functools.partial(spread_kernel, inner, outer),
        out_shape=[part] * inner,
        in_specs=[in_smem()] + [in_vmem()] * (inner + outer - 1),
        out_specs=[in_vmem()] * inner,
        compiler_params=params(),
        name="sums",
    )(pos, *shares, *far)
    states = [sums[0]] + [
        lax.ppermute(sums[i], "ctx", plan.inner_turn(i)) for i in range(1, inner)
    ]

    packed = pl.pallas_call(
        input_rows_kernel,
        out_shape=jax.ShapeDtypeStruct((items, width + DH), BF16),
        in_specs=[in_vmem()] * 3,
        out_specs=in_vmem(),
        compiler_params=params(),
        cost_estimate=cost(2 * items * rows * width, 2 * rows * width),
        name="input_rows",
    )(pick, slot_weight, inputs[0])
    head = pl.BlockSpec((rows, DH), lambda h: (0, h))
    near = pl.pallas_call(
        functools.partial(near_kernel, scaling),
        out_shape=jax.ShapeDtypeStruct((3, rows, channels), BF16),
        grid=(heads,),
        in_specs=[head] * 4,
        out_specs=pl.BlockSpec((3, rows, DH), lambda h: (0, 0, h)),
        compiler_params=params(),
        cost_estimate=cost(10 * rows * rows * channels, 14 * rows * channels),
        name="near",
    )(q, k, v, g)

    def exchange(array):
        moved = lax.all_to_all(
            array.reshape(experts, slots, array.shape[1]),
            ("grp", "ctx"),
            split_axis=0,
            concat_axis=0,
            tiled=True,
        )
        return moved.reshape(items, array.shape[1])

    arrived = exchange(packed)
    steps = 4
    deep = pl.BlockSpec((width // steps, hidden), lambda i: (i, 0))
    front_out = jax.ShapeDtypeStruct((items, hidden), F32)
    active, slope = pl.pallas_call(
        front_kernel,
        out_shape=[front_out] * 2,
        grid=(steps,),
        in_specs=[pl.BlockSpec((items, width // steps), lambda i: (0, i)), deep, deep],
        out_specs=[pl.BlockSpec((items, hidden), lambda i: (0, 0))] * 2,
        scratch_shapes=[pltpu.VMEM((items, hidden), F32)] * 2,
        compiler_params=params(),
        cost_estimate=cost(4 * items * width * hidden, 4 * width * hidden),
        name="front",
    )(arrived[:, :width], gate_mat, up_mat)

    qkv_grad, sent_rows = pl.pallas_call(
        functools.partial(far_kernel, inner, heads, scaling),
        out_shape=[
            jax.ShapeDtypeStruct((rows, 3 * channels), BF16),
            jax.ShapeDtypeStruct((items, 3 * channels), BF16),
        ],
        in_specs=[in_smem()] + [in_vmem()] * (5 + inner),
        out_specs=[in_vmem()] * 2,
        compiler_params=params(),
        cost_estimate=cost(6 * rows * DH * channels, 18 * rows * channels),
        name="far",
    )(pos, pick, near, k, v, g, *states)
    grad_rows = exchange(sent_rows)

    span = inner * qkv_weight.shape[0]
    buffer = pltpu.VMEM((span, 3 * channels), BF16)
    token_parts = []
    back = jnp.zeros((items, hidden), F32)
    for turn, group in enumerate(groups):
        keys, pieces = list(group), list(group.values())
        back = pl.pallas_call(
            functools.partial(back_kernel, plan, keys, turn),
            out_shape=jax.ShapeDtypeStruct((items, hidden), F32),
            in_specs=[in_smem(), in_vmem(), in_vmem(), anywhere()] + [anywhere()] * len(keys),
            out_specs=in_vmem(),
            scratch_shapes=[
                buffer,
                pltpu.VMEM((hidden, span), BF16),
                pltpu.SemaphoreType.DMA((len(keys) + 1,)),
            ],
            compiler_params=params(),
            cost_estimate=cost(2 * items * span * (3 * channels + hidden), 6 * span * channels),
            name="back",
        )(pos, grad_rows, back, down_mat, *pieces)
        token_parts.append(
            pl.pallas_call(
                functools.partial(project_kernel, plan, keys),
                out_shape=jax.ShapeDtypeStruct((rows, span), BF16),
                in_specs=[in_smem(), in_vmem()] + [anywhere()] * len(keys),
                out_specs=in_vmem(),
                scratch_shapes=[buffer, pltpu.SemaphoreType.DMA((len(keys),))],
                compiler_params=params(),
                cost_estimate=cost(6 * rows * span * channels, 6 * (span + rows) * channels),
                name="project",
            )(pos, qkv_grad, *pieces)
        )
    wide = pl.BlockSpec((width // steps, hidden), lambda i: (i, 0))
    fixed = pl.BlockSpec((items, hidden), lambda i: (0, 0))
    slot_grad = pl.pallas_call(
        slot_kernel,
        out_shape=jax.ShapeDtypeStruct((items, width), BF16),
        grid=(steps,),
        in_specs=[fixed, pl.BlockSpec((items, DH), lambda i: (0, width // DH)), fixed, fixed]
        + [wide, wide],
        out_specs=pl.BlockSpec((items, width // steps), lambda i: (0, i)),
        compiler_params=params(),
        cost_estimate=cost(4 * items * width * hidden, 4 * width * hidden),
        name="slot",
    )(back, arrived, active, slope, gate_mat, up_mat)
    returned = exchange(slot_grad)
    total = pl.pallas_call(
        functools.partial(join_kernel, plan),
        out_shape=jax.ShapeDtypeStruct((rows, width), BF16),
        in_specs=[in_smem()] + [in_vmem()] * (2 + outer),
        out_specs=in_vmem(),
        compiler_params=params(),
        cost_estimate=cost(2 * items * rows * width, 4 * rows * width),
        name="join",
    )(pos, pick, returned, *token_parts)
    return total[None]


def solution(mesh):
    rows = P("grp", "ctx", None)
    expert = P(("grp", "ctx"), None, None)
    lists = P("grp", "ctx", None, None)
    return jax.shard_map(
        local,
        mesh=mesh,
        in_specs=(rows,) * 5 + (P("ctx", None),) + (expert,) * 3 + (lists, rows, lists),
        out_specs=rows,
        check_vma=False,
    )
```

time: 369 us -> 188 us (0.51)
  waiting for transfers between devices: 229 us -> 36.3 us
  Pallas kernels: 0 us -> 89.9 us
  matrix products: 52 us -> 0 us
  starting transfers between devices: 13.4 us -> 42.4 us
  other arithmetic: 18.6 us -> 3.6 us
  local copies, waits for them, and re-layouts: 27.9 us -> 14.3 us
  between operations: 13.7 us -> 0.35 us
  blocking collectives: 13.3 us -> 0 us
    all_gather x2 -> x0, waiting for transfers between devices: 211 us -> none  [the longest x1 154 us: local(): lax.all_gather(qkv_weight, 'ctx', axis=0, tiled=True)]
    pallas_call x0 -> x17, Pallas kernels: none -> 89.9 us  [the longest x4 25.8 us: local(): pl.pallas_call(functools.partial(project_kernel, plan, keys), out_shape=j...]
    dot_general x17 -> x0, matrix products: 52 us -> none  [the longest x1 13.7 us: local(): jnp.einsum('tc,rc->tr', qkv_grad, lax.all_gather(qkv_weight, 'ctx', axis=...]
    ppermute x0 -> x33, waiting for transfers between devices: none -> 36.3 us  [the longest x3 8.92 us: gather_projection(): pieces[dx, 0, 0] = lax.ppermute(held, 'grp', plan.cross_turn(dx))]
    ppermute x0 -> x33, starting transfers between devices: none -> 31.3 us  [the longest x3 5.9 us: gather_projection(): held = lax.ppermute(held, 'ctx', plan.outer_turn(1))]
    all_to_all x3, waiting for transfers between devices: 16.6 us -> 0.01 us  [exchange(): lax.all_to_all(array.reshape(experts, slots, array.shape[1]), ('grp', 'ct...]
    all_to_all x1 -> x0, blocking collectives: 13.3 us -> none  [local(): lax.all_to_all(input_rows, ('grp', 'ctx'), split_axis=0, concat_axis=0, t...]
    unnamed x29 -> x52, local copies, waits for them, and re-layouts: 10.8 us -> 2.29 us
  transfers between devices with their start and end apart: 5 -> 36, of which waited for: 4 -> 10; matrix products, arithmetic and copies ran while one was open for 15% -> 6% of each run, Pallas kernels for 0% -> 40%
where the time goes in v1:
time: 188 us; the launch traced here: 187 us
  Pallas kernels  89.9 us (48%)
  starting transfers between devices  42.4 us (23%)
  waiting for transfers between devices  36.3 us (19%)
  local copies, waits for them, and re-layouts  14.3 us (8%)
  other arithmetic  3.6 us (2%)
    pallas_call x4, Pallas kernels, local(): pl.pallas_call(functools.partial(project_kernel, plan, keys), out_shape=j...  25.8 us
    pallas_call x4, Pallas kernels, local(): pl.pallas_call(functools.partial(back_kernel, plan, keys, turn), out_shap...  21.2 us
    all_to_all x3, starting transfers between devices, exchange(): lax.all_to_all(array.reshape(experts, slots, array.shape[1]), ('grp', 'ct...  11.1 us
    pallas_call x1, Pallas kernels, local(): pl.pallas_call(functools.partial(near_kernel, scaling), out_shape=jax.Sha...  9.99 us
    ppermute x3, waiting for transfers between devices, gather_projection(): pieces[dx, 0, 0] = lax.ppermute(held, 'grp', plan.cross_turn(dx))  8.92 us
    ppermute x3, waiting for transfers between devices, gather_projection(): lax.ppermute(jnp.where(core == 0, pieces[0, 0, dy], pieces[dx, 0, 0]), ('...  8.58 us
    ppermute x1, waiting for transfers between devices, local(): lax.ppermute(own[i], 'ctx', plan.inner_turn(i))  7.08 us
    pallas_call x1, Pallas kernels, local(): pl.pallas_call(functools.partial(far_kernel, inner, heads, scaling), out_...  6.92 us
  transfers between devices with their start and end apart: 36, of which 10 were waited for; matrix products, arithmetic and copies ran while one was open for 6% of the time, Pallas kernels for 40%

profile of v1, /device:TPU:0, one launch (start us, length us, event | category | flops | bytes accessed | tf_op | source)
XLA Modules:
  0.0 186.9 jit_solution(2138947730745223243)
XLA Ops:
  1.1 3.0 %collective-permute-start.5 = (bf16[64,3072]{1,0:T(8,128)(2,1)S(1)}, bf16[64,3072]{1,0:T(8,128)(2,1)S(1)}, u32[]{:S(2)}, u32[]{:S(2)}) collective-permute-start(bf16[64,3072]{1,0:T(8,128)(2,1)S(1)} %constant_dynamic-slice_fusion), channel_id=1, source_target_pairs={{0,1},{1,0},{2,3},{3,2},{4,5},{5,4},{6,7},{7,6},{8,9},{9,8},{10,11... | collective-permute-start | bytes 1179656 | tf_op jit(solution)/shard_map/ppermute | solution.py:273
  6.3 4.4 %states.1 = (bf16[2,512,128]{2,1,0:T(8,128)(2,1)}, bf16[2,512,128]{2,1,0:T(8,128)(2,1)}) custom-call(s32[4]{0:T(128)} %pad_add_fusion.pos_ref, bf16[512,1024]{1,0:T(8,128)(2,1)} %bitcast.37, bf16[512,1024]{1,0:T(8,128)(2,1)} %bitcast.27, bf16[512,1024]{1,0:T(8,128)(2,1)} %bitcast.30, bf16[512,1024]{1,0:T(8,128)(2,1)} %bitcast.33), custom_call_target="tpu_custom_call" | custom-call | flops 268435456 | bytes 4194304 | tf_op jit(solution)/shard_map/states/pallas_call | solution.py:338
  11.8 7.1 %collective-permute-done.refs_1_ = bf16[2,512,128]{2,1,0:T(8,128)(2,1)S(1)} collective-permute-done((bf16[2,512,128]{2,1,0:T(8,128)(2,1)}, bf16[2,512,128]{2,1,0:T(8,128)(2,1)S(1)}, u32[]{:S(2)}, u32[]{:S(2)}) %collective-permute-start) | collective-permute-done | bytes 262176 | tf_op jit(solution)/shard_map/ppermute | solution.py:348
  46.2 4.7 %all-to-all-start.1 = ((bf16[32,2,2176]{2,1,0:T(2,128)(2,1)}), bf16[32,2,2176]{2,1,0:T(2,128)(2,1)}, u32[]{:S(2)}, u32[]{:S(2)}) async-start(bf16[32,2,2176]{2,1,0:T(2,128)(2,1)} %reshape.83), calls=%async_computation.1 | async-start | bytes 557056 | tf_op jit(solution)/shard_map/all_to_all | solution.py:393
  50.9 10.0 %near.1.near_ref = bf16[3,512,1024]{2,1,0:T(8,128)(2,1)} custom-call(bf16[512,1024]{1,0:T(8,128)(2,1)} %bitcast.38, bf16[512,1024]{1,0:T(8,128)(2,1)} %bitcast.28, bf16[512,1024]{1,0:T(8,128)(2,1)} %bitcast.31, bf16[512,1024]{1,0:T(8,128)(2,1)} %bitcast.34), custom_call_target="tpu_custom_call" | custom-call | flops 2684354560 | bytes 7340032 | tf_op jit(solution)/shard_map/near/pallas_call | solution.py:381
  63.3 6.9 %far.1 = (bf16[512,3072]{1,0:T(8,128)(2,1)}, bf16[64,3072]{1,0:T(8,128)(2,1)}) custom-call(s32[4]{0:T(128)} %pad_add_fusion.pos_ref, s32[64,1]{1,0:T(8,128)} %broadcast_select_fusion.4.pick_ref, bf16[3,512,1024]{2,1,0:T(8,128)(2,1)} %near.1.near_ref, bf16[512,1024]{1,0:T(8,128)(2,1)} %bitcast.29, bf16[512,1024]{1,0:T(8,128)(2,1)} %bitcast.32, ...), custom_call_target="tpu_custom_call" | custom-call | flops 402653184 | bytes 9437184 | tf_op jit(solution)/shard_map/far/pallas_call | solution.py:418
  76.5 6.6 %collective-permute-done.18.refs_1_ = bf16[64,3072]{1,0:T(8,128)(2,1)S(1)} collective-permute-done((bf16[64,3072]{1,0:T(8,128)(2,1)S(1)}, bf16[64,3072]{1,0:T(8,128)(2,1)S(1)}, u32[]{:S(2)}, u32[]{:S(2)}) %collective-permute-start.18) | collective-permute-done | bytes 393248 | tf_op jit(solution)/shard_map/ppermute | solution.py:282
  83.1 3.4 %collective-permute-done.25.refs_0_ = bf16[64,3072]{1,0:T(8,128)(2,1)} collective-permute-done((bf16[64,3072]{1,0:T(8,128)(2,1)S(1)}, bf16[64,3072]{1,0:T(8,128)(2,1)}, u32[]{:S(2)}, u32[]{:S(2)}) %collective-permute-start.25) | collective-permute-done | bytes 393248 | tf_op jit(solution)/shard_map/ppermute | solution.py:279
  89.3 3.5 %all-to-all-start = ((bf16[32,2,3072]{2,1,0:T(2,128)(2,1)}), bf16[32,2,3072]{2,1,0:T(2,128)(2,1)}, u32[]{:S(2)}, u32[]{:S(2)}) async-start(bf16[32,2,3072]{2,1,0:T(2,128)(2,1)} %reshape.81), calls=%async_computation | async-start | bytes 786432 | tf_op jit(solution)/shard_map/all_to_all | solution.py:393
  97.2 5.4 %collective-permute-done.27.refs_2_ = bf16[64,3072]{1,0:T(8,128)(2,1)S(1)} collective-permute-done((bf16[64,3072]{1,0:T(8,128)(2,1)}, bf16[64,3072]{1,0:T(8,128)(2,1)S(1)}, u32[]{:S(2)}, u32[]{:S(2)}) %collective-permute-start.27) | collective-permute-done | bytes 393248 | tf_op jit(solution)/shard_map/ppermute | solution.py:284
  106.8 3.9 %collective-permute-done.20.refs_3_ = bf16[64,3072]{1,0:T(8,128)(2,1)} collective-permute-done((bf16[64,3072]{1,0:T(8,128)(2,1)}, bf16[64,3072]{1,0:T(8,128)(2,1)}, u32[]{:S(2)}, u32[]{:S(2)}) %collective-permute-start.20) | collective-permute-done | bytes 393248 | tf_op jit(solution)/shard_map/ppermute | solution.py:287
  111.8 3.2 %collective-permute-done.28.refs_3_ = bf16[64,3072]{1,0:T(8,128)(2,1)} collective-permute-done((bf16[64,3072]{1,0:T(8,128)(2,1)S(1)}, bf16[64,3072]{1,0:T(8,128)(2,1)}, u32[]{:S(2)}, u32[]{:S(2)}) %collective-permute-start.28) | collective-permute-done | bytes 393248 | tf_op jit(solution)/shard_map/ppermute | solution.py:287
  116.9 5.0 %front.1 = (f32[64,768]{1,0:T(8,128)}, f32[64,768]{1,0:T(8,128)}) custom-call(bf16[64,2048]{1,0:T(8,128)(2,1)} %slice.4.x_ref, bf16[2048,768]{1,0:T(8,128)(2,1)} %bitcast.23, bf16[2048,768]{1,0:T(8,128)(2,1)} %bitcast.25), custom_call_target="tpu_custom_call" | custom-call | flops 402653184 | bytes 6291456 | tf_op jit(solution)/shard_map/front/pallas_call | solution.py:406
  124.6 5.3 %back.4.so_far_ref = f32[64,768]{1,0:T(8,128)} custom-call(s32[4]{0:T(128)} %pad_add_fusion.pos_ref, bf16[64,3072]{1,0:T(8,128)(2,1)} %reshape.82.rows_ref, f32[64,768]{1,0:T(8,128)} %broadcast_in_dim.16.so_far_ref, bf16[768,2048]{1,0:T(8,128)(2,1)} %bitcast.19, bf16[64,3072]{1,0:T(8,128)(2,1)} %copy-done.8, ...), custom_call_target="tpu_custom_call" | custom-call | flops 251658240 | bytes 3145728 | tf_op jit(solution)/shard_map/back/pallas_call | solution.py:438
  129.9 5.3 %back.5.so_far_ref = f32[64,768]{1,0:T(8,128)} custom-call(s32[4]{0:T(128)} %pad_add_fusion.pos_ref, bf16[64,3072]{1,0:T(8,128)(2,1)} %reshape.82.rows_ref, f32[64,768]{1,0:T(8,128)} %back.4.so_far_ref, bf16[768,2048]{1,0:T(8,128)(2,1)} %bitcast.20, bf16[64,3072]{1,0:T(8,128)(2,1)} %copy-done.7, bf16[64,3072]{1,0:T(8,128)(2,1)} %copy-done, ...), custom_call_target="tpu_custom_call" | custom-call | flops 251658240 | bytes 3145728 | tf_op jit(solution)/shard_map/back/pallas_call | solution.py:438
  135.2 5.3 %back.6.so_far_ref = f32[64,768]{1,0:T(8,128)} custom-call(s32[4]{0:T(128)} %pad_add_fusion.pos_ref, bf16[64,3072]{1,0:T(8,128)(2,1)} %reshape.82.rows_ref, f32[64,768]{1,0:T(8,128)} %back.5.so_far_ref, bf16[768,2048]{1,0:T(8,128)(2,1)} %bitcast.21, bf16[64,3072]{1,0:T(8,128)(2,1)} %copy-done.9, bf16[64,3072]{1,0:T(8,128)(2,1)} %copy-done.2, ...), custom_call_target="tpu_custom_call" | custom-call | flops 251658240 | bytes 3145728 | tf_op jit(solution)/shard_map/back/pallas_call | solution.py:438
  140.6 5.3 %back.7.back_ref = f32[64,768]{1,0:T(8,128)} custom-call(s32[4]{0:T(128)} %pad_add_fusion.pos_ref, bf16[64,3072]{1,0:T(8,128)(2,1)} %reshape.82.rows_ref, f32[64,768]{1,0:T(8,128)} %back.6.so_far_ref, bf16[768,2048]{1,0:T(8,128)(2,1)} %bitcast.22, bf16[64,3072]{1,0:T(8,128)(2,1)} %collective-permute-done.25.refs_0_, bf16[64,3072]{1,0:T(8,128)(2,1)} %copy-done.4, ...), custom_call_target="tpu_custom_call" | custom-call | flops 251658240 | bytes 3145728 | tf_op jit(solution)/shard_map/back/pallas_call | solution.py:438
  145.9 5.8 %slot.1 = bf16[64,2048]{1,0:T(8,128)(2,1)} custom-call(f32[64,768]{1,0:T(8,128)} %back.7.back_ref, bf16[64,2176]{1,0:T(8,128)(2,1)} %copy-done.6, f32[64,768]{1,0:T(8,128)} %get-tuple-element.24.active_ref, f32[64,768]{1,0:T(8,128)} %get-tuple-element.25.slope_ref, bf16[2048,768]{1,0:T(8,128)(2,1)} %bitcast.24, bf16[2048,768]{1,0:T(8,128)(2,1)} %bitcast.26), custom_call_target="tpu_custom_call" | custom-call | flops 402653184 | bytes 6291456 | tf_op jit(solution)/shard_map/slot/pallas_call | solution.py:466
  153.5 2.9 %all-to-all-start.2 = ((bf16[32,2,2048]{2,1,0:T(2,128)(2,1)}), bf16[32,2,2048]{2,1,0:T(2,128)(2,1)S(1)}, u32[]{:S(2)}, u32[]{:S(2)}) async-start(bf16[32,2,2048]{2,1,0:T(2,128)(2,1)} %reshape.85), calls=%async_computation.2 | async-start | bytes 524288 | tf_op jit(solution)/shard_map/all_to_all | solution.py:393
  156.5 6.5 %project.4.refs_0_ = bf16[512,512]{1,0:T(8,128)(2,1)} custom-call(s32[4]{0:T(128)} %pad_add_fusion.pos_ref, bf16[512,3072]{1,0:T(8,128)(2,1)} %get-tuple-element.26.qkv_ref, bf16[64,3072]{1,0:T(8,128)(2,1)} %copy-done.8, bf16[64,3072]{1,0:T(8,128)(2,1)} %collective-permute-done.6.refs_1_, bf16[64,3072]{1,0:T(8,128)(2,1)} %collective-permute-done.7.refs_2_, ...), custom_call_target="tpu_custom_call" | custom-call | flops 1610612736 | bytes 6291456 | tf_op jit(solution)/shard_map/project/pallas_call | solution.py:453
  163.0 6.4 %project.5.refs_1_ = bf16[512,512]{1,0:T(8,128)(2,1)} custom-call(s32[4]{0:T(128)} %pad_add_fusion.pos_ref, bf16[512,3072]{1,0:T(8,128)(2,1)} %get-tuple-element.26.qkv_ref, bf16[64,3072]{1,0:T(8,128)(2,1)} %copy-done.7, bf16[64,3072]{1,0:T(8,128)(2,1)} %copy-done, bf16[64,3072]{1,0:T(8,128)(2,1)} %copy-done.1, bf16[64,3072]{1,0:T(8,128)(2,1)} %copy-done.10, ...), custom_call_target="tpu_custom_call" | custom-call | flops 1610612736 | bytes 6291456 | tf_op jit(solution)/shard_map/project/pallas_call | solution.py:453
  169.4 6.5 %project.6.refs_2_ = bf16[512,512]{1,0:T(8,128)(2,1)} custom-call(s32[4]{0:T(128)} %pad_add_fusion.pos_ref, bf16[512,3072]{1,0:T(8,128)(2,1)} %get-tuple-element.26.qkv_ref, bf16[64,3072]{1,0:T(8,128)(2,1)} %copy-done.9, bf16[64,3072]{1,0:T(8,128)(2,1)} %copy-done.2, bf16[64,3072]{1,0:T(8,128)(2,1)} %copy-done.3, ...), custom_call_target="tpu_custom_call" | custom-call | flops 1610612736 | bytes 6291456 | tf_op jit(solution)/shard_map/project/pallas_call | solution.py:453
  175.9 6.4 %project.7.refs_3_ = bf16[512,512]{1,0:T(8,128)(2,1)} custom-call(s32[4]{0:T(128)} %pad_add_fusion.pos_ref, bf16[512,3072]{1,0:T(8,128)(2,1)} %get-tuple-element.26.qkv_ref, bf16[64,3072]{1,0:T(8,128)(2,1)} %collective-permute-done.25.refs_0_, bf16[64,3072]{1,0:T(8,128)(2,1)} %copy-done.4, bf16[64,3072]{1,0:T(8,128)(2,1)} %copy-done.5, ...), custom_call_target="tpu_custom_call" | custom-call | flops 1610612736 | bytes 6291456 | tf_op jit(solution)/shard_map/project/pallas_call | solution.py:453
  183.1 3.7 %join.1 = bf16[512,2048]{1,0:T(8,128)(2,1)} custom-call(s32[4]{0:T(128)} %pad_add_fusion.pos_ref, s32[64,1]{1,0:T(8,128)} %broadcast_select_fusion.4.pick_ref, bf16[64,2048]{1,0:T(8,128)(2,1)} %reshape.86.returned_ref, bf16[512,512]{1,0:T(8,128)(2,1)} %project.4.refs_0_, bf16[512,512]{1,0:T(8,128)(2,1)} %project.5.refs_1_, bf16[512,512]{1,0:T(8,128)(2,1)} %project.6.refs_2_, ...), custom_call_target="tpu_custom_call" | custom-call | flops 134217728 | bytes 4194304 | tf_op jit(solution)/shard_map/join/pallas_call | solution.py:478
  (137 shorter events, 59.9 us)
Async XLA Ops:
  1.1 59.8 %collective-permute-start.5 = (bf16[64,3072]{1,0:T(8,128)(2,1)S(1)}, bf16[64,3072]{1,0:T(8,128)(2,1)S(1)}, u32[]{:S(2)}, u32[]{:S(2)}) collective-permute-start(bf16[64,3072]{1,0:T(8,128)(2,1)S(1)} %constant_dynamic-slice_fusion), channel_id=1, source_target_pairs={{0,1},{1,0},{2,3},{3,2},{4,5},{5,4},{6,7},{7,6},{8,9},{9,8},{10,11... | collective-permute-start | bytes 1179656 | tf_op jit(solution)/shard_map/ppermute | solution.py:273
  4.1 23.7 %collective-permute-start.9 = (bf16[64,3072]{1,0:T(8,128)(2,1)S(1)}, bf16[64,3072]{1,0:T(8,128)(2,1)S(1)}, u32[]{:S(2)}, u32[]{:S(2)}) collective-permute-start(bf16[64,3072]{1,0:T(8,128)(2,1)S(1)} %constant_dynamic-slice_fusion), channel_id=1, source_target_pairs={{0,2},{1,3},{2,4},{3,5},{4,6},{5,7},{6,0},{7,1},{8,10},{9,11},{10,... | collective-permute-start | bytes 1179656 | tf_op jit(solution)/shard_map/ppermute | solution.py:279
  27.8 44.8 %collective-permute-start.10 = (bf16[64,3072]{1,0:T(8,128)(2,1)S(1)}, bf16[64,3072]{1,0:T(8,128)(2,1)S(1)}, u32[]{:S(2)}, u32[]{:S(2)}) collective-permute-start(bf16[64,3072]{1,0:T(8,128)(2,1)S(1)} %collective-permute-done.9.refs_0_), channel_id=1, source_target_pairs={{0,16},{8,24},{16,0},{24,8},{1,17},{9,25},{17,1},{25,9},{2,18},{10... | collective-permute-start | bytes 1179656 | tf_op jit(solution)/shard_map/ppermute | solution.py:282
  30.0 44.3 %collective-permute-start.11 = (bf16[64,3072]{1,0:T(8,128)(2,1)S(1)}, bf16[64,3072]{1,0:T(8,128)(2,1)S(1)}, u32[]{:S(2)}, u32[]{:S(2)}) collective-permute-start(bf16[64,3072]{1,0:T(8,128)(2,1)S(1)} %collective-permute-done.9.refs_0_), channel_id=1, source_target_pairs={{0,1},{1,0},{2,3},{3,2},{4,5},{5,4},{6,7},{7,6},{8,9},{9,8},{10,11... | collective-permute-start | bytes 1179656 | tf_op jit(solution)/shard_map/ppermute | solution.py:284
  33.8 38.4 %collective-permute-start.17 = (bf16[64,3072]{1,0:T(8,128)(2,1)S(1)}, bf16[64,3072]{1,0:T(8,128)(2,1)S(1)}, u32[]{:S(2)}, u32[]{:S(2)}) collective-permute-start(bf16[64,3072]{1,0:T(8,128)(2,1)S(1)} %collective-permute-done.9.refs_0_), channel_id=1, source_target_pairs={{0,2},{1,3},{2,4},{3,5},{4,6},{5,7},{6,0},{7,1},{8,10},{9,11},{10,... | collective-permute-start | bytes 1179656 | tf_op jit(solution)/shard_map/ppermute | solution.py:279
  40.1 22.5 %collective-permute-start.4 = (bf16[2,512,128]{2,1,0:T(8,128)(2,1)}, bf16[2,512,128]{2,1,0:T(8,128)(2,1)S(1)}, u32[]{:S(2)}, u32[]{:S(2)}) collective-permute-start(bf16[2,512,128]{2,1,0:T(8,128)(2,1)} %get-tuple-element.22), channel_id=1, source_target_pairs={{0,1},{1,0},{2,3},{3,2},{4,5},{5,4},{6,7},{7,6},{8,9},{9,8},{10,11... | collective-permute-start | bytes 786440 | tf_op jit(solution)/shard_map/ppermute | solution.py:368
  46.2 43.1 %all-to-all-start.1 = ((bf16[32,2,2176]{2,1,0:T(2,128)(2,1)}), bf16[32,2,2176]{2,1,0:T(2,128)(2,1)}, u32[]{:S(2)}, u32[]{:S(2)}) async-start(bf16[32,2,2176]{2,1,0:T(2,128)(2,1)} %reshape.83), calls=%async_computation.1 | async-start | bytes 557056 | tf_op jit(solution)/shard_map/all_to_all | solution.py:393
  60.9 15.7 %collective-permute-start.6 = (bf16[64,3072]{1,0:T(8,128)(2,1)S(1)}, bf16[64,3072]{1,0:T(8,128)(2,1)}, u32[]{:S(2)}, u32[]{:S(2)}) collective-permute-start(bf16[64,3072]{1,0:T(8,128)(2,1)S(1)} %collective-permute-done.5.refs_0_), channel_id=1, source_target_pairs={{0,16},{8,24},{16,0},{24,8},{1,17},{9,25},{17,1},{25,9},{2,18},{10... | collective-permute-start | bytes 1179656 | tf_op jit(solution)/shard_map/ppermute | solution.py:275
  62.6 30.2 %collective-permute-start.7 = (bf16[64,3072]{1,0:T(8,128)(2,1)S(1)}, bf16[64,3072]{1,0:T(8,128)(2,1)}, u32[]{:S(2)}, u32[]{:S(2)}) collective-permute-start(bf16[64,3072]{1,0:T(8,128)(2,1)S(1)} %collective-permute-done.5.refs_0_), channel_id=1, source_target_pairs={{0,8},{8,0},{16,24},{24,16},{1,9},{9,1},{17,25},{25,17},{2,10},{10... | collective-permute-start | bytes 1179656 | tf_op jit(solution)/shard_map/ppermute | solution.py:294
  72.5 15.4 %collective-permute-start.19 = (bf16[64,3072]{1,0:T(8,128)(2,1)S(1)}, bf16[64,3072]{1,0:T(8,128)(2,1)S(1)}, u32[]{:S(2)}, u32[]{:S(2)}) collective-permute-start(bf16[64,3072]{1,0:T(8,128)(2,1)S(1)} %collective-permute-done.17.refs_0_), channel_id=1, source_target_pairs={{0,1},{1,0},{2,3},{3,2},{4,5},{5,4},{6,7},{7,6},{8,9},{9,8},{10,11... | collective-permute-start | bytes 1179656 | tf_op jit(solution)/shard_map/ppermute | solution.py:284
  74.3 12.2 %collective-permute-start.25 = (bf16[64,3072]{1,0:T(8,128)(2,1)S(1)}, bf16[64,3072]{1,0:T(8,128)(2,1)}, u32[]{:S(2)}, u32[]{:S(2)}) collective-permute-start(bf16[64,3072]{1,0:T(8,128)(2,1)S(1)} %collective-permute-done.17.refs_0_), channel_id=1, source_target_pairs={{0,2},{1,3},{2,4},{3,5},{4,6},{5,7},{6,0},{7,1},{8,10},{9,11},{10,... | collective-permute-start | bytes 1179656 | tf_op jit(solution)/shard_map/ppermute | solution.py:279
  76.5 17.8 %collective-permute-start.13 = (bf16[64,3072]{1,0:T(8,128)(2,1)S(1)}, bf16[64,3072]{1,0:T(8,128)(2,1)}, u32[]{:S(2)}, u32[]{:S(2)}) collective-permute-start(bf16[64,3072]{1,0:T(8,128)(2,1)S(1)} %collective-permute-done.9.refs_0_), channel_id=1, source_target_pairs={{0,8},{8,0},{16,24},{24,16},{1,9},{9,1},{17,25},{25,17},{2,10},{10... | collective-permute-start | bytes 1179656 | tf_op jit(solution)/shard_map/ppermute | solution.py:294
  83.1 11.2 %collective-permute-start.8 = (bf16[64,3072]{1,0:T(8,128)(2,1)}, bf16[64,3072]{1,0:T(8,128)(2,1)}, u32[]{:S(2)}, u32[]{:S(2)}) collective-permute-start(bf16[64,3072]{1,0:T(8,128)(2,1)} %collective-permute-done.6.refs_1_), channel_id=1, source_target_pairs={{0,8},{8,0},{16,24},{24,16},{1,9},{9,1},{17,25},{25,17},{2,10},{10... | collective-permute-start | bytes 1179656 | tf_op jit(solution)/shard_map/ppermute | solution.py:294
  88.0 14.7 %collective-permute-start.27 = (bf16[64,3072]{1,0:T(8,128)(2,1)}, bf16[64,3072]{1,0:T(8,128)(2,1)S(1)}, u32[]{:S(2)}, u32[]{:S(2)}) collective-permute-start(bf16[64,3072]{1,0:T(8,128)(2,1)} %collective-permute-done.25.refs_0_), channel_id=1, source_target_pairs={{0,1},{1,0},{2,3},{3,2},{4,5},{5,4},{6,7},{7,6},{8,9},{9,8},{10,11... | collective-permute-start | bytes 1179656 | tf_op jit(solution)/shard_map/ppermute | solution.py:284
  89.3 32.7 %all-to-all-start = ((bf16[32,2,3072]{2,1,0:T(2,128)(2,1)}), bf16[32,2,3072]{2,1,0:T(2,128)(2,1)}, u32[]{:S(2)}, u32[]{:S(2)}) async-start(bf16[32,2,3072]{2,1,0:T(2,128)(2,1)} %reshape.81), calls=%async_computation | async-start | bytes 786432 | tf_op jit(solution)/shard_map/all_to_all | solution.py:393
  92.8 11.3 %collective-permute-start.12 = (bf16[64,3072]{1,0:T(8,128)(2,1)}, bf16[64,3072]{1,0:T(8,128)(2,1)S(1)}, u32[]{:S(2)}, u32[]{:S(2)}) collective-permute-start(bf16[64,3072]{1,0:T(8,128)(2,1)} %broadcast_select_fusion.2), channel_id=1, source_target_pairs={{0,16},{1,17},{2,18},{3,19},{4,20},{5,21},{6,22},{7,23},{8,9},{9,8... | collective-permute-start | bytes 1179656 | tf_op jit(solution)/shard_map/ppermute | solution.py:287
  94.3 11.4 %collective-permute-start.14 = (bf16[64,3072]{1,0:T(8,128)(2,1)S(1)}, bf16[64,3072]{1,0:T(8,128)(2,1)S(1)}, u32[]{:S(2)}, u32[]{:S(2)}) collective-permute-start(bf16[64,3072]{1,0:T(8,128)(2,1)S(1)} %collective-permute-done.10.refs_1_), channel_id=1, source_target_pairs={{0,8},{8,0},{16,24},{24,16},{1,9},{9,1},{17,25},{25,17},{2,10},{10... | collective-permute-start | bytes 1179656 | tf_op jit(solution)/shard_map/ppermute | solution.py:294
  94.3 11.5 %collective-permute-start.15 = (bf16[64,3072]{1,0:T(8,128)(2,1)S(1)}, bf16[64,3072]{1,0:T(8,128)(2,1)S(1)}, u32[]{:S(2)}, u32[]{:S(2)}) collective-permute-start(bf16[64,3072]{1,0:T(8,128)(2,1)S(1)} %collective-permute-done.11.refs_2_), channel_id=1, source_target_pairs={{0,8},{8,0},{16,24},{24,16},{1,9},{9,1},{17,25},{25,17},{2,10},{10... | collective-permute-start | bytes 1179656 | tf_op jit(solution)/shard_map/ppermute | solution.py:294
  110.7 24.5 %collective-permute-start.24 = (bf16[64,3072]{1,0:T(8,128)(2,1)}, bf16[64,3072]{1,0:T(8,128)(2,1)}, u32[]{:S(2)}, u32[]{:S(2)}) collective-permute-start(bf16[64,3072]{1,0:T(8,128)(2,1)} %collective-permute-done.20.refs_3_), channel_id=1, source_target_pairs={{0,8},{8,0},{16,24},{24,16},{1,9},{9,1},{17,25},{25,17},{2,10},{10... | collective-permute-start | bytes 1179656 | tf_op jit(solution)/shard_map/ppermute | solution.py:294
  110.7 29.8 %collective-permute-start.29 = (bf16[64,3072]{1,0:T(8,128)(2,1)}, bf16[64,3072]{1,0:T(8,128)(2,1)}, u32[]{:S(2)}, u32[]{:S(2)}) collective-permute-start(bf16[64,3072]{1,0:T(8,128)(2,1)} %collective-permute-done.25.refs_0_), channel_id=1, source_target_pairs={{0,8},{8,0},{16,24},{24,16},{1,9},{9,1},{17,25},{25,17},{2,10},{10... | collective-permute-start | bytes 1179656 | tf_op jit(solution)/shard_map/ppermute | solution.py:294
  111.2 29.3 %collective-permute-start.30 = (bf16[64,3072]{1,0:T(8,128)(2,1)S(1)}, bf16[64,3072]{1,0:T(8,128)(2,1)}, u32[]{:S(2)}, u32[]{:S(2)}) collective-permute-start(bf16[64,3072]{1,0:T(8,128)(2,1)S(1)} %collective-permute-done.26.refs_1_), channel_id=1, source_target_pairs={{0,8},{8,0},{16,24},{24,16},{1,9},{9,1},{17,25},{25,17},{2,10},{10... | collective-permute-start | bytes 1179656 | tf_op jit(solution)/shard_map/ppermute | solution.py:294
  111.3 29.2 %collective-permute-start.31 = (bf16[64,3072]{1,0:T(8,128)(2,1)S(1)}, bf16[64,3072]{1,0:T(8,128)(2,1)}, u32[]{:S(2)}, u32[]{:S(2)}) collective-permute-start(bf16[64,3072]{1,0:T(8,128)(2,1)S(1)} %collective-permute-done.27.refs_2_), channel_id=1, source_target_pairs={{0,8},{8,0},{16,24},{24,16},{1,9},{9,1},{17,25},{25,17},{2,10},{10... | collective-permute-start | bytes 1179656 | tf_op jit(solution)/shard_map/ppermute | solution.py:294
  115.0 25.6 %collective-permute-start.32 = (bf16[64,3072]{1,0:T(8,128)(2,1)}, bf16[64,3072]{1,0:T(8,128)(2,1)}, u32[]{:S(2)}, u32[]{:S(2)}) collective-permute-start(bf16[64,3072]{1,0:T(8,128)(2,1)} %collective-permute-done.28.refs_3_), channel_id=1, source_target_pairs={{0,8},{8,0},{16,24},{24,16},{1,9},{9,1},{17,25},{25,17},{2,10},{10... | collective-permute-start | bytes 1179656 | tf_op jit(solution)/shard_map/ppermute | solution.py:294
  153.5 28.8 %all-to-all-start.2 = ((bf16[32,2,2048]{2,1,0:T(2,128)(2,1)}), bf16[32,2,2048]{2,1,0:T(2,128)(2,1)S(1)}, u32[]{:S(2)}, u32[]{:S(2)}) async-start(bf16[32,2,2048]{2,1,0:T(2,128)(2,1)} %reshape.85), calls=%async_computation.2 | async-start | bytes 524288 | tf_op jit(solution)/shard_map/all_to_all | solution.py:393
  (37 other events, 534.8 us)

commit v2 on v0

v2 whole, which is shorter than its diff:
```python
import functools
import math

import jax
import jax.numpy as jnp
from jax import lax
from jax.experimental import pallas as pl
from jax.experimental.pallas import tpu as pltpu
from jax.sharding import PartitionSpec as P

DH = 128
MIB = 1024 * 1024
LARGE = 52
F32 = jnp.float32
BF16 = jnp.bfloat16
LAST = (((1,), (1,)), ((), ()))
FIRST = (((0,), (0,)), ((), ()))
PLAIN = (((1,), (0,)), ((), ()))


def dot(left, right, contract):
    return lax.dot_general(left, right, contract, preferred_element_type=F32)


def in_vmem():
    return pl.BlockSpec(memory_space=pltpu.VMEM)


def in_smem():
    return pl.BlockSpec(memory_space=pltpu.SMEM)


def anywhere():
    return pl.BlockSpec(memory_space=pl.ANY)


def params(mib=6):
    return pltpu.CompilerParams(vmem_limit_bytes=mib * MIB)


def small():
    return pl.CostEstimate(flops=1, bytes_accessed=1, transcendentals=0)


def lane_slice(start, size):
    return pl.ds(pl.multiple_of(start, DH), size)


class Plan:
    def __init__(self):
        self.grp = lax.axis_size("grp")
        self.ctx = lax.axis_size("ctx")
        self.cores = 2 if self.grp % 2 == 0 else 1
        self.cross = self.grp // self.cores
        inner = 1
        while inner * inner * 4 <= self.ctx and self.ctx % (inner * 2) == 0:
            inner *= 2
        self.inner = inner
        self.outer = self.ctx // inner

    def outer_turn(self, k):
        a, b = self.outer, self.inner
        return [(z * b + y, ((z + k) % a) * b + y) for z in range(a) for y in range(b)]

    def inner_turn(self, k):
        a, b = self.outer, self.inner
        return [(z * b + y, z * b + (y + k) % b) for z in range(a) for y in range(b)]

    def pairs(self, go):
        found = []
        for g in range(self.grp):
            x, c = divmod(g, self.cores)
            for at in range(self.ctx):
                z, y = divmod(at, self.inner)
                goal = go(x, c, z, y)
                if goal is not None:
                    x2, c2, z2, y2 = goal
                    to = (x2 % self.cross * self.cores + c2) * self.ctx
                    found.append((g * self.ctx + at, to + z2 * self.inner + y2 % self.inner))
        return found

    def move(self, array, go):
        return lax.ppermute(array, ("grp", "ctx"), self.pairs(go))

    def swap(self, array):
        return self.move(array, lambda x, c, z, y: (x, 1 - c, z, y))


def state_kernel(inner, turn, pos_ref, q_ref, k_ref, v_ref, g_ref, out_ref):
    each = out_ref.shape[1]
    base = lax.rem(pos_ref[3] + turn, inner) * each
    for h in range(each // DH):
        lanes = lane_slice(base + h * DH, DH)
        rows = slice(h * DH, (h + 1) * DH)
        out_ref[0, rows, :] = dot(v_ref[:, lanes], k_ref[:, lanes], FIRST).astype(BF16)
        out_ref[1, rows, :] = dot(g_ref[:, lanes], q_ref[:, lanes], FIRST).astype(BF16)


def total_kernel(inner, outer, pos_ref, *refs):
    ins, outs = refs[:inner], refs[inner:]
    total = ins[0][...].astype(F32)
    for ref in ins[1:]:
        total = total + ref[...].astype(F32)
    values, grads = total[0].astype(BF16), total[1].astype(BF16)
    for k, out in enumerate(outs, 1):
        out[...] = jnp.where(pos_ref[2] + k < outer, values, grads)


def spread_kernel(inner, outer, pos_ref, *refs):
    own, far, outs = refs[:inner], refs[inner : inner + outer - 1], refs[inner + outer - 1 :]
    z, y = pos_ref[2], pos_ref[3]
    shape = own[0].shape[1:]
    before = jnp.zeros(shape, F32)
    after = jnp.zeros(shape, F32)
    for k, ref in enumerate(far, 1):
        piece = ref[...].astype(F32)
        before = before + jnp.where(z >= k, piece, 0.0)
        after = after + jnp.where(z < k, piece, 0.0)
    for i, out in enumerate(outs):
        goal = lax.rem(y + i, inner)
        low, high = before, after
        for k, ref in enumerate(own):
            source = lax.rem(y + inner - k, inner)
            low = low + jnp.where(source < goal, ref[0].astype(F32), 0.0)
            high = high + jnp.where(source > goal, ref[1].astype(F32), 0.0)
        out[0] = low.astype(BF16)
        out[1] = high.astype(BF16)


def near_kernel(scaling, first, pos_ref, q_ref, k_ref, v_ref, g_ref, out_ref):
    rows = q_ref.shape[0]
    half = rows // 2
    early, late = slice(0, half), slice(half, rows)
    row = lax.broadcasted_iota(jnp.int32, (half, half), 0)
    column = lax.broadcasted_iota(jnp.int32, (half, half), 1)

    def scores(left, right, keep):
        value = scaling * dot(left, right, LAST)
        if keep is not None:
            value = jnp.where(keep, value, 0.0)
        return value.astype(BF16)

    def past(left, right, values):
        first = scores(left[early], right[early], row >= column)
        cross = scores(left[late], right[early], None)
        second = scores(left[late], right[late], row >= column)
        low = dot(first, values[early], PLAIN)
        high = dot(cross, values[early], PLAIN) + dot(second, values[late], PLAIN)
        return low, high

    def future(left, right, values):
        first = scores(left[early], right[early], row <= column)
        cross = scores(left[early], right[late], None)
        second = scores(left[late], right[late], row <= column)
        low = dot(first, values[early], PLAIN) + dot(cross, values[late], PLAIN)
        high = dot(second, values[late], PLAIN)
        return low, high

    def one_head(h, carry):
        lanes = lane_slice((first + h) * DH, DH)
        q, k, v, g = q_ref[:, lanes], k_ref[:, lanes], v_ref[:, lanes], g_ref[:, lanes]
        goal = lane_slice(h * DH, DH)
        for n, (low, high) in enumerate((past(g, v, k), future(v, g, q), future(k, q, g))):
            out_ref[n, early, goal] = low.astype(BF16)
            out_ref[n, late, goal] = high.astype(BF16)
        return carry

    lax.fori_loop(0, out_ref.shape[2] // DH, one_head, 0)


def input_rows_kernel(chosen_ref, pad_ref, combine_ref, x_ref, out_ref, picks_ref, ones, tail):
    rows, width = x_ref.shape
    slots = chosen_ref.shape[3]
    row = lax.broadcasted_iota(jnp.int32, (1, rows), 1)
    lane = lax.broadcasted_iota(jnp.int32, (1, DH), 1)

    def one_slot(n, carry):
        expert, slot = lax.div(n, slots), lax.rem(n, slots)
        live = slot < slots - pad_ref[0, 0, expert]
        token = jnp.where(live, chosen_ref[0, 0, expert, slot], -1)
        ones[pl.ds(n, 1), :] = jnp.where(row == token, 1.0, 0.0)
        weight = jnp.full((1, DH), jnp.where(live, combine_ref[0, 0, expert, slot], 0.0), F32)
        upper = weight.astype(BF16).astype(F32)
        both = jnp.where(lane == 0, upper, jnp.where(lane == 1, weight - upper, 0.0))
        tail[pl.ds(n, 1), :] = both
        return carry

    lax.fori_loop(0, out_ref.shape[0], one_slot, 0)
    picks = ones[...].astype(BF16)
    picks_ref[...] = picks
    out_ref[:, :width] = dot(picks, x_ref[...], PLAIN).astype(BF16)
    out_ref[:, width:] = tail[...].astype(BF16)


def far_kernel(plan, cuts, scaling, pos_ref, picks_ref, k_ref, v_ref, g_ref, *refs):
    inner = plan.inner
    states, near, (qkv_ref, rows_ref) = refs[:inner], refs[inner : inner + cuts], refs[-2:]
    picks = picks_ref[...]
    x = lax.div(pos_ref[0], plan.cores)
    depth = qkv_ref.shape[1] // plan.cross
    rows, channels = k_ref.shape
    heads = channels // DH
    each = heads // inner
    for h in range(heads):
        lanes = slice(h * DH, (h + 1) * DH)
        turn = lax.rem(pos_ref[3] + inner - h // each, inner)
        inside = slice((h % each) * DH, (h % each + 1) * DH)
        pair = states[0][:, inside, :]
        for i in range(1, inner):
            pair = jnp.where(turn == i, states[i][:, inside, :], pair)
        parts = (
            dot(g_ref[:, lanes], pair[0], PLAIN),
            dot(v_ref[:, lanes], pair[1], PLAIN),
            dot(k_ref[:, lanes], pair[1], LAST),
        )
        share = heads // cuts
        near_lanes = slice((h % share) * DH, (h % share + 1) * DH)
        for n, part in enumerate(parts):
            whole = near[h // share][n, :, near_lanes].astype(F32) + scaling * part
            whole = whole.astype(BF16)
            part_at, inside_at = divmod((n * heads + h) * DH, depth)
            start = lax.rem(x + plan.cross - part_at, plan.cross) * depth + inside_at
            qkv_ref[:, lane_slice(start, DH)] = whole
            start = (n * heads + h) * DH
            rows_ref[:, start : start + DH] = dot(picks, whole, PLAIN).astype(BF16)


def turn_kernel(pos_ref, in_ref, out_ref):
    out_ref[...] = in_ref[...].T


def turned(plan, weight, pos, mode):
    block = (weight.shape[0], weight.shape[1] // plan.grp)
    cross, cores = plan.cross, plan.cores
    steps = {"own": 1, "part": cores, "whole": plan.grp}[mode]

    def source(n, at):
        if mode == "whole":
            return (0, n)
        return (0, at[0] // cores * cores + n if mode == "part" else at[0])

    def place(n, at):
        if mode != "whole":
            return (n, 0)
        return (lax.rem(at[0] // cores + cross - n // cores, cross) * cores + n % cores, 0)

    return pl.pallas_call(
        turn_kernel,
        out_shape=jax.ShapeDtypeStruct((steps * block[1], weight.shape[0]), BF16),
        grid_spec=pltpu.PrefetchScalarGridSpec(
            num_scalar_prefetch=1,
            grid=(steps,),
            in_specs=[pl.BlockSpec(block, source)],
            out_specs=pl.BlockSpec((block[1], block[0]), place),
        ),
        compiler_params=params(),
        cost_estimate=small(),
        name="turned",
    )(pos, weight)


class Pieces:
    def __init__(self, plan, entries, pos_ref, refs, ring, sems):
        self.plan, self.pos_ref, self.ring, self.sems = plan, pos_ref, ring, sems
        self.core = lax.rem(pos_ref[0], plan.cores)
        self.found = {}
        sources = list(refs)
        for turn, dx, dy, skip, first in entries:
            pair = [sources.pop(0) for _ in range(1 if first is None else 2)]
            self.found.setdefault((turn, dy), []).append((dx, skip, first, pair))
        for n in range(len(self.found)):
            self.copy(n, True)

    def copy(self, n, start):
        depth = self.ring.shape[1] // self.plan.cross
        parts = list(self.found.values())[n]
        for m, (dx, skip, first, pair) in enumerate(parts):
            deep = pair[0].shape[0]
            at = 0 if dx is None else dx * depth + skip * (depth // 2)
            goal = self.ring.at[n, pl.ds(at, deep), :]
            copy = pltpu.make_async_copy(pair[0], goal, self.sems.at[n, m])
            if not start:
                copy.wait()
            elif first is None:
                copy.start()
            else:
                other = pltpu.make_async_copy(pair[1], goal, self.sems.at[n, m])
                pl.when(self.core == first)(copy.start)
                pl.when(self.core != first)(other.start)

    def blocks(self):
        plan = self.plan
        wide = self.ring.shape[2]
        for n, (turn, dy) in enumerate(self.found):
            self.copy(n, False)
            z = lax.rem(self.pos_ref[2] + plan.outer - turn, plan.outer)
            y = lax.rem(self.pos_ref[3] + plan.inner - dy, plan.inner)
            yield lane_slice((z * plan.inner + y) * wide, wide), self.ring.at[n]


def ring_scratch(found):
    wide = found[0][1][0].shape[1]
    depths = {}
    for (turn, _, dy, _, _), buffers in found:
        depths[turn, dy] = depths.get((turn, dy), 0) + buffers[0].shape[0]
    ring = pltpu.VMEM((len(depths), max(depths.values()), wide), BF16)
    return [ring, pltpu.SemaphoreType.DMA((len(depths), len(found)))]


def reach_blocks(plan, pos_ref, rows_ref, pieces, turned_ref):
    x = lax.div(pos_ref[0], plan.cores)
    depth = turned_ref.shape[1] // plan.cross
    for dx in range(plan.cross):
        lanes = lane_slice(lax.rem(x + plan.cross - dx, plan.cross) * depth, depth)
        turned_ref[:, dx * depth : (dx + 1) * depth] = rows_ref[:, lanes]
    return [
        (lanes, dot(turned_ref[...], block[...], PLAIN).astype(BF16))
        for lanes, block in pieces.blocks()
    ]


def start_loads(sems, *pairs):
    loads = [pltpu.make_async_copy(x, y, sems.at[n]) for n, (x, y) in enumerate(pairs)]
    for load in loads:
        load.start()
    return loads


def reach_kernel(plan, entries, pos_ref, rows_ref, down_hbm, *refs):
    pieces, (back_ref, turned_ref, down_ref, loaded, ring, sems) = refs[:-6], refs[-6:]
    pieces = Pieces(plan, entries, pos_ref, pieces, ring, sems)
    (load,) = start_loads(loaded, (down_hbm, down_ref))
    blocks = reach_blocks(plan, pos_ref, rows_ref, pieces, turned_ref)
    load.wait()
    back_ref[...] = jnp.zeros_like(back_ref)
    for lanes, grads in blocks:
        back_ref[...] += dot(down_ref[:, lanes], grads, LAST)


def expert_kernel(plan, entries, pos_ref, rows_ref, packed_ref, back_ref, *refs):
    hbm, refs = refs[:3], refs[3:]
    pieces, (out_ref, held, turned_ref) = refs[:-9], refs[-9:-6]
    (gate_ref, up_ref, down_ref), (loaded, ring, sems) = refs[-6:-3], refs[-3:]
    pieces = Pieces(plan, entries, pos_ref, pieces, ring, sems)
    loads = start_loads(loaded, *zip(hbm, (gate_ref, up_ref, down_ref), strict=True))
    blocks = reach_blocks(plan, pos_ref, rows_ref, pieces, turned_ref)
    width = out_ref.shape[1]
    loads[0].wait()
    gate = dot(packed_ref[:, :width], gate_ref[...], PLAIN)
    loads[1].wait()
    up = dot(packed_ref[:, :width], up_ref[...], PLAIN)
    sigma = jax.nn.sigmoid(gate)
    active = gate * sigma
    slope = up * (sigma * (1.0 + gate * (1.0 - sigma)))
    loads[2].wait()
    held[...] = back_ref[...]
    for lanes, grads in blocks:
        held[...] += dot(down_ref[:, lanes], grads, LAST)
    weight = packed_ref[:, width : width + 1].astype(F32)
    weight = weight + packed_ref[:, width + 1 : width + 2].astype(F32)
    hidden = weight * held[...].T
    up_grad = (hidden * active).astype(BF16)
    gate_grad = (hidden * slope).astype(BF16)
    steps = 4
    for n in range(steps):
        some = slice(n * width // steps, (n + 1) * width // steps)
        total = dot(gate_ref[some], gate_grad, LAST) + dot(up_ref[some], up_grad, LAST)
        out_ref[:, some] = total.T.astype(BF16)


def project_kernel(plan, entries, pos_ref, qkv_hbm, *refs):
    pieces, (out_ref, qkv_ref, loaded, ring, sems) = refs[:-5], refs[-5:]
    (load,) = start_loads(loaded, (qkv_hbm, qkv_ref))
    pieces = Pieces(plan, entries, pos_ref, pieces, ring, sems)
    load.wait()
    half = out_ref.shape[0] // 2
    depth = qkv_ref.shape[1] // plan.cross
    for lanes, block in pieces.blocks():
        for n in range(2):
            rows = slice(n * half, (n + 1) * half)
            total = None
            for dx in range(plan.cross):
                deep = slice(dx * depth, (dx + 1) * depth)
                term = dot(qkv_ref[rows, deep], block[deep, :], PLAIN)
                total = term if total is None else total + term
            out_ref[rows, lanes] = total.astype(BF16)


def join_kernel(picks_ref, returned_ref, token_ref, out_ref):
    added = dot(picks_ref[...], returned_ref[...], FIRST)
    out_ref[...] = (token_ref[...].astype(F32) + added).astype(BF16)


def together(*values):
    return lax.optimization_barrier(values)


class Turn:
    def __init__(self, plan, turn, held):
        self.plan, self.turn, self.held = plan, turn, held
        self.core = lax.rem(lax.axis_index("grp"), plan.cores)
        self.first = self.mixed(held)

    def mixed(self, array):
        plan, moved = self.plan, {}
        for k in range(1, max(plan.cross, plan.inner)):

            def go(x, c, z, y, k=k):
                if c == 0:
                    return (x + k, c, z, y) if k < plan.cross else None
                return (x, c, z, y + k) if k < plan.inner else None

            moved[k] = plan.move(array, go)
        return moved

    def swap(self):
        self.other = self.plan.swap(self.held)

    def again(self):
        self.second = self.mixed(self.other)

    def turn_corners(self):
        plan = self.plan
        self.corners = {}
        for dx in range(1, plan.cross):
            for dy in range(1, plan.inner):
                sent = self.second[dx]
                if dx != dy:
                    sent = jnp.where(self.core == 0, sent, self.second[dy])

                def go(x, c, z, y, dx=dx, dy=dy):
                    return (x, c, z, y + dy) if c == 0 else (x + dx, c, z, y)

                self.corners[dx, dy] = plan.move(sent, go)

    def pieces(self):
        plan, turn = self.plan, self.turn
        found = [((turn, 0, 0, n, n), (self.held, self.other)) for n in range(2)]
        for k, array in self.first.items():
            first = (array, plan.swap(array))
            second = (self.second[k], plan.swap(self.second[k]))
            if k < plan.cross:
                found.append(((turn, k, 0, 0, 0), first))
                found.append(((turn, k, 0, 1, 0), second))
            if k < plan.inner:
                found.append(((turn, 0, k, 0, 1), second))
                found.append(((turn, 0, k, 1, 1), first))
        for (dx, dy), array in self.corners.items():
            pair = (array, plan.swap(array))
            found.append(((turn, dx, dy, 0, 1), pair))
            found.append(((turn, dx, dy, 1, 0), pair))
        return found


def local(
    inputs,
    queries,
    key_heads,
    value_heads,
    out_grad,
    qkv_weight,
    gate_weight,
    up_weight,
    down_weight,
    chosen,
    pad_counts,
    combine,
):
    plan = Plan()
    rows, width = inputs.shape[1:]
    channels = queries.shape[2]
    heads = channels // DH
    scaling = 1.0 / math.sqrt(plan.ctx * rows * DH)
    q, k, v, g = queries[0], key_heads[0], value_heads[0], out_grad[0]
    gate_mat, up_mat, down_mat = gate_weight[0], up_weight[0], down_weight[0]
    hidden = gate_mat.shape[1]
    experts, slots = chosen.shape[2:]
    items = experts * slots
    inner, outer = plan.inner, plan.outer
    grp_at, ctx_at = lax.axis_index("grp"), lax.axis_index("ctx")
    pos = jnp.stack([grp_at, ctx_at, ctx_at // inner, ctx_at % inner]).astype(jnp.int32)
    across = range(1, plan.cross)
    part = jax.ShapeDtypeStruct((2, channels // inner, DH), BF16)
    own = [None] * inner
    for i in reversed(range(inner)):
        own[i] = pl.pallas_call(
            functools.partial(state_kernel, inner, i),
            out_shape=part,
            in_specs=[in_smem()] + [in_vmem()] * 4,
            out_specs=in_vmem(),
            compiler_params=params(),
            cost_estimate=small(),
            name="states",
        )(pos, q, k, v, g)
    shares = [lax.ppermute(own[i], "ctx", plan.inner_turn(i)) for i in range(1, inner)]
    (later, *_) = together(pos, own[-1])
    held = turned(plan, qkv_weight, later, "own")
    held = lax.ppermute(held, "ctx", plan.outer_turn(1))
    packed, picks = pl.pallas_call(
        input_rows_kernel,
        out_shape=[
            jax.ShapeDtypeStruct((items, width + DH), BF16),
            jax.ShapeDtypeStruct((items, rows), BF16),
        ],
        in_specs=[in_smem()] * 3 + [in_vmem()],
        out_specs=[in_vmem()] * 2,
        scratch_shapes=[pltpu.VMEM((items, rows), F32), pltpu.VMEM((items, DH), F32)],
        compiler_params=params(),
        cost_estimate=small(),
        name="input_rows",
    )(chosen, pad_counts, combine, inputs[0])
    packed, picks, *shares = together(packed, picks, own[0], *shares)
    totals = pl.pallas_call(
        functools.partial(total_kernel, inner, outer),
        out_shape=[jax.ShapeDtypeStruct(part.shape[1:], BF16)] * (outer - 1),
        in_specs=[in_smem()] + [in_vmem()] * inner,
        out_specs=[in_vmem()] * (outer - 1),
        compiler_params=params(),
        cost_estimate=small(),
        name="totals",
    )(pos, *shares)
    after_totals, *totals = together(pos, *totals)
    far = [lax.ppermute(totals[i - 1], "ctx", plan.outer_turn(i)) for i in range(1, outer)]
    aside = turned(plan, qkv_weight, after_totals, "part")
    beside = [
        plan.move(aside, lambda x, c, z, y, dy=dy: (x, c, z, y + dy) if c == 1 else None)
        for dy in range(1, inner)
    ]

    cuts = 2 if heads % 2 == 0 else 1

    def near_part(cut, after):
        return pl.pallas_call(
            functools.partial(near_kernel, scaling, cut * (heads // cuts)),
            out_shape=jax.ShapeDtypeStruct((3, rows, channels // cuts), BF16),
            in_specs=[in_smem()] + [in_vmem()] * 4,
            out_specs=in_vmem(),
            compiler_params=params(),
            cost_estimate=small(),
            name="near",
        )(after, q, k, v, g)

    near = [near_part(0, after_totals)]
    after_near, held, near[0], *arrived = together(after_totals, held, near[0], *far[:1])
    far[:1] = arrived
    turns = []
    if outer > 1:
        turns.append(Turn(plan, 1, held))
        turns[0].swap()
    if outer > 2:
        held = lax.ppermute(held, "ctx", plan.outer_turn(1))
    near += [near_part(cut, after_near) for cut in range(1, cuts)]
    if turns:
        near[-1], turns[0].other = together(near[-1], turns[0].other)
        turns[0].again()

    def exchange(array):
        return lax.all_to_all(array, ("grp", "ctx"), split_axis=0, concat_axis=0, tiled=True)

    shares[0], *arrived = together(shares[0], *far, *near, *beside)
    far, near = arrived[: outer - 1], arrived[outer - 1 : outer - 1 + cuts]
    beside = arrived[outer - 1 + cuts :]
    sums = pl.pallas_call(
        functools.partial(spread_kernel, inner, outer),
        out_shape=[part] * inner,
        in_specs=[in_smem()] + [in_vmem()] * (inner + outer - 1),
        out_specs=[in_vmem()] * inner,
        compiler_params=params(),
        cost_estimate=small(),
        name="sums",
    )(pos, *shares, *far)
    states = [lax.ppermute(sums[i], "ctx", plan.inner_turn(i)) for i in range(1, inner)]
    state = sums[0]
    behind = []
    if turns:
        state, held, *arrived = together(state, held, *turns[0].first.values())
        turns[0].first = dict(zip(turns[0].first, arrived, strict=True))
    moving = dict(turns[0].second) if turns else {}
    if outer > 2:
        turns.append(Turn(plan, 2, held))
        turns[1].swap()
        if outer > 3:
            held = lax.ppermute(held, "ctx", plan.outer_turn(1))
        behind = [held, turns[1].other, *turns[1].first.values()]
    state, *arrived = together(state, *states, *moving.values(), *behind)
    states, arrived = [state, *arrived[: len(states)]], arrived[len(states) :]
    if turns:
        turns[0].second = dict(zip(moving, arrived, strict=False))
        turns[0].turn_corners()
        arrived = arrived[len(moving) :]
    if outer > 2:
        held, turns[1].other, *arrived = arrived
        turns[1].first = dict(zip(turns[1].first, arrived, strict=True))
        turns[1].again()

    qkv_grad, sent_rows = pl.pallas_call(
        functools.partial(far_kernel, plan, cuts, scaling),
        out_shape=[
            jax.ShapeDtypeStruct((rows, 3 * channels), BF16),
            jax.ShapeDtypeStruct((items, 3 * channels), BF16),
        ],
        in_specs=[in_smem()] + [in_vmem()] * (4 + inner + cuts),
        out_specs=[in_vmem()] * 2,
        compiler_params=params(8),
        cost_estimate=small(),
        name="far",
    )(pos, picks, k, v, g, *states, *near)
    for turn in range(3, outer):
        if turn > 3:
            held = lax.ppermute(held, "ctx", plan.outer_turn(1))
        turns.append(Turn(plan, turn, held))
        turns[-1].swap()
    qkv_grad, *beside = together(qkv_grad, *beside)
    aside = [
        [plan.move(x0, lambda x, c, z, y, dx=dx: (x + dx, c, z, y) if c == 1 else None) for dx in across]
        for x0 in beside
    ]
    others = [turn.other for turn in turns[2:]]
    for turn in turns[2:]:
        turn.again()
    sent_rows, *_ = together(sent_rows, *others)
    grad_rows = exchange(sent_rows)
    waits = [turn.first for turn in turns] + [turns[0].corners] + [turn.second for turn in turns[:2]]
    waits.append(dict(enumerate(beside)))
    waits += [dict(enumerate(arrays)) for arrays in aside]
    flat = [array for wait in waits for array in wait.values()]
    grad_rows, packed, *arrived = together(grad_rows, packed, *flat)
    came = exchange(packed)
    for wait in waits:
        for key in wait:
            wait[key] = arrived.pop(0)
    beside, aside = waits[-1 - len(aside)], waits[len(waits) - len(aside) :]
    if outer > 2:
        turns[1].turn_corners()
    whole = turned(plan, qkv_weight, later, "whole")
    found = [((0, None, 0, 0, None), (whole,))]
    for turn in turns[:-1]:
        found.extend(turn.pieces())
    for dy in range(1, inner):
        for dx in range(plan.cross):
            array = beside[dy - 1] if dx == 0 else aside[dy - 1][dx - 1]
            copied = plan.move(array, lambda x, c, z, y: (x, 0, z, y) if c == 1 else None)
            found.append(((0, dx, dy, 0, 1), (array, copied)))

    def some(keep):
        kept = [item for item in found if keep(item[0][0])]
        return kept, [item[0] for item in kept], [x for item in kept for x in item[1]]

    span = inner * qkv_weight.shape[0]

    turned_rows = pltpu.VMEM((items, 3 * channels), BF16)
    qkv_held = pltpu.VMEM((rows, 3 * channels), BF16)
    down_held = pltpu.VMEM((hidden, width), BF16)

    split = max(outer - 2, 1)
    kept, entries, pieces = some(lambda turn: turn < split)
    back = pl.pallas_call(
        functools.partial(reach_kernel, plan, entries),
        out_shape=jax.ShapeDtypeStruct((hidden, items), F32),
        in_specs=[in_smem(), in_vmem()] + [anywhere()] * (1 + len(pieces)),
        out_specs=in_vmem(),
        scratch_shapes=[
            *(turned_rows, down_held, pltpu.SemaphoreType.DMA((1,))),
            *ring_scratch(kept),
        ],
        compiler_params=params(LARGE),
        cost_estimate=small(),
        name="reach",
    )(pos, grad_rows, down_mat, *pieces)
    if turns:
        last = turns[-1]
        if outer > 2:
            last.turn_corners()
        back, *arrived = together(back, *last.corners.values())
        last.corners = dict(zip(last.corners, arrived, strict=True))
    if turns:
        found.extend(turns[-1].pieces())
    kept, entries, pieces = some(lambda turn: turn >= split)
    slot_grad = pl.pallas_call(
        functools.partial(expert_kernel, plan, entries),
        out_shape=jax.ShapeDtypeStruct((items, width), BF16),
        in_specs=[in_smem()] + [in_vmem()] * 3 + [anywhere()] * (3 + len(pieces)),
        out_specs=in_vmem(),
        scratch_shapes=[
            *(pltpu.VMEM((hidden, items), F32), turned_rows),
            *[pltpu.VMEM((width, hidden), BF16)] * 2,
            *(down_held, pltpu.SemaphoreType.DMA((3,))),
            *ring_scratch(kept),
        ],
        compiler_params=params(LARGE),
        cost_estimate=small(),
        name="expert",
    )(pos, grad_rows, came, back, gate_mat, up_mat, down_mat, *pieces)
    returned = exchange(slot_grad)
    kept, entries, pieces = some(lambda turn: True)
    (after_expert, *_) = together(pos, slot_grad)
    token_grad = pl.pallas_call(
        functools.partial(project_kernel, plan, entries),
        out_shape=jax.ShapeDtypeStruct((rows, width), BF16),
        in_specs=[in_smem()] + [anywhere()] * (1 + len(pieces)),
        out_specs=in_vmem(),
        scratch_shapes=[qkv_held, pltpu.SemaphoreType.DMA((1,)), *ring_scratch(kept)],
        compiler_params=params(LARGE),
        cost_estimate=small(),
        name="project",
    )(after_expert, qkv_grad, *pieces)
    column = pl.BlockSpec((rows, span), lambda n: (0, n))
    total = pl.pallas_call(
        join_kernel,
        out_shape=jax.ShapeDtypeStruct((rows, width), BF16),
        grid=(outer,),
        in_specs=[
            pl.BlockSpec((items, rows), lambda n: (0, 0)),
            pl.BlockSpec((items, span), lambda n: (0, n)),
            column,
        ],
        out_specs=column,
        compiler_params=params(8),
        cost_estimate=small(),
        name="join",
    )(picks, returned, token_grad)
    return total[None]


def solution(mesh):
    rows = P("grp", "ctx", None)
    expert = P(("grp", "ctx"), None, None)
    lists = P("grp", "ctx", None, None)
    return jax.shard_map(
        local,
        mesh=mesh,
        in_specs=(rows,) * 5 + (P("ctx", None),) + (expert,) * 3 + (lists, rows, lists),
        out_specs=rows,
        check_vma=False,
    )
```

time: 369 us -> 166 us (0.45)
  waiting for transfers between devices: 229 us -> 40.1 us
  Pallas kernels: 0 us -> 53.9 us
  matrix products: 52 us -> 0 us
  starting transfers between devices: 13.4 us -> 46.9 us
  other arithmetic: 18.6 us -> 0.08 us
  blocking collectives: 13.3 us -> 0 us
  between operations: 13.7 us -> 0.48 us
  local copies, waits for them, and re-layouts: 27.9 us -> 23.5 us
    all_gather x2 -> x0, waiting for transfers between devices: 211 us -> none  [the longest x1 154 us: local(): lax.all_gather(qkv_weight, 'ctx', axis=0, tiled=True)]
    pallas_call x0 -> x15, Pallas kernels: none -> 53.9 us  [the longest x1 14.1 us: local(): pl.pallas_call(functools.partial(project_kernel, plan, entries), out_shap...]
    dot_general x17 -> x0, matrix products: 52 us -> none  [the longest x1 13.7 us: local(): jnp.einsum('tc,rc->tr', qkv_grad, lax.all_gather(qkv_weight, 'ctx', axis=...]
    ppermute x0 -> x33, starting transfers between devices: none -> 33.5 us  [the longest x25 21 us: move(): return lax.ppermute(array, ('grp', 'ctx'), self.pairs(go))]
    ppermute x0 -> x33, waiting for transfers between devices: none -> 30 us  [the longest x3 11.8 us: local(): lax.ppermute(totals[i - 1], 'ctx', plan.outer_turn(i))]
    all_to_all x1 -> x0, blocking collectives: 13.3 us -> none  [local(): lax.all_to_all(input_rows, ('grp', 'ctx'), split_axis=0, concat_axis=0, t...]
    gather x4 -> x0, local copies, waits for them, and re-layouts: 7.62 us -> none  [the longest x2 3.88 us: local(): input_rows = jnp.take(inputs[0], chosen_rows, axis=0)]
    all_to_all x0 -> x6, local copies, waits for them, and re-layouts: none -> 7.6 us  [exchange(): lax.all_to_all(array, ('grp', 'ctx'), split_axis=0, concat_axis=0, tiled=...]
  transfers between devices with their start and end apart: 5 -> 36, of which waited for: 4 -> 11; matrix products, arithmetic and copies ran while one was open for 15% -> 0% of each run, Pallas kernels for 0% -> 24%
where the time goes in v2:
time: 166 us; the launch traced here: 165 us
  Pallas kernels  53.9 us (32%)
  starting transfers between devices  46.9 us (28%)
  waiting for transfers between devices  40.1 us (24%)
  local copies, waits for them, and re-layouts  23.5 us (14%)
    ppermute x25, starting transfers between devices, move(): return lax.ppermute(array, ('grp', 'ctx'), self.pairs(go))  21 us
    unnamed x84, local copies, waits for them, and re-layouts  15.9 us
    pallas_call x1, Pallas kernels, local(): pl.pallas_call(functools.partial(project_kernel, plan, entries), out_shap...  14.1 us
    all_to_all x3, starting transfers between devices, exchange(): lax.all_to_all(array, ('grp', 'ctx'), split_axis=0, concat_axis=0, tiled=...  13.3 us
    ppermute x3, waiting for transfers between devices, local(): lax.ppermute(totals[i - 1], 'ctx', plan.outer_turn(i))  11.8 us
    all_to_all x3, waiting for transfers between devices, exchange(): lax.all_to_all(array, ('grp', 'ctx'), split_axis=0, concat_axis=0, tiled=...  10.1 us
    ppermute x25, waiting for transfers between devices, move(): return lax.ppermute(array, ('grp', 'ctx'), self.pairs(go))  9.69 us
    pallas_call x1, Pallas kernels, local(): pl.pallas_call(functools.partial(expert_kernel, plan, entries), out_shape...  9.48 us
  transfers between devices with their start and end apart: 36, of which 11 were waited for; matrix products, arithmetic and copies ran while one was open for 0% of the time, Pallas kernels for 24%

profile of v2, /device:TPU:0, one launch (start us, length us, event | category | flops | bytes accessed | tf_op | source)
XLA Modules:
  0.0 164.9 jit_solution(3506761073298066811)
XLA Ops:
  5.0 2.1 %states.3 = bf16[2,512,128]{2,1,0:T(8,128)(2,1)} custom-call(s32[4]{0:T(128)S(1)} %pad_add_fusion.pos_ref, bf16[512,1024]{1,0:T(8,128)(2,1)S(1)} %bitcast.28, bf16[512,1024]{1,0:T(8,128)(2,1)S(1)} %bitcast.13, bf16[512,1024]{1,0:T(8,128)(2,1)S(1)} %bitcast.18, bf16[512,1024]{1,0:T(8,128)(2,1)S(1)} %bitcast.23), custom_call_target="tpu_custom_call" | custom-call | flops 1 | bytes 1 | tf_op jit(solution)/shard_map/states/pallas_call | solution.py:486
  7.1 3.0 %collective-permute-start = (bf16[2,512,128]{2,1,0:T(8,128)(2,1)}, bf16[2,512,128]{2,1,0:T(8,128)(2,1)S(1)}, u32[]{:S(2)}, u32[]{:S(2)}) collective-permute-start(bf16[2,512,128]{2,1,0:T(8,128)(2,1)} %states.3), channel_id=1, source_target_pairs={{0,1},{1,0},{2,3},{3,2},{4,5},{5,4},{6,7},{7,6},{8,9},{9,8},{10,11... | collective-permute-start | bytes 786440 | tf_op jit(solution)/shard_map/ppermute | solution.py:495
  15.7 2.5 %input_rows.1 = (bf16[64,2176]{1,0:T(8,128)(2,1)S(1)}, bf16[64,512]{1,0:T(8,128)(2,1)S(1)}) custom-call(s32[1,1,32,2]{3,2,1,0:T(8,128)S(1)} %copy.13.chosen_ref, s32[1,1,32]{2,1,0:T(1,128)S(1)} %copy-done.32, f32[1,1,32,2]{3,2,1,0:T(8,128)S(1)} %copy.14.combine_ref, bf16[512,2048]{1,0:T(8,128)(2,1)S(1)} %bitcast.32), custom_call_target="tpu_custom_call" | custom-call | flops 1 | bytes 1 | tf_op jit(solution)/shard_map/input_rows/pallas_call | solution.py:499
  23.1 4.3 %near.2.refs_2_ = bf16[3,512,512]{2,1,0:T(8,128)(2,1)S(1)} custom-call(s32[4]{0:T(128)S(1)} %pad_add_fusion.pos_ref, bf16[512,1024]{1,0:T(8,128)(2,1)S(1)} %bitcast.30, bf16[512,1024]{1,0:T(8,128)(2,1)S(1)} %bitcast.15, bf16[512,1024]{1,0:T(8,128)(2,1)S(1)} %bitcast.20, bf16[512,1024]{1,0:T(8,128)(2,1)S(1)} %bitcast.25), custom_call_target="tpu_custom_call" | custom-call | flops 1 | bytes 1 | tf_op jit(solution)/shard_map/near/pallas_call | solution.py:533
  32.0 2.1 %collective-permute-start.4 = (bf16[512,128]{1,0:T(8,128)(2,1)S(1)}, bf16[512,128]{1,0:T(8,128)(2,1)S(1)}, u32[]{:S(2)}, u32[]{:S(2)}) collective-permute-start(bf16[512,128]{1,0:T(8,128)(2,1)S(1)} %get-tuple-element.74), channel_id=1, source_target_pairs={{0,6},{1,7},{2,0},{3,1},{4,2},{5,3},{6,4},{7,5},{8,14},{9,15},{10,... | collective-permute-start | bytes 393224 | tf_op jit(solution)/shard_map/ppermute | solution.py:523
  34.0 4.3 %near.3.refs_3_ = bf16[3,512,512]{2,1,0:T(8,128)(2,1)S(1)} custom-call(s32[4]{0:T(128)S(1)} %pad_add_fusion.pos_ref, bf16[512,1024]{1,0:T(8,128)(2,1)S(1)} %bitcast.31, bf16[512,1024]{1,0:T(8,128)(2,1)S(1)} %bitcast.16, bf16[512,1024]{1,0:T(8,128)(2,1)S(1)} %bitcast.21, bf16[512,1024]{1,0:T(8,128)(2,1)S(1)} %bitcast.26), custom_call_target="tpu_custom_call" | custom-call | flops 1 | bytes 1 | tf_op jit(solution)/shard_map/near/pallas_call | solution.py:533
  38.4 10.6 %collective-permute-done.3.refs_3_ = bf16[512,128]{1,0:T(8,128)(2,1)S(1)} collective-permute-done((bf16[512,128]{1,0:T(8,128)(2,1)S(1)}, bf16[512,128]{1,0:T(8,128)(2,1)S(1)}, u32[]{:S(2)}, u32[]{:S(2)}) %collective-permute-start.3) | collective-permute-done | bytes 131104 | tf_op jit(solution)/shard_map/ppermute | solution.py:523
  52.0 1.8 %collective-permute-start.11 = (bf16[768,256]{1,0:T(8,128)(2,1)S(1)}, bf16[768,256]{1,0:T(8,128)(2,1)S(1)}, u32[]{:S(2)}, u32[]{:S(2)}) collective-permute-start(bf16[768,256]{1,0:T(8,128)(2,1)S(1)} %collective-permute-done.7.refs_3_.refs_5_.refs_17_.refs_19_), channel_id=1, source_target_pairs={{0,2},{1,3},{2,4},{3,5},{4,6},{5,7},{6,0},{7,1},{8,10},{9,11},{10,... | collective-permute-start | bytes 1179656 | tf_op jit(solution)/shard_map/ppermute | solution.py:583
  56.8 6.9 %collective-permute-done.9.refs_1_ = bf16[2,512,128]{2,1,0:T(8,128)(2,1)S(1)} collective-permute-done((bf16[2,512,128]{2,1,0:T(8,128)(2,1)S(1)}, bf16[2,512,128]{2,1,0:T(8,128)(2,1)S(1)}, u32[]{:S(2)}, u32[]{:S(2)}) %collective-permute-start.9) | collective-permute-done | bytes 262176 | tf_op jit(solution)/shard_map/ppermute | solution.py:572
  65.3 2.9 %far.1 = (bf16[512,3072]{1,0:T(8,128)(2,1)S(1)}, bf16[64,3072]{1,0:T(8,128)(2,1)S(1)}) custom-call(s32[4]{0:T(128)S(1)} %pad_add_fusion.pos_ref, bf16[64,512]{1,0:T(8,128)(2,1)S(1)} %get-tuple-element.63.picks_ref, bf16[512,1024]{1,0:T(8,128)(2,1)S(1)} %bitcast.17, bf16[512,1024]{1,0:T(8,128)(2,1)S(1)} %bitcast.22, bf16[512,1024]{1,0:T(8,128)(2,1)S(1)} %bitcast.27, ...), custom_call_target="tpu_custom_call" | custom-call | flops 1 | bytes 1 | tf_op jit(solution)/shard_map/far/pallas_call | solution.py:596
  73.1 1.9 %all_to_all.22 = bf16[32,2,3072]{2,1,0:T(2,128)(2,1)} reshape(bf16[64,3072]{1,0:T(8,128)(2,1)} %copy-done.25) | data formatting | bytes 786432 | tf_op jit(solution)/shard_map/all_to_all | solution.py:558
  75.0 4.2 %all-to-all-start = ((bf16[32,2,3072]{2,1,0:T(2,128)(2,1)}), bf16[32,2,3072]{2,1,0:T(2,128)(2,1)}, u32[]{:S(2)}, u32[]{:S(2)}) async-start(bf16[32,2,3072]{2,1,0:T(2,128)(2,1)} %all_to_all.22), calls=%async_computation | async-start | bytes 786432 | tf_op jit(solution)/shard_map/all_to_all | solution.py:558
  84.5 8.3 %all-to-all-done = bf16[32,2,3072]{2,1,0:T(2,128)(2,1)} async-done(((bf16[32,2,3072]{2,1,0:T(2,128)(2,1)}), bf16[32,2,3072]{2,1,0:T(2,128)(2,1)}, u32[]{:S(2)}, u32[]{:S(2)}) %all-to-all-start) | async-done | bytes 393248 | tf_op jit(solution)/shard_map/all_to_all | solution.py:558
  92.8 1.9 %all_to_all.24.rows_ref = bf16[64,3072]{1,0:T(8,128)(2,1)} reshape(bf16[32,2,3072]{2,1,0:T(2,128)(2,1)} %all-to-all-done) | data formatting | bytes 786432 | tf_op jit(solution)/shard_map/all_to_all | solution.py:558
  95.6 5.8 %collective-permute-done.15.refs_23_.refs_29_.refs_41_.refs_47_ = bf16[768,256]{1,0:T(8,128)(2,1)} collective-permute-done((bf16[768,256]{1,0:T(8,128)(2,1)}, bf16[768,256]{1,0:T(8,128)(2,1)}, u32[]{:S(2)}, u32[]{:S(2)}) %collective-permute-start.15) | collective-permute-done | bytes 393248 | tf_op jit(solution)/shard_map/ppermute | solution.py:83
  104.0 3.0 %collective-permute-start.19 = (bf16[768,256]{1,0:T(8,128)(2,1)S(1)}, bf16[768,256]{1,0:T(8,128)(2,1)S(1)}, u32[]{:S(2)}, u32[]{:S(2)}) collective-permute-start(bf16[768,256]{1,0:T(8,128)(2,1)S(1)} %collective-permute-done.8.refs_5_.refs_11_), channel_id=1, source_target_pairs={{0,8},{1,9},{2,10},{3,11},{4,12},{5,13},{6,14},{7,15},{8,0},{9,1},... | collective-permute-start | bytes 1179656 | tf_op jit(solution)/shard_map/ppermute | solution.py:83
  112.1 3.9 %all-to-all-start.1 = ((bf16[32,2,2176]{2,1,0:T(2,128)(2,1)}), bf16[32,2,2176]{2,1,0:T(2,128)(2,1)}, u32[]{:S(2)}, u32[]{:S(2)}) async-start(bf16[32,2,2176]{2,1,0:T(2,128)(2,1)} %all_to_all.25), calls=%async_computation.1 | async-start | bytes 557056 | tf_op jit(solution)/shard_map/all_to_all | solution.py:558
  119.2 5.5 %reach.1.back_ref = f32[768,64]{1,0:T(8,128)S(1)} custom-call(s32[4]{0:T(128)S(1)} %copy-done.31, bf16[64,3072]{1,0:T(8,128)(2,1)S(1)} %copy-done.19, bf16[768,2048]{1,0:T(8,128)(2,1)} %bitcast.33, bf16[3072,256]{1,0:T(8,128)(2,1)} %copy-done.11, bf16[768,256]{1,0:T(8,128)(2,1)S(1)} %collective-permute-done.1.refs_1_.refs_3_, ...), custom_call_target="tpu_custom_call" | custom-call | flops 1 | bytes 1 | tf_op jit(solution)/shard_map/reach/pallas_call | solution.py:657
  125.3 1.8 %all-to-all-done.1 = bf16[32,2,2176]{2,1,0:T(2,128)(2,1)} async-done(((bf16[32,2,2176]{2,1,0:T(2,128)(2,1)}), bf16[32,2,2176]{2,1,0:T(2,128)(2,1)}, u32[]{:S(2)}, u32[]{:S(2)}) %all-to-all-start.1) | async-done | bytes 278560 | tf_op jit(solution)/shard_map/all_to_all | solution.py:558
  129.2 9.5 %expert.1 = bf16[64,2048]{1,0:T(8,128)(2,1)S(1)} custom-call(s32[4]{0:T(128)S(1)} %copy-done.31, bf16[64,3072]{1,0:T(8,128)(2,1)S(1)} %copy-done.19, bf16[64,2176]{1,0:T(8,128)(2,1)S(1)} %all_to_all.27.packed_ref, f32[768,64]{1,0:T(8,128)S(1)} %reach.1.back_ref, bf16[2048,768]{1,0:T(8,128)(2,1)} %bitcast.35, bf16[2048,768]{1,0:T(8,128)(2,1)} %bitcast.36, ...), custom_call_target="tpu_custom_call" | custom-call | flops 1 | bytes 1 | tf_op jit(solution)/shard_map/expert/pallas_call | solution.py:679
  139.4 1.8 %all_to_all.28 = bf16[32,2,2048]{2,1,0:T(2,128)(2,1)} reshape(bf16[64,2048]{1,0:T(8,128)(2,1)} %copy-done.22) | data formatting | bytes 524288 | tf_op jit(solution)/shard_map/all_to_all | solution.py:558
  141.2 5.2 %all-to-all-start.2 = ((bf16[32,2,2048]{2,1,0:T(2,128)(2,1)}), bf16[32,2,2048]{2,1,0:T(2,128)(2,1)S(1)}, u32[]{:S(2)}, u32[]{:S(2)}) async-start(bf16[32,2,2048]{2,1,0:T(2,128)(2,1)} %all_to_all.28), calls=%async_computation.2 | async-start | bytes 524288 | tf_op jit(solution)/shard_map/all_to_all | solution.py:558
  146.4 14.1 %project.1.token_ref = bf16[512,2048]{1,0:T(8,128)(2,1)} custom-call(s32[4]{0:T(128)S(1)} %copy-done.31, bf16[512,3072]{1,0:T(8,128)(2,1)} %copy-done.20, bf16[3072,256]{1,0:T(8,128)(2,1)} %copy-done.11, bf16[768,256]{1,0:T(8,128)(2,1)S(1)} %collective-permute-done.1.refs_1_.refs_3_, bf16[768,256]{1,0:T(8,128)(2,1)S(1)} %collective-permute-done.5.refs_2_.refs_4_, ...), custom_call_target="tpu_custom_call" | custom-call | flops 1 | bytes 1 | tf_op jit(solution)/shard_map/project/pallas_call | solution.py:697
  162.2 2.7 %join.1 = bf16[512,2048]{1,0:T(8,128)(2,1)} custom-call(bf16[64,512]{1,0:T(8,128)(2,1)S(1)} %copy-done.29, bf16[64,2048]{1,0:T(8,128)(2,1)S(1)} %all_to_all.30.returned_ref, bf16[512,2048]{1,0:T(8,128)(2,1)S(1)} %copy-done.12), custom_call_target="tpu_custom_call" | custom-call | flops 1 | bytes 1 | tf_op jit(solution)/shard_map/join/pallas_call | solution.py:708
  (154 shorter events, 54.3 us)
Async XLA Ops:
  7.1 11.2 %collective-permute-start = (bf16[2,512,128]{2,1,0:T(8,128)(2,1)}, bf16[2,512,128]{2,1,0:T(8,128)(2,1)S(1)}, u32[]{:S(2)}, u32[]{:S(2)}) collective-permute-start(bf16[2,512,128]{2,1,0:T(8,128)(2,1)} %states.3), channel_id=1, source_target_pairs={{0,1},{1,0},{2,3},{3,2},{4,5},{5,4},{6,7},{7,6},{8,9},{9,8},{10,11... | collective-permute-start | bytes 786440 | tf_op jit(solution)/shard_map/ppermute | solution.py:495
  10.8 17.9 %collective-permute-start.1 = (bf16[768,256]{1,0:T(8,128)(2,1)S(1)}, bf16[768,256]{1,0:T(8,128)(2,1)S(1)}, u32[]{:S(2)}, u32[]{:S(2)}) collective-permute-start(bf16[768,256]{1,0:T(8,128)(2,1)S(1)} %turned.3), channel_id=1, source_target_pairs={{0,2},{1,3},{2,4},{3,5},{4,6},{5,7},{6,0},{7,1},{8,10},{9,11},{10,... | collective-permute-start | bytes 1179656 | tf_op jit(solution)/shard_map/ppermute | solution.py:498
  20.0 29.8 %collective-permute-start.6 = (bf16[1536,256]{1,0:T(8,128)(2,1)S(1)}, bf16[1536,256]{1,0:T(8,128)(2,1)}, u32[]{:S(2)}, u32[]{:S(2)}) collective-permute-start(bf16[1536,256]{1,0:T(8,128)(2,1)S(1)} %turned.4), channel_id=1, source_target_pairs={{8,9},{9,8},{10,11},{11,10},{12,13},{13,12},{14,15},{15,14},{24,25... | collective-permute-start | bytes 2359304 | tf_op jit(solution)/shard_map/ppermute | solution.py:83
  28.6 22.0 %collective-permute-start.8 = (bf16[768,256]{1,0:T(8,128)(2,1)S(1)}, bf16[768,256]{1,0:T(8,128)(2,1)S(1)}, u32[]{:S(2)}, u32[]{:S(2)}) collective-permute-start(bf16[768,256]{1,0:T(8,128)(2,1)S(1)} %collective-permute-done.1.refs_1_.refs_3_), channel_id=1, source_target_pairs={{0,16},{1,17},{2,18},{3,19},{4,20},{5,21},{6,22},{7,23},{8,9},{9,8... | collective-permute-start | bytes 1179656 | tf_op jit(solution)/shard_map/ppermute | solution.py:83
  30.2 20.5 %collective-permute-start.7 = (bf16[768,256]{1,0:T(8,128)(2,1)S(1)}, bf16[768,256]{1,0:T(8,128)(2,1)S(1)}, u32[]{:S(2)}, u32[]{:S(2)}) collective-permute-start(bf16[768,256]{1,0:T(8,128)(2,1)S(1)} %collective-permute-done.1.refs_1_.refs_3_), channel_id=1, source_target_pairs={{0,2},{1,3},{2,4},{3,5},{4,6},{5,7},{6,0},{7,1},{8,10},{9,11},{10,... | collective-permute-start | bytes 1179656 | tf_op jit(solution)/shard_map/ppermute | solution.py:551
  30.7 18.3 %collective-permute-start.3 = (bf16[512,128]{1,0:T(8,128)(2,1)S(1)}, bf16[512,128]{1,0:T(8,128)(2,1)S(1)}, u32[]{:S(2)}, u32[]{:S(2)}) collective-permute-start(bf16[512,128]{1,0:T(8,128)(2,1)S(1)} %get-tuple-element.73), channel_id=1, source_target_pairs={{0,4},{1,5},{2,6},{3,7},{4,0},{5,1},{6,2},{7,3},{8,12},{9,13},{10,... | collective-permute-start | bytes 393224 | tf_op jit(solution)/shard_map/ppermute | solution.py:523
  32.0 17.8 %collective-permute-start.4 = (bf16[512,128]{1,0:T(8,128)(2,1)S(1)}, bf16[512,128]{1,0:T(8,128)(2,1)S(1)}, u32[]{:S(2)}, u32[]{:S(2)}) collective-permute-start(bf16[512,128]{1,0:T(8,128)(2,1)S(1)} %get-tuple-element.74), channel_id=1, source_target_pairs={{0,6},{1,7},{2,0},{3,1},{4,2},{5,3},{6,4},{7,5},{8,14},{9,15},{10,... | collective-permute-start | bytes 393224 | tf_op jit(solution)/shard_map/ppermute | solution.py:523
  50.7 13.0 %collective-permute-start.13 = (bf16[768,256]{1,0:T(8,128)(2,1)S(1)}, bf16[768,256]{1,0:T(8,128)(2,1)}, u32[]{:S(2)}, u32[]{:S(2)}) collective-permute-start(bf16[768,256]{1,0:T(8,128)(2,1)S(1)} %collective-permute-done.7.refs_3_.refs_5_.refs_17_.refs_19_), channel_id=1, source_target_pairs={{0,16},{1,17},{2,18},{3,19},{4,20},{5,21},{6,22},{7,23},{8,9},{9,8... | collective-permute-start | bytes 1179656 | tf_op jit(solution)/shard_map/ppermute | solution.py:83
  52.0 11.7 %collective-permute-start.12 = (bf16[768,256]{1,0:T(8,128)(2,1)S(1)}, bf16[768,256]{1,0:T(8,128)(2,1)}, u32[]{:S(2)}, u32[]{:S(2)}) collective-permute-start(bf16[768,256]{1,0:T(8,128)(2,1)S(1)} %collective-permute-done.7.refs_3_.refs_5_.refs_17_.refs_19_), channel_id=1, source_target_pairs={{0,8},{1,9},{2,10},{3,11},{4,12},{5,13},{6,14},{7,15},{8,0},{9,1},... | collective-permute-start | bytes 1179656 | tf_op jit(solution)/shard_map/ppermute | solution.py:83
  52.0 13.3 %collective-permute-start.11 = (bf16[768,256]{1,0:T(8,128)(2,1)S(1)}, bf16[768,256]{1,0:T(8,128)(2,1)S(1)}, u32[]{:S(2)}, u32[]{:S(2)}) collective-permute-start(bf16[768,256]{1,0:T(8,128)(2,1)S(1)} %collective-permute-done.7.refs_3_.refs_5_.refs_17_.refs_19_), channel_id=1, source_target_pairs={{0,2},{1,3},{2,4},{3,5},{4,6},{5,7},{6,0},{7,1},{8,10},{9,11},{10,... | collective-permute-start | bytes 1179656 | tf_op jit(solution)/shard_map/ppermute | solution.py:583
  70.7 30.7 %collective-permute-start.18 = (bf16[1536,256]{1,0:T(8,128)(2,1)}, bf16[1536,256]{1,0:T(8,128)(2,1)}, u32[]{:S(2)}, u32[]{:S(2)}) collective-permute-start(bf16[1536,256]{1,0:T(8,128)(2,1)} %collective-permute-done.6.refs_17_.refs_33_), channel_id=1, source_target_pairs={{8,24},{9,25},{10,26},{11,27},{12,28},{13,29},{14,30},{15,31},{24,... | collective-permute-start | bytes 2359304 | tf_op jit(solution)/shard_map/ppermute | solution.py:83
  75.0 17.8 %all-to-all-start = ((bf16[32,2,3072]{2,1,0:T(2,128)(2,1)}), bf16[32,2,3072]{2,1,0:T(2,128)(2,1)}, u32[]{:S(2)}, u32[]{:S(2)}) async-start(bf16[32,2,3072]{2,1,0:T(2,128)(2,1)} %all_to_all.22), calls=%async_computation | async-start | bytes 786432 | tf_op jit(solution)/shard_map/all_to_all | solution.py:558
  79.2 15.4 %collective-permute-start.16 = (bf16[768,256]{1,0:T(8,128)(2,1)S(1)}, bf16[768,256]{1,0:T(8,128)(2,1)}, u32[]{:S(2)}, u32[]{:S(2)}) collective-permute-start(bf16[768,256]{1,0:T(8,128)(2,1)S(1)} %collective-permute-done.10.refs_7_.refs_9_), channel_id=1, source_target_pairs={{0,1},{1,0},{2,3},{3,2},{4,5},{5,4},{6,7},{7,6},{8,24},{9,25},{10,... | collective-permute-start | bytes 1179656 | tf_op jit(solution)/shard_map/ppermute | solution.py:83
  81.0 14.6 %collective-permute-start.17 = (bf16[768,256]{1,0:T(8,128)(2,1)}, bf16[768,256]{1,0:T(8,128)(2,1)}, u32[]{:S(2)}, u32[]{:S(2)}) collective-permute-start(bf16[768,256]{1,0:T(8,128)(2,1)} %collective-permute-done.12.refs_4_.refs_6_.refs_18_.refs_20_), channel_id=1, source_target_pairs={{0,16},{1,17},{2,18},{3,19},{4,20},{5,21},{6,22},{7,23},{8,9},{9,8... | collective-permute-start | bytes 1179656 | tf_op jit(solution)/shard_map/ppermute | solution.py:83
  82.5 18.9 %collective-permute-start.15 = (bf16[768,256]{1,0:T(8,128)(2,1)}, bf16[768,256]{1,0:T(8,128)(2,1)}, u32[]{:S(2)}, u32[]{:S(2)}) collective-permute-start(bf16[768,256]{1,0:T(8,128)(2,1)} %copy-done.33), channel_id=1, source_target_pairs={{0,16},{1,17},{2,18},{3,19},{4,20},{5,21},{6,22},{7,23},{8,9},{9,8... | collective-permute-start | bytes 1179656 | tf_op jit(solution)/shard_map/ppermute | solution.py:83
  83.0 23.9 %collective-permute-start.24 = (bf16[768,256]{1,0:T(8,128)(2,1)}, bf16[768,256]{1,0:T(8,128)(2,1)}, u32[]{:S(2)}, u32[]{:S(2)}) collective-permute-start(bf16[768,256]{1,0:T(8,128)(2,1)} %copy-done.34), channel_id=1, source_target_pairs={{0,16},{1,17},{2,18},{3,19},{4,20},{5,21},{6,22},{7,23},{8,9},{9,8... | collective-permute-start | bytes 1179656 | tf_op jit(solution)/shard_map/ppermute | solution.py:83
  101.4 17.3 %collective-permute-start.22 = (bf16[1536,256]{1,0:T(8,128)(2,1)}, bf16[1536,256]{1,0:T(8,128)(2,1)}, u32[]{:S(2)}, u32[]{:S(2)}) collective-permute-start(bf16[1536,256]{1,0:T(8,128)(2,1)} %collective-permute-done.6.refs_17_.refs_33_), channel_id=1, source_target_pairs={{8,0},{9,1},{10,2},{11,3},{12,4},{13,5},{14,6},{15,7},{24,16},{25,... | collective-permute-start | bytes 2359304 | tf_op jit(solution)/shard_map/ppermute | solution.py:83
  102.7 16.2 %collective-permute-start.23 = (bf16[1536,256]{1,0:T(8,128)(2,1)}, bf16[1536,256]{1,0:T(8,128)(2,1)}, u32[]{:S(2)}, u32[]{:S(2)}) collective-permute-start(bf16[1536,256]{1,0:T(8,128)(2,1)} %collective-permute-done.18.refs_19_.refs_35_), channel_id=1, source_target_pairs={{8,0},{9,1},{10,2},{11,3},{12,4},{13,5},{14,6},{15,7},{24,16},{25,... | collective-permute-start | bytes 2359304 | tf_op jit(solution)/shard_map/ppermute | solution.py:83
  108.3 16.3 %collective-permute-start.25 = (bf16[768,256]{1,0:T(8,128)(2,1)}, bf16[768,256]{1,0:T(8,128)(2,1)}, u32[]{:S(2)}, u32[]{:S(2)}) collective-permute-start(bf16[768,256]{1,0:T(8,128)(2,1)} %collective-permute-done.24.refs_25_.refs_27_.refs_43_.refs_45_), channel_id=1, source_target_pairs={{0,1},{1,0},{2,3},{3,2},{4,5},{5,4},{6,7},{7,6},{8,24},{9,25},{10,... | collective-permute-start | bytes 1179656 | tf_op jit(solution)/shard_map/ppermute | solution.py:83
  109.5 15.4 %collective-permute-start.28 = (bf16[768,256]{1,0:T(8,128)(2,1)}, bf16[768,256]{1,0:T(8,128)(2,1)}, u32[]{:S(2)}, u32[]{:S(2)}) collective-permute-start(bf16[768,256]{1,0:T(8,128)(2,1)} %collective-permute-done.17.refs_9_.refs_11_.refs_23_.refs_25_), channel_id=1, source_target_pairs={{0,1},{1,0},{2,3},{3,2},{4,5},{5,4},{6,7},{7,6},{8,24},{9,25},{10,... | collective-permute-start | bytes 1179656 | tf_op jit(solution)/shard_map/ppermute | solution.py:83
  111.2 14.1 %collective-permute-start.31 = (bf16[768,256]{1,0:T(8,128)(2,1)}, bf16[768,256]{1,0:T(8,128)(2,1)}, u32[]{:S(2)}, u32[]{:S(2)}) collective-permute-start(bf16[768,256]{1,0:T(8,128)(2,1)} %collective-permute-done.24.refs_25_.refs_27_.refs_43_.refs_45_), channel_id=1, source_target_pairs={{0,8},{1,9},{2,10},{3,11},{4,12},{5,13},{6,14},{7,15},{8,0},{9,1},... | collective-permute-start | bytes 1179656 | tf_op jit(solution)/shard_map/ppermute | solution.py:83
  112.1 15.0 %all-to-all-start.1 = ((bf16[32,2,2176]{2,1,0:T(2,128)(2,1)}), bf16[32,2,2176]{2,1,0:T(2,128)(2,1)}, u32[]{:S(2)}, u32[]{:S(2)}) async-start(bf16[32,2,2176]{2,1,0:T(2,128)(2,1)} %all_to_all.25), calls=%async_computation.1 | async-start | bytes 557056 | tf_op jit(solution)/shard_map/all_to_all | solution.py:558
  118.7 9.6 %collective-permute-start.27 = (bf16[768,256]{1,0:T(8,128)(2,1)}, bf16[768,256]{1,0:T(8,128)(2,1)S(1)}, u32[]{:S(2)}, u32[]{:S(2)}) collective-permute-start(bf16[768,256]{1,0:T(8,128)(2,1)} %collective-permute-done.17.refs_9_.refs_11_.refs_23_.refs_25_), channel_id=1, source_target_pairs={{0,8},{1,9},{2,10},{3,11},{4,12},{5,13},{6,14},{7,15},{8,0},{9,1},... | collective-permute-start | bytes 1179656 | tf_op jit(solution)/shard_map/ppermute | solution.py:83
  141.2 19.3 %all-to-all-start.2 = ((bf16[32,2,2048]{2,1,0:T(2,128)(2,1)}), bf16[32,2,2048]{2,1,0:T(2,128)(2,1)S(1)}, u32[]{:S(2)}, u32[]{:S(2)}) async-start(bf16[32,2,2048]{2,1,0:T(2,128)(2,1)} %all_to_all.28), calls=%async_computation.2 | async-start | bytes 524288 | tf_op jit(solution)/shard_map/all_to_all | solution.py:558
  (53 other events, 528.6 us)

commit v3 on v2

--- a/solution.py
+++ b/solution.py
@@ -10,6 +10,7 @@
 
 DH = 128
 MIB = 1024 * 1024
+FOLD = 8
 LARGE = 52
 F32 = jnp.float32
 BF16 = jnp.bfloat16
@@ -86,14 +87,20 @@
         return self.move(array, lambda x, c, z, y: (x, 1 - c, z, y))
 
 
-def state_kernel(inner, turn, pos_ref, q_ref, k_ref, v_ref, g_ref, out_ref):
+def state_kernel(inner, turn, pos_ref, *refs):
+    arrays, out_ref, (q_ref, k_ref, v_ref, g_ref, sems) = refs[:4], refs[4], refs[5:]
     each = out_ref.shape[1]
-    base = lax.rem(pos_ref[3] + turn, inner) * each
-    for h in range(each // DH):
-        lanes = lane_slice(base + h * DH, DH)
-        rows = slice(h * DH, (h + 1) * DH)
-        out_ref[0, rows, :] = dot(v_ref[:, lanes], k_ref[:, lanes], FIRST).astype(BF16)
-        out_ref[1, rows, :] = dot(g_ref[:, lanes], q_ref[:, lanes], FIRST).astype(BF16)
+    lanes = lane_slice(lax.rem(pos_ref[3] + turn, inner) * each, each)
+    q_hbm, k_hbm, v_hbm, g_hbm = (array.at[:, lanes] for array in arrays)
+    loads = start_loads(
+        sems, (v_hbm, v_ref), (k_hbm, k_ref), (g_hbm, g_ref), (q_hbm, q_ref)
+    )
+    for n, (left, right) in enumerate(((v_ref, k_ref), (g_ref, q_ref))):
+        loads[2 * n].wait()
+        loads[2 * n + 1].wait()
+        for h in range(each // DH):
+            head = slice(h * DH, (h + 1) * DH)
+            out_ref[n, head, :] = dot(left[:, head], right[:, head], FIRST).astype(BF16)
 
 
 def total_kernel(inner, outer, pos_ref, *refs):
@@ -168,7 +175,8 @@
     lax.fori_loop(0, out_ref.shape[2] // DH, one_head, 0)
 
 
-def input_rows_kernel(chosen_ref, pad_ref, combine_ref, x_ref, out_ref, picks_ref, ones, tail):
+def input_rows_kernel(chosen_ref, pad_ref, combine_ref, x_ref, out_ref, picks_ref, *scratch):
+    ones, tail, folded = scratch
     rows, width = x_ref.shape
     slots = chosen_ref.shape[3]
     row = lax.broadcasted_iota(jnp.int32, (1, rows), 1)
@@ -185,16 +193,24 @@
         tail[pl.ds(n, 1), :] = both
         return carry
 
-    lax.fori_loop(0, out_ref.shape[0], one_slot, 0)
+    lax.fori_loop(0, ones.shape[0], one_slot, 0)
     picks = ones[...].astype(BF16)
     picks_ref[...] = picks
-    out_ref[:, :width] = dot(picks, x_ref[...], PLAIN).astype(BF16)
-    out_ref[:, width:] = tail[...].astype(BF16)
+    picked = dot(picks, x_ref[...], PLAIN)
+    each = folded.shape[0]
+    for m in range(each * FOLD):
+        part = jnp.zeros_like(tail) if m * DH > width else tail[...]
+        if m * DH < width:
+            part = picked[:, m * DH : (m + 1) * DH]
+        folded[m % each, pl.ds(m // each, ones.shape[0], stride=FOLD), :] = part
+    for at in range(each):
+        out_ref[:, at * DH : (at + 1) * DH] = folded[at].astype(BF16)
 
 
 def far_kernel(plan, cuts, scaling, pos_ref, picks_ref, k_ref, v_ref, g_ref, *refs):
     inner = plan.inner
-    states, near, (qkv_ref, rows_ref) = refs[:inner], refs[inner : inner + cuts], refs[-2:]
+    states, near = refs[:inner], refs[inner : inner + cuts]
+    qkv_ref, rows_ref, folded = refs[-3:]
     picks = picks_ref[...]
     x = lax.div(pos_ref[0], plan.cores)
     depth = qkv_ref.shape[1] // plan.cross
@@ -222,7 +238,10 @@
             start = lax.rem(x + plan.cross - part_at, plan.cross) * depth + inside_at
             qkv_ref[:, lane_slice(start, DH)] = whole
             start = (n * heads + h) * DH
-            rows_ref[:, start : start + DH] = dot(picks, whole, PLAIN).astype(BF16)
+            fold, at = divmod(start // DH, folded.shape[0])
+            folded[at, pl.ds(fold, picks.shape[0], stride=FOLD), :] = dot(picks, whole, PLAIN)
+    for at in range(folded.shape[0]):
+        rows_ref[:, at * DH : (at + 1) * DH] = folded[at].astype(BF16)
 
 
 def turn_kernel(pos_ref, in_ref, out_ref):
@@ -307,12 +326,17 @@
     return [ring, pltpu.SemaphoreType.DMA((len(depths), len(found)))]
 
 
-def reach_blocks(plan, pos_ref, rows_ref, pieces, turned_ref):
+def reach_blocks(plan, pos_ref, rows_ref, pieces, turned_ref, folded):
     x = lax.div(pos_ref[0], plan.cores)
     depth = turned_ref.shape[1] // plan.cross
-    for dx in range(plan.cross):
-        lanes = lane_slice(lax.rem(x + plan.cross - dx, plan.cross) * depth, depth)
-        turned_ref[:, dx * depth : (dx + 1) * depth] = rows_ref[:, lanes]
+    count, each = turned_ref.shape[0], folded.shape[0]
+    for at in range(each):
+        folded[at] = rows_ref[:, at * DH : (at + 1) * DH].astype(F32)
+        for fold in range(FOLD):
+            part, inside = divmod((fold * each + at) * DH, depth)
+            lanes = lane_slice(lax.rem(x + plan.cross - part, plan.cross) * depth + inside, DH)
+            rows = folded[at, pl.ds(fold, count, stride=FOLD), :]
+            turned_ref[:, lanes] = rows.astype(BF16)
     return [
         (lanes, dot(turned_ref[...], block[...], PLAIN).astype(BF16))
         for lanes, block in pieces.blocks()
@@ -327,10 +351,10 @@
 
 
 def reach_kernel(plan, entries, pos_ref, rows_ref, down_hbm, *refs):
-    pieces, (back_ref, turned_ref, down_ref, loaded, ring, sems) = refs[:-6], refs[-6:]
+    pieces, (back_ref, turned_ref, folded, down_ref, loaded, ring, sems) = refs[:-7], refs[-7:]
     pieces = Pieces(plan, entries, pos_ref, pieces, ring, sems)
     (load,) = start_loads(loaded, (down_hbm, down_ref))
-    blocks = reach_blocks(plan, pos_ref, rows_ref, pieces, turned_ref)
+    blocks = reach_blocks(plan, pos_ref, rows_ref, pieces, turned_ref, folded)
     load.wait()
     back_ref[...] = jnp.zeros_like(back_ref)
     for lanes, grads in blocks:
@@ -339,16 +363,25 @@
 
 def expert_kernel(plan, entries, pos_ref, rows_ref, packed_ref, back_ref, *refs):
     hbm, refs = refs[:3], refs[3:]
-    pieces, (out_ref, held, turned_ref) = refs[:-9], refs[-9:-6]
+    pieces, (out_ref, held, turned_ref, folded, result) = refs[:-13], refs[-13:-8]
+    packed, folded_packed = refs[-8:-6]
     (gate_ref, up_ref, down_ref), (loaded, ring, sems) = refs[-6:-3], refs[-3:]
     pieces = Pieces(plan, entries, pos_ref, pieces, ring, sems)
     loads = start_loads(loaded, *zip(hbm, (gate_ref, up_ref, down_ref), strict=True))
-    blocks = reach_blocks(plan, pos_ref, rows_ref, pieces, turned_ref)
-    width = out_ref.shape[1]
+    blocks = reach_blocks(plan, pos_ref, rows_ref, pieces, turned_ref, folded)
+    width = gate_ref.shape[0]
+    each = folded_packed.shape[0]
+    for at in range(each):
+        folded_packed[at] = packed_ref[:, at * DH : (at + 1) * DH].astype(F32)
+        for fold in range(FOLD):
+            start = (fold * each + at) * DH
+            if start <= width:
+                part = folded_packed[at, pl.ds(fold, packed.shape[0], stride=FOLD), :]
+                packed[:, start : start + DH] = part.astype(BF16)
     loads[0].wait()
-    gate = dot(packed_ref[:, :width], gate_ref[...], PLAIN)
+    gate = dot(packed[:, :width], gate_ref[...], PLAIN)
     loads[1].wait()
-    up = dot(packed_ref[:, :width], up_ref[...], PLAIN)
+    up = dot(packed[:, :width], up_ref[...], PLAIN)
     sigma = jax.nn.sigmoid(gate)
     active = gate * sigma
     slope = up * (sigma * (1.0 + gate * (1.0 - sigma)))
@@ -356,8 +389,8 @@
     held[...] = back_ref[...]
     for lanes, grads in blocks:
         held[...] += dot(down_ref[:, lanes], grads, LAST)
-    weight = packed_ref[:, width : width + 1].astype(F32)
-    weight = weight + packed_ref[:, width + 1 : width + 2].astype(F32)
+    weight = packed[:, width : width + 1].astype(F32)
+    weight = weight + packed[:, width + 1 : width + 2].astype(F32)
     hidden = weight * held[...].T
     up_grad = (hidden * active).astype(BF16)
     gate_grad = (hidden * slope).astype(BF16)
@@ -365,7 +398,13 @@
     for n in range(steps):
         some = slice(n * width // steps, (n + 1) * width // steps)
         total = dot(gate_ref[some], gate_grad, LAST) + dot(up_ref[some], up_grad, LAST)
-        out_ref[:, some] = total.T.astype(BF16)
+        total = total.T
+        for m in range(width // steps // DH):
+            fold, at = divmod(n * (width // steps // DH) + m, result.shape[0])
+            goal = pl.ds(fold, total.shape[0], stride=FOLD)
+            result[at, goal, :] = total[:, m * DH : (m + 1) * DH]
+    for at in range(result.shape[0]):
+        out_ref[:, at * DH : (at + 1) * DH] = result[at].astype(BF16)
 
 
 def project_kernel(plan, entries, pos_ref, qkv_hbm, *refs):
@@ -386,8 +425,21 @@
             out_ref[rows, lanes] = total.astype(BF16)
 
 
-def join_kernel(picks_ref, returned_ref, token_ref, out_ref):
-    added = dot(picks_ref[...], returned_ref[...], FIRST)
+def join_kernel(picks_ref, returned_ref, token_ref, out_ref, folded, unfolded):
+    count, each = picks_ref.shape[0], folded.shape[0]
+
+    @pl.when(pl.program_id(0) == 0)
+    def _():
+        for at in range(each):
+            folded[at] = returned_ref[:, at * DH : (at + 1) * DH].astype(F32)
+            for fold in range(FOLD):
+                start = (fold * each + at) * DH
+                part = folded[at, pl.ds(fold, count, stride=FOLD), :]
+                unfolded[:, start : start + DH] = part.astype(BF16)
+
+    size = out_ref.shape[1]
+    lanes = lane_slice(pl.program_id(0) * size, size)
+    added = dot(picks_ref[...], unfolded[:, lanes], FIRST)
     out_ref[...] = (token_ref[...].astype(F32) + added).astype(BF16)
 
 
@@ -486,9 +538,11 @@
         own[i] = pl.pallas_call(
             functools.partial(state_kernel, inner, i),
             out_shape=part,
-            in_specs=[in_smem()] + [in_vmem()] * 4,
+            in_specs=[in_smem()] + [anywhere()] * 4,
             out_specs=in_vmem(),
-            compiler_params=params(),
+            scratch_shapes=[pltpu.VMEM((rows, channels // inner), BF16)] * 4
+            + [pltpu.SemaphoreType.DMA((4,))],
+            compiler_params=params(LARGE),
             cost_estimate=small(),
             name="states",
         )(pos, q, k, v, g)
@@ -496,15 +550,19 @@
     (later, *_) = together(pos, own[-1])
     held = turned(plan, qkv_weight, later, "own")
     held = lax.ppermute(held, "ctx", plan.outer_turn(1))
+    packed_each = pl.cdiv(width + DH, FOLD * DH)
     packed, picks = pl.pallas_call(
         input_rows_kernel,
         out_shape=[
-            jax.ShapeDtypeStruct((items, width + DH), BF16),
+            jax.ShapeDtypeStruct((items * FOLD, packed_each * DH), BF16),
             jax.ShapeDtypeStruct((items, rows), BF16),
         ],
         in_specs=[in_smem()] * 3 + [in_vmem()],
         out_specs=[in_vmem()] * 2,
-        scratch_shapes=[pltpu.VMEM((items, rows), F32), pltpu.VMEM((items, DH), F32)],
+        scratch_shapes=[
+            *(pltpu.VMEM((items, rows), F32), pltpu.VMEM((items, DH), F32)),
+            pltpu.VMEM((packed_each, items * FOLD, DH), F32),
+        ],
         compiler_params=params(),
         cost_estimate=small(),
         name="input_rows",
@@ -557,7 +615,8 @@
     def exchange(array):
         return lax.all_to_all(array, ("grp", "ctx"), split_axis=0, concat_axis=0, tiled=True)
 
-    shares[0], *arrived = together(shares[0], *far, *near, *beside)
+    whole = turned(plan, qkv_weight, after_near, "whole")
+    shares[0], whole, *arrived = together(shares[0], whole, *far, *near, *beside)
     far, near = arrived[: outer - 1], arrived[outer - 1 : outer - 1 + cuts]
     beside = arrived[outer - 1 + cuts :]
     sums = pl.pallas_call(
@@ -593,14 +652,17 @@
         turns[1].first = dict(zip(turns[1].first, arrived, strict=True))
         turns[1].again()
 
+    folded_rows = pltpu.VMEM((3 * channels // FOLD // DH, items * FOLD, DH), F32)
+    folded_result = pltpu.VMEM((width // FOLD // DH, items * FOLD, DH), F32)
     qkv_grad, sent_rows = pl.pallas_call(
         functools.partial(far_kernel, plan, cuts, scaling),
         out_shape=[
             jax.ShapeDtypeStruct((rows, 3 * channels), BF16),
-            jax.ShapeDtypeStruct((items, 3 * channels), BF16),
+            jax.ShapeDtypeStruct((items * FOLD, 3 * channels // FOLD), BF16),
         ],
         in_specs=[in_smem()] + [in_vmem()] * (4 + inner + cuts),
         out_specs=[in_vmem()] * 2,
+        scratch_shapes=[folded_rows],
         compiler_params=params(8),
         cost_estimate=small(),
         name="far",
@@ -632,7 +694,6 @@
     beside, aside = waits[-1 - len(aside)], waits[len(waits) - len(aside) :]
     if outer > 2:
         turns[1].turn_corners()
-    whole = turned(plan, qkv_weight, later, "whole")
     found = [((0, None, 0, 0, None), (whole,))]
     for turn in turns[:-1]:
         found.extend(turn.pieces())
@@ -660,7 +721,7 @@
         in_specs=[in_smem(), in_vmem()] + [anywhere()] * (1 + len(pieces)),
         out_specs=in_vmem(),
         scratch_shapes=[
-            *(turned_rows, down_held, pltpu.SemaphoreType.DMA((1,))),
+            *(turned_rows, folded_rows, down_held, pltpu.SemaphoreType.DMA((1,))),
             *ring_scratch(kept),
         ],
         compiler_params=params(LARGE),
@@ -678,11 +739,13 @@
     kept, entries, pieces = some(lambda turn: turn >= split)
     slot_grad = pl.pallas_call(
         functools.partial(expert_kernel, plan, entries),
-        out_shape=jax.ShapeDtypeStruct((items, width), BF16),
+        out_shape=jax.ShapeDtypeStruct((items * FOLD, width // FOLD), BF16),
         in_specs=[in_smem()] + [in_vmem()] * 3 + [anywhere()] * (3 + len(pieces)),
         out_specs=in_vmem(),
         scratch_shapes=[
-            *(pltpu.VMEM((hidden, items), F32), turned_rows),
+            *(pltpu.VMEM((hidden, items), F32), turned_rows, folded_rows, folded_result),
+            *(pltpu.VMEM((items, width + DH), BF16),),
+            pltpu.VMEM((packed_each, items * FOLD, DH), F32),
             *[pltpu.VMEM((width, hidden), BF16)] * 2,
             *(down_held, pltpu.SemaphoreType.DMA((3,))),
             *ring_scratch(kept),
@@ -711,10 +774,11 @@
         grid=(outer,),
         in_specs=[
             pl.BlockSpec((items, rows), lambda n: (0, 0)),
-            pl.BlockSpec((items, span), lambda n: (0, n)),
+            pl.BlockSpec((items * FOLD, width // FOLD), lambda n: (0, 0)),
             column,
         ],
         out_specs=column,
+        scratch_shapes=[folded_result, pltpu.VMEM((items, width), BF16)],
         compiler_params=params(8),
         cost_estimate=small(),
         name="join",

time: 166 us -> 160 us (0.964)
  local copies, waits for them, and re-layouts: 23.5 us -> 9.67 us
  waiting for transfers between devices: 40.1 us -> 46.9 us
  Pallas kernels: 53.9 us -> 58.1 us
  starting transfers between devices: 46.9 us -> 44.1 us
    ppermute x25, waiting for transfers between devices: 9.69 us -> 27.1 us  [move(): return lax.ppermute(array, ('grp', 'ctx'), self.pairs(go))]
    all_to_all x3, waiting for transfers between devices: 10.1 us -> 2.04 us  [exchange(): lax.all_to_all(array, ('grp', 'ctx'), split_axis=0, concat_axis=0, tiled=...]
    all_to_all x6 -> x0, local copies, waits for them, and re-layouts: 7.6 us -> none  [exchange(): lax.all_to_all(array, ('grp', 'ctx'), split_axis=0, concat_axis=0, tiled=...]
    unnamed x84 -> x66, local copies, waits for them, and re-layouts: 15.9 us -> 9.67 us
    all_to_all x3, starting transfers between devices: 13.3 us -> 10.5 us  [exchange(): lax.all_to_all(array, ('grp', 'ctx'), split_axis=0, concat_axis=0, tiled=...]
    ppermute x3, waiting for transfers between devices: 11.8 us -> 9.3 us  [local(): lax.ppermute(totals[i - 1], 'ctx', plan.outer_turn(i))]
  transfers between devices with their start and end apart: 36 -> 36, of which waited for: 11 -> 12; matrix products, arithmetic and copies ran while one was open for 0% -> 0% of each run, Pallas kernels for 24% -> 27%
where the time goes in v3:
time: 160 us; the launch traced here: 159 us
  Pallas kernels  58.1 us (36%)
  waiting for transfers between devices  46.9 us (29%)
  starting transfers between devices  44.1 us (28%)
  local copies, waits for them, and re-layouts  9.67 us (6%)
    ppermute x25, waiting for transfers between devices, move(): return lax.ppermute(array, ('grp', 'ctx'), self.pairs(go))  27.1 us
    ppermute x25, starting transfers between devices, move(): return lax.ppermute(array, ('grp', 'ctx'), self.pairs(go))  21.1 us
    pallas_call x1, Pallas kernels, local(): pl.pallas_call(functools.partial(project_kernel, plan, entries), out_shap...  14.1 us
    all_to_all x3, starting transfers between devices, exchange(): lax.all_to_all(array, ('grp', 'ctx'), split_axis=0, concat_axis=0, tiled=...  10.5 us
    pallas_call x1, Pallas kernels, local(): pl.pallas_call(functools.partial(expert_kernel, plan, entries), out_shape...  9.71 us
    unnamed x66, local copies, waits for them, and re-layouts  9.67 us
    ppermute x3, waiting for transfers between devices, local(): lax.ppermute(totals[i - 1], 'ctx', plan.outer_turn(i))  9.3 us
    pallas_call x2, Pallas kernels, near_part(): pl.pallas_call(functools.partial(near_kernel, scaling, cut * (heads // cu...  8.7 us
  transfers between devices with their start and end apart: 36, of which 12 were waited for; matrix products, arithmetic and copies ran while one was open for 0% of the time, Pallas kernels for 27%

profile of v3, /device:TPU:0, one launch (start us, length us, event | category | flops | bytes accessed | tf_op | source)
XLA Modules:
  0.0 159.3 jit_solution(2656398738231275431)
XLA Ops:
  1.3 2.5 %states.3 = bf16[2,512,128]{2,1,0:T(8,128)(2,1)S(1)} custom-call(s32[4]{0:T(128)S(1)} %pad_add_fusion.pos_ref, bf16[512,1024]{1,0:T(8,128)(2,1)S(1)} %bitcast.34, bf16[512,1024]{1,0:T(8,128)(2,1)} %bitcast.19, bf16[512,1024]{1,0:T(8,128)(2,1)} %bitcast.24, bf16[512,1024]{1,0:T(8,128)(2,1)} %bitcast.29), custom_call_target="tpu_custom_call" | custom-call | flops 1 | bytes 1 | tf_op jit(solution)/shard_map/states/pallas_call | solution.py:538
  3.8 3.0 %collective-permute-start = (bf16[2,512,128]{2,1,0:T(8,128)(2,1)S(1)}, bf16[2,512,128]{2,1,0:T(8,128)(2,1)S(1)}, u32[]{:S(2)}, u32[]{:S(2)}) collective-permute-start(bf16[2,512,128]{2,1,0:T(8,128)(2,1)S(1)} %states.3), channel_id=1, source_target_pairs={{0,1},{1,0},{2,3},{3,2},{4,5},{5,4},{6,7},{7,6},{8,9},{9,8},{10,11... | collective-permute-start | bytes 786440 | tf_op jit(solution)/shard_map/ppermute | solution.py:549
  9.9 2.5 %states.2.refs_0_ = bf16[2,512,128]{2,1,0:T(8,128)(2,1)S(1)} custom-call(s32[4]{0:T(128)S(1)} %pad_add_fusion.pos_ref, bf16[512,1024]{1,0:T(8,128)(2,1)S(1)} %bitcast.35, bf16[512,1024]{1,0:T(8,128)(2,1)} %bitcast.20, bf16[512,1024]{1,0:T(8,128)(2,1)} %bitcast.25, bf16[512,1024]{1,0:T(8,128)(2,1)} %bitcast.30), custom_call_target="tpu_custom_call" | custom-call | flops 1 | bytes 1 | tf_op jit(solution)/shard_map/states/pallas_call | solution.py:538
  14.2 3.3 %input_rows.1 = (bf16[512,384]{1,0:T(8,128)(2,1)}, bf16[64,512]{1,0:T(8,128)(2,1)S(1)}) custom-call(s32[1,1,32,2]{3,2,1,0:T(8,128)S(1)} %copy.13.chosen_ref, s32[1,1,32]{2,1,0:T(1,128)S(1)} %copy-done.20, f32[1,1,32,2]{3,2,1,0:T(8,128)S(1)} %copy.14.combine_ref, bf16[512,2048]{1,0:T(8,128)(2,1)S(1)} %bitcast.40), custom_call_target="tpu_custom_call" | custom-call | flops 1 | bytes 1 | tf_op jit(solution)/shard_map/input_rows/pallas_call | solution.py:554
  22.3 4.3 %near.2.refs_2_ = bf16[3,512,512]{2,1,0:T(8,128)(2,1)S(1)} custom-call(s32[4]{0:T(128)S(1)} %pad_add_fusion.pos_ref, bf16[512,1024]{1,0:T(8,128)(2,1)S(1)} %bitcast.36, bf16[512,1024]{1,0:T(8,128)(2,1)S(1)} %bitcast.21, bf16[512,1024]{1,0:T(8,128)(2,1)S(1)} %bitcast.26, bf16[512,1024]{1,0:T(8,128)(2,1)S(1)} %bitcast.31), custom_call_target="tpu_custom_call" | custom-call | flops 1 | bytes 1 | tf_op jit(solution)/shard_map/near/pallas_call | solution.py:591
  31.2 2.0 %collective-permute-start.4 = (bf16[512,128]{1,0:T(8,128)(2,1)S(1)}, bf16[512,128]{1,0:T(8,128)(2,1)S(1)}, u32[]{:S(2)}, u32[]{:S(2)}) collective-permute-start(bf16[512,128]{1,0:T(8,128)(2,1)S(1)} %get-tuple-element.76), channel_id=1, source_target_pairs={{0,6},{1,7},{2,0},{3,1},{4,2},{5,3},{6,4},{7,5},{8,14},{9,15},{10,... | collective-permute-start | bytes 393224 | tf_op jit(solution)/shard_map/ppermute | solution.py:581
  33.2 4.4 %near.3.refs_3_ = bf16[3,512,512]{2,1,0:T(8,128)(2,1)S(1)} custom-call(s32[4]{0:T(128)S(1)} %pad_add_fusion.pos_ref, bf16[512,1024]{1,0:T(8,128)(2,1)S(1)} %bitcast.37, bf16[512,1024]{1,0:T(8,128)(2,1)S(1)} %bitcast.22, bf16[512,1024]{1,0:T(8,128)(2,1)S(1)} %bitcast.27, bf16[512,1024]{1,0:T(8,128)(2,1)S(1)} %bitcast.32), custom_call_target="tpu_custom_call" | custom-call | flops 1 | bytes 1 | tf_op jit(solution)/shard_map/near/pallas_call | solution.py:591
  40.1 8.2 %collective-permute-done.3.refs_3_ = bf16[512,128]{1,0:T(8,128)(2,1)S(1)} collective-permute-done((bf16[512,128]{1,0:T(8,128)(2,1)S(1)}, bf16[512,128]{1,0:T(8,128)(2,1)S(1)}, u32[]{:S(2)}, u32[]{:S(2)}) %collective-permute-start.3) | collective-permute-done | bytes 131104 | tf_op jit(solution)/shard_map/ppermute | solution.py:581
  53.8 2.2 %collective-permute-done.10.refs_7_.refs_9_ = bf16[768,256]{1,0:T(8,128)(2,1)S(1)} collective-permute-done((bf16[768,256]{1,0:T(8,128)(2,1)S(1)}, bf16[768,256]{1,0:T(8,128)(2,1)S(1)}, u32[]{:S(2)}, u32[]{:S(2)}) %collective-permute-start.10) | collective-permute-done | bytes 393248 | tf_op jit(solution)/shard_map/ppermute | solution.py:84
  56.0 6.3 %collective-permute-done.9.refs_1_ = bf16[2,512,128]{2,1,0:T(8,128)(2,1)S(1)} collective-permute-done((bf16[2,512,128]{2,1,0:T(8,128)(2,1)S(1)}, bf16[2,512,128]{2,1,0:T(8,128)(2,1)S(1)}, u32[]{:S(2)}, u32[]{:S(2)}) %collective-permute-start.9) | collective-permute-done | bytes 262176 | tf_op jit(solution)/shard_map/ppermute | solution.py:631
  62.3 2.3 %collective-permute-done.11.refs_19_.refs_21_.refs_37_.refs_39_ = bf16[768,256]{1,0:T(8,128)(2,1)S(1)} collective-permute-done((bf16[768,256]{1,0:T(8,128)(2,1)S(1)}, bf16[768,256]{1,0:T(8,128)(2,1)S(1)}, u32[]{:S(2)}, u32[]{:S(2)}) %collective-permute-start.11) | collective-permute-done | bytes 393248 | tf_op jit(solution)/shard_map/ppermute | solution.py:642
  64.6 3.7 %far.1 = (bf16[512,3072]{1,0:T(8,128)(2,1)S(1)}, bf16[512,384]{1,0:T(8,128)(2,1)}) custom-call(s32[4]{0:T(128)S(1)} %pad_add_fusion.pos_ref, bf16[64,512]{1,0:T(8,128)(2,1)S(1)} %get-tuple-element.64.picks_ref, bf16[512,1024]{1,0:T(8,128)(2,1)S(1)} %bitcast.23, bf16[512,1024]{1,0:T(8,128)(2,1)S(1)} %bitcast.28, bf16[512,1024]{1,0:T(8,128)(2,1)S(1)} %bitcast.33, ...), custom_call_target="tpu_custom_call" | custom-call | flops 1 | bytes 1 | tf_op jit(solution)/shard_map/far/pallas_call | solution.py:657
  71.4 4.0 %all-to-all-start = ((bf16[32,16,384]{2,1,0:T(8,128)(2,1)}), bf16[32,16,384]{2,1,0:T(8,128)(2,1)S(1)}, u32[]{:S(2)}, u32[]{:S(2)}) async-start(bf16[32,16,384]{2,1,0:T(8,128)(2,1)} %bitcast.9), calls=%async_computation | async-start | bytes 786432 | tf_op jit(solution)/shard_map/all_to_all | solution.py:616
  80.8 10.0 %collective-permute-done.16.refs_13_.refs_15_ = bf16[768,256]{1,0:T(8,128)(2,1)} collective-permute-done((bf16[768,256]{1,0:T(8,128)(2,1)S(1)}, bf16[768,256]{1,0:T(8,128)(2,1)}, u32[]{:S(2)}, u32[]{:S(2)}) %collective-permute-start.16) | collective-permute-done | bytes 393248 | tf_op jit(solution)/shard_map/ppermute | solution.py:84
  91.6 8.4 %collective-permute-done.15.refs_23_.refs_29_.refs_41_.refs_47_ = bf16[768,256]{1,0:T(8,128)(2,1)S(1)} collective-permute-done((bf16[768,256]{1,0:T(8,128)(2,1)}, bf16[768,256]{1,0:T(8,128)(2,1)S(1)}, u32[]{:S(2)}, u32[]{:S(2)}) %collective-permute-start.15) | collective-permute-done | bytes 393248 | tf_op jit(solution)/shard_map/ppermute | solution.py:84
  103.4 3.4 %collective-permute-start.19 = (bf16[768,256]{1,0:T(8,128)(2,1)S(1)}, bf16[768,256]{1,0:T(8,128)(2,1)S(1)}, u32[]{:S(2)}, u32[]{:S(2)}) collective-permute-start(bf16[768,256]{1,0:T(8,128)(2,1)S(1)} %collective-permute-done.8.refs_5_.refs_11_), channel_id=1, source_target_pairs={{0,8},{1,9},{2,10},{3,11},{4,12},{5,13},{6,14},{7,15},{8,0},{9,1},... | collective-permute-start | bytes 1179656 | tf_op jit(solution)/shard_map/ppermute | solution.py:84
  110.2 3.7 %all-to-all-start.1 = ((bf16[32,16,384]{2,1,0:T(8,128)(2,1)}), bf16[32,16,384]{2,1,0:T(8,128)(2,1)S(1)}, u32[]{:S(2)}, u32[]{:S(2)}) async-start(bf16[32,16,384]{2,1,0:T(8,128)(2,1)} %bitcast.11), calls=%async_computation.1 | async-start | bytes 786432 | tf_op jit(solution)/shard_map/all_to_all | solution.py:616
  114.6 5.5 %reach.1.back_ref = f32[768,64]{1,0:T(8,128)S(1)} custom-call(s32[4]{0:T(128)S(1)} %pad_add_fusion.pos_ref, bf16[512,384]{1,0:T(8,128)(2,1)S(1)} %bitcast.38, bf16[768,2048]{1,0:T(8,128)(2,1)} %bitcast.44, bf16[3072,256]{1,0:T(8,128)(2,1)} %copy-done.6, bf16[768,256]{1,0:T(8,128)(2,1)S(1)} %collective-permute-done.1.refs_1_.refs_3_, ...), custom_call_target="tpu_custom_call" | custom-call | flops 1 | bytes 1 | tf_op jit(solution)/shard_map/reach/pallas_call | solution.py:718
  120.3 3.9 %collective-permute-done.28.refs_15_.refs_17_.refs_29_.refs_31_ = bf16[768,256]{1,0:T(8,128)(2,1)} collective-permute-done((bf16[768,256]{1,0:T(8,128)(2,1)}, bf16[768,256]{1,0:T(8,128)(2,1)}, u32[]{:S(2)}, u32[]{:S(2)}) %collective-permute-start.28) | collective-permute-done | bytes 393248 | tf_op jit(solution)/shard_map/ppermute | solution.py:84
  125.5 2.0 %all-to-all-done.1 = bf16[32,16,384]{2,1,0:T(8,128)(2,1)S(1)} async-done(((bf16[32,16,384]{2,1,0:T(8,128)(2,1)}), bf16[32,16,384]{2,1,0:T(8,128)(2,1)S(1)}, u32[]{:S(2)}, u32[]{:S(2)}) %all-to-all-start.1) | async-done | bytes 393248 | tf_op jit(solution)/shard_map/all_to_all | solution.py:616
  127.6 9.7 %expert.1 = bf16[512,256]{1,0:T(8,128)(2,1)S(1)} custom-call(s32[4]{0:T(128)S(1)} %pad_add_fusion.pos_ref, bf16[512,384]{1,0:T(8,128)(2,1)S(1)} %bitcast.39, bf16[512,384]{1,0:T(8,128)(2,1)S(1)} %bitcast.41, f32[768,64]{1,0:T(8,128)S(1)} %reach.1.back_ref, bf16[2048,768]{1,0:T(8,128)(2,1)} %bitcast.46, bf16[2048,768]{1,0:T(8,128)(2,1)} %bitcast.47, ...), custom_call_target="tpu_custom_call" | custom-call | flops 1 | bytes 1 | tf_op jit(solution)/shard_map/expert/pallas_call | solution.py:740
  138.0 2.7 %all-to-all-start.2 = ((bf16[32,16,256]{2,1,0:T(8,128)(2,1)}), bf16[32,16,256]{2,1,0:T(8,128)(2,1)S(1)}, u32[]{:S(2)}, u32[]{:S(2)}) async-start(bf16[32,16,256]{2,1,0:T(8,128)(2,1)} %bitcast.42), calls=%async_computation.2 | async-start | bytes 524288 | tf_op jit(solution)/shard_map/all_to_all | solution.py:616
  140.7 14.1 %project.1.token_ref = bf16[512,2048]{1,0:T(8,128)(2,1)} custom-call(s32[4]{0:T(128)S(1)} %pad_add_fusion.pos_ref, bf16[512,3072]{1,0:T(8,128)(2,1)} %copy-done.13, bf16[3072,256]{1,0:T(8,128)(2,1)} %copy-done.6, bf16[768,256]{1,0:T(8,128)(2,1)S(1)} %collective-permute-done.1.refs_1_.refs_3_, bf16[768,256]{1,0:T(8,128)(2,1)S(1)} %collective-permute-done.5.refs_2_.refs_4_, ...), custom_call_target="tpu_custom_call" | custom-call | flops 1 | bytes 1 | tf_op jit(solution)/shard_map/project/pallas_call | solution.py:760
  156.5 2.8 %join.1 = bf16[512,2048]{1,0:T(8,128)(2,1)} custom-call(bf16[64,512]{1,0:T(8,128)(2,1)S(1)} %copy-done.19, bf16[512,256]{1,0:T(8,128)(2,1)S(1)} %bitcast.43, bf16[512,2048]{1,0:T(8,128)(2,1)S(1)} %copy-done.7), custom_call_target="tpu_custom_call" | custom-call | flops 1 | bytes 1 | tf_op jit(solution)/shard_map/join/pallas_call | solution.py:771
  (130 shorter events, 43.9 us)
Async XLA Ops:
  3.8 13.7 %collective-permute-start = (bf16[2,512,128]{2,1,0:T(8,128)(2,1)S(1)}, bf16[2,512,128]{2,1,0:T(8,128)(2,1)S(1)}, u32[]{:S(2)}, u32[]{:S(2)}) collective-permute-start(bf16[2,512,128]{2,1,0:T(8,128)(2,1)S(1)} %states.3), channel_id=1, source_target_pairs={{0,1},{1,0},{2,3},{3,2},{4,5},{5,4},{6,7},{7,6},{8,9},{9,8},{10,11... | collective-permute-start | bytes 786440 | tf_op jit(solution)/shard_map/ppermute | solution.py:549
  8.3 19.5 %collective-permute-start.1 = (bf16[768,256]{1,0:T(8,128)(2,1)}, bf16[768,256]{1,0:T(8,128)(2,1)S(1)}, u32[]{:S(2)}, u32[]{:S(2)}) collective-permute-start(bf16[768,256]{1,0:T(8,128)(2,1)} %turned.3), channel_id=1, source_target_pairs={{0,2},{1,3},{2,4},{3,5},{4,6},{5,7},{6,0},{7,1},{8,10},{9,11},{10,... | collective-permute-start | bytes 1179656 | tf_op jit(solution)/shard_map/ppermute | solution.py:552
  19.2 29.8 %collective-permute-start.6 = (bf16[1536,256]{1,0:T(8,128)(2,1)S(1)}, bf16[1536,256]{1,0:T(8,128)(2,1)}, u32[]{:S(2)}, u32[]{:S(2)}) collective-permute-start(bf16[1536,256]{1,0:T(8,128)(2,1)S(1)} %turned.5), channel_id=1, source_target_pairs={{8,9},{9,8},{10,11},{11,10},{12,13},{13,12},{14,15},{15,14},{24,25... | collective-permute-start | bytes 2359304 | tf_op jit(solution)/shard_map/ppermute | solution.py:84
  27.9 22.0 %collective-permute-start.8 = (bf16[768,256]{1,0:T(8,128)(2,1)S(1)}, bf16[768,256]{1,0:T(8,128)(2,1)S(1)}, u32[]{:S(2)}, u32[]{:S(2)}) collective-permute-start(bf16[768,256]{1,0:T(8,128)(2,1)S(1)} %collective-permute-done.1.refs_1_.refs_3_), channel_id=1, source_target_pairs={{0,16},{1,17},{2,18},{3,19},{4,20},{5,21},{6,22},{7,23},{8,9},{9,8... | collective-permute-start | bytes 1179656 | tf_op jit(solution)/shard_map/ppermute | solution.py:84
  29.3 20.5 %collective-permute-start.7 = (bf16[768,256]{1,0:T(8,128)(2,1)S(1)}, bf16[768,256]{1,0:T(8,128)(2,1)S(1)}, u32[]{:S(2)}, u32[]{:S(2)}) collective-permute-start(bf16[768,256]{1,0:T(8,128)(2,1)S(1)} %collective-permute-done.1.refs_1_.refs_3_), channel_id=1, source_target_pairs={{0,2},{1,3},{2,4},{3,5},{4,6},{5,7},{6,0},{7,1},{8,10},{9,11},{10,... | collective-permute-start | bytes 1179656 | tf_op jit(solution)/shard_map/ppermute | solution.py:609
  29.9 18.3 %collective-permute-start.3 = (bf16[512,128]{1,0:T(8,128)(2,1)S(1)}, bf16[512,128]{1,0:T(8,128)(2,1)S(1)}, u32[]{:S(2)}, u32[]{:S(2)}) collective-permute-start(bf16[512,128]{1,0:T(8,128)(2,1)S(1)} %get-tuple-element.75), channel_id=1, source_target_pairs={{0,4},{1,5},{2,6},{3,7},{4,0},{5,1},{6,2},{7,3},{8,12},{9,13},{10,... | collective-permute-start | bytes 393224 | tf_op jit(solution)/shard_map/ppermute | solution.py:581
  31.2 17.8 %collective-permute-start.4 = (bf16[512,128]{1,0:T(8,128)(2,1)S(1)}, bf16[512,128]{1,0:T(8,128)(2,1)S(1)}, u32[]{:S(2)}, u32[]{:S(2)}) collective-permute-start(bf16[512,128]{1,0:T(8,128)(2,1)S(1)} %get-tuple-element.76), channel_id=1, source_target_pairs={{0,6},{1,7},{2,0},{3,1},{4,2},{5,3},{6,4},{7,5},{8,14},{9,15},{10,... | collective-permute-start | bytes 393224 | tf_op jit(solution)/shard_map/ppermute | solution.py:581
  49.8 12.4 %collective-permute-start.13 = (bf16[768,256]{1,0:T(8,128)(2,1)S(1)}, bf16[768,256]{1,0:T(8,128)(2,1)S(1)}, u32[]{:S(2)}, u32[]{:S(2)}) collective-permute-start(bf16[768,256]{1,0:T(8,128)(2,1)S(1)} %collective-permute-done.7.refs_3_.refs_5_.refs_17_.refs_19_), channel_id=1, source_target_pairs={{0,16},{1,17},{2,18},{3,19},{4,20},{5,21},{6,22},{7,23},{8,9},{9,8... | collective-permute-start | bytes 1179656 | tf_op jit(solution)/shard_map/ppermute | solution.py:84
  51.2 11.1 %collective-permute-start.12 = (bf16[768,256]{1,0:T(8,128)(2,1)S(1)}, bf16[768,256]{1,0:T(8,128)(2,1)S(1)}, u32[]{:S(2)}, u32[]{:S(2)}) collective-permute-start(bf16[768,256]{1,0:T(8,128)(2,1)S(1)} %collective-permute-done.7.refs_3_.refs_5_.refs_17_.refs_19_), channel_id=1, source_target_pairs={{0,8},{1,9},{2,10},{3,11},{4,12},{5,13},{6,14},{7,15},{8,0},{9,1},... | collective-permute-start | bytes 1179656 | tf_op jit(solution)/shard_map/ppermute | solution.py:84
  51.2 13.3 %collective-permute-start.11 = (bf16[768,256]{1,0:T(8,128)(2,1)S(1)}, bf16[768,256]{1,0:T(8,128)(2,1)S(1)}, u32[]{:S(2)}, u32[]{:S(2)}) collective-permute-start(bf16[768,256]{1,0:T(8,128)(2,1)S(1)} %collective-permute-done.7.refs_3_.refs_5_.refs_17_.refs_19_), channel_id=1, source_target_pairs={{0,2},{1,3},{2,4},{3,5},{4,6},{5,7},{6,0},{7,1},{8,10},{9,11},{10,... | collective-permute-start | bytes 1179656 | tf_op jit(solution)/shard_map/ppermute | solution.py:642
  69.9 30.9 %collective-permute-start.18 = (bf16[1536,256]{1,0:T(8,128)(2,1)}, bf16[1536,256]{1,0:T(8,128)(2,1)}, u32[]{:S(2)}, u32[]{:S(2)}) collective-permute-start(bf16[1536,256]{1,0:T(8,128)(2,1)} %collective-permute-done.6.refs_17_.refs_33_), channel_id=1, source_target_pairs={{8,24},{9,25},{10,26},{11,27},{12,28},{13,29},{14,30},{15,31},{24,... | collective-permute-start | bytes 2359304 | tf_op jit(solution)/shard_map/ppermute | solution.py:84
  71.4 29.4 %all-to-all-start = ((bf16[32,16,384]{2,1,0:T(8,128)(2,1)}), bf16[32,16,384]{2,1,0:T(8,128)(2,1)S(1)}, u32[]{:S(2)}, u32[]{:S(2)}) async-start(bf16[32,16,384]{2,1,0:T(8,128)(2,1)} %bitcast.9), calls=%async_computation | async-start | bytes 786432 | tf_op jit(solution)/shard_map/all_to_all | solution.py:616
  75.4 15.3 %collective-permute-start.16 = (bf16[768,256]{1,0:T(8,128)(2,1)S(1)}, bf16[768,256]{1,0:T(8,128)(2,1)}, u32[]{:S(2)}, u32[]{:S(2)}) collective-permute-start(bf16[768,256]{1,0:T(8,128)(2,1)S(1)} %collective-permute-done.10.refs_7_.refs_9_), channel_id=1, source_target_pairs={{0,1},{1,0},{2,3},{3,2},{4,5},{5,4},{6,7},{7,6},{8,24},{9,25},{10,... | collective-permute-start | bytes 1179656 | tf_op jit(solution)/shard_map/ppermute | solution.py:84
  77.3 14.3 %collective-permute-start.17 = (bf16[768,256]{1,0:T(8,128)(2,1)S(1)}, bf16[768,256]{1,0:T(8,128)(2,1)S(1)}, u32[]{:S(2)}, u32[]{:S(2)}) collective-permute-start(bf16[768,256]{1,0:T(8,128)(2,1)S(1)} %collective-permute-done.12.refs_4_.refs_6_.refs_18_.refs_20_), channel_id=1, source_target_pairs={{0,16},{1,17},{2,18},{3,19},{4,20},{5,21},{6,22},{7,23},{8,9},{9,8... | collective-permute-start | bytes 1179656 | tf_op jit(solution)/shard_map/ppermute | solution.py:84
  78.7 21.3 %collective-permute-start.15 = (bf16[768,256]{1,0:T(8,128)(2,1)}, bf16[768,256]{1,0:T(8,128)(2,1)S(1)}, u32[]{:S(2)}, u32[]{:S(2)}) collective-permute-start(bf16[768,256]{1,0:T(8,128)(2,1)} %copy-done.23), channel_id=1, source_target_pairs={{0,16},{1,17},{2,18},{3,19},{4,20},{5,21},{6,22},{7,23},{8,9},{9,8... | collective-permute-start | bytes 1179656 | tf_op jit(solution)/shard_map/ppermute | solution.py:84
  79.3 27.5 %collective-permute-start.24 = (bf16[768,256]{1,0:T(8,128)(2,1)}, bf16[768,256]{1,0:T(8,128)(2,1)}, u32[]{:S(2)}, u32[]{:S(2)}) collective-permute-start(bf16[768,256]{1,0:T(8,128)(2,1)} %collective-permute-done.14.refs_20_.refs_22_.refs_38_.refs_40_), channel_id=1, source_target_pairs={{0,16},{1,17},{2,18},{3,19},{4,20},{5,21},{6,22},{7,23},{8,9},{9,8... | collective-permute-start | bytes 1179656 | tf_op jit(solution)/shard_map/ppermute | solution.py:84
  100.8 13.2 %collective-permute-start.22 = (bf16[1536,256]{1,0:T(8,128)(2,1)}, bf16[1536,256]{1,0:T(8,128)(2,1)}, u32[]{:S(2)}, u32[]{:S(2)}) collective-permute-start(bf16[1536,256]{1,0:T(8,128)(2,1)} %collective-permute-done.6.refs_17_.refs_33_), channel_id=1, source_target_pairs={{8,0},{9,1},{10,2},{11,3},{12,4},{13,5},{14,6},{15,7},{24,16},{25,... | collective-permute-start | bytes 2359304 | tf_op jit(solution)/shard_map/ppermute | solution.py:84
  102.1 12.2 %collective-permute-start.23 = (bf16[1536,256]{1,0:T(8,128)(2,1)}, bf16[1536,256]{1,0:T(8,128)(2,1)}, u32[]{:S(2)}, u32[]{:S(2)}) collective-permute-start(bf16[1536,256]{1,0:T(8,128)(2,1)} %collective-permute-done.18.refs_19_.refs_35_), channel_id=1, source_target_pairs={{8,0},{9,1},{10,2},{11,3},{12,4},{13,5},{14,6},{15,7},{24,16},{25,... | collective-permute-start | bytes 2359304 | tf_op jit(solution)/shard_map/ppermute | solution.py:84
  108.2 11.9 %collective-permute-start.25 = (bf16[768,256]{1,0:T(8,128)(2,1)}, bf16[768,256]{1,0:T(8,128)(2,1)}, u32[]{:S(2)}, u32[]{:S(2)}) collective-permute-start(bf16[768,256]{1,0:T(8,128)(2,1)} %collective-permute-done.24.refs_25_.refs_27_.refs_43_.refs_45_), channel_id=1, source_target_pairs={{0,1},{1,0},{2,3},{3,2},{4,5},{5,4},{6,7},{7,6},{8,24},{9,25},{10,... | collective-permute-start | bytes 1179656 | tf_op jit(solution)/shard_map/ppermute | solution.py:84
  109.3 14.9 %collective-permute-start.28 = (bf16[768,256]{1,0:T(8,128)(2,1)}, bf16[768,256]{1,0:T(8,128)(2,1)}, u32[]{:S(2)}, u32[]{:S(2)}) collective-permute-start(bf16[768,256]{1,0:T(8,128)(2,1)} %copy-done.24), channel_id=1, source_target_pairs={{0,1},{1,0},{2,3},{3,2},{4,5},{5,4},{6,7},{7,6},{8,24},{9,25},{10,... | collective-permute-start | bytes 1179656 | tf_op jit(solution)/shard_map/ppermute | solution.py:84
  110.2 14.0 %collective-permute-start.31 = (bf16[768,256]{1,0:T(8,128)(2,1)}, bf16[768,256]{1,0:T(8,128)(2,1)}, u32[]{:S(2)}, u32[]{:S(2)}) collective-permute-start(bf16[768,256]{1,0:T(8,128)(2,1)} %collective-permute-done.24.refs_25_.refs_27_.refs_43_.refs_45_), channel_id=1, source_target_pairs={{0,8},{1,9},{2,10},{3,11},{4,12},{5,13},{6,14},{7,15},{8,0},{9,1},... | collective-permute-start | bytes 1179656 | tf_op jit(solution)/shard_map/ppermute | solution.py:84
  110.2 17.3 %all-to-all-start.1 = ((bf16[32,16,384]{2,1,0:T(8,128)(2,1)}), bf16[32,16,384]{2,1,0:T(8,128)(2,1)S(1)}, u32[]{:S(2)}, u32[]{:S(2)}) async-start(bf16[32,16,384]{2,1,0:T(8,128)(2,1)} %bitcast.11), calls=%async_computation.1 | async-start | bytes 786432 | tf_op jit(solution)/shard_map/all_to_all | solution.py:616
  114.0 11.5 %collective-permute-start.27 = (bf16[768,256]{1,0:T(8,128)(2,1)}, bf16[768,256]{1,0:T(8,128)(2,1)}, u32[]{:S(2)}, u32[]{:S(2)}) collective-permute-start(bf16[768,256]{1,0:T(8,128)(2,1)} %copy-done.24), channel_id=1, source_target_pairs={{0,8},{1,9},{2,10},{3,11},{4,12},{5,13},{6,14},{7,15},{8,0},{9,1},... | collective-permute-start | bytes 1179656 | tf_op jit(solution)/shard_map/ppermute | solution.py:84
  138.0 16.9 %all-to-all-start.2 = ((bf16[32,16,256]{2,1,0:T(8,128)(2,1)}), bf16[32,16,256]{2,1,0:T(8,128)(2,1)S(1)}, u32[]{:S(2)}, u32[]{:S(2)}) async-start(bf16[32,16,256]{2,1,0:T(8,128)(2,1)} %bitcast.42), calls=%async_computation.2 | async-start | bytes 524288 | tf_op jit(solution)/shard_map/all_to_all | solution.py:616
  (44 other events, 461.9 us)

commit v4 on v3

--- a/solution.py
+++ b/solution.py
@@ -682,7 +682,7 @@
         turn.again()
     sent_rows, *_ = together(sent_rows, *others)
     grad_rows = exchange(sent_rows)
-    waits = [turn.first for turn in turns] + [turns[0].corners] + [turn.second for turn in turns[:2]]
+    waits = [turn.first for turn in turns[:2]] + [turns[0].corners] + [turn.second for turn in turns[:2]]
     waits.append(dict(enumerate(beside)))
     waits += [dict(enumerate(arrays)) for arrays in aside]
     flat = [array for wait in waits for array in wait.values()]

time: 160 us -> 159 us (level)
  waiting for transfers between devices: 46.9 us -> 38.9 us
  starting transfers between devices: 44.1 us -> 50.9 us
    ppermute x25, waiting for transfers between devices: 27.1 us -> 19.5 us  [move(): return lax.ppermute(array, ('grp', 'ctx'), self.pairs(go))]
    ppermute x25, starting transfers between devices: 21.1 us -> 28.4 us  [move(): return lax.ppermute(array, ('grp', 'ctx'), self.pairs(go))]
    unnamed x66 -> x62, local copies, waits for them, and re-layouts: 9.67 us -> 9.64 us
  transfers between devices with their start and end apart: 36 -> 36, of which waited for: 12 -> 11; matrix products, arithmetic and copies ran while one was open for 0% -> 0% of each run, Pallas kernels for 27% -> 27%
where the time goes in v4:
time: 159 us; the launch traced here: 158 us
  Pallas kernels  58.1 us (37%)
  starting transfers between devices  50.9 us (32%)
  waiting for transfers between devices  38.9 us (24%)
  local copies, waits for them, and re-layouts  9.64 us (6%)
    ppermute x25, starting transfers between devices, move(): return lax.ppermute(array, ('grp', 'ctx'), self.pairs(go))  28.4 us
    ppermute x25, waiting for transfers between devices, move(): return lax.ppermute(array, ('grp', 'ctx'), self.pairs(go))  19.5 us
    pallas_call x1, Pallas kernels, local(): pl.pallas_call(functools.partial(project_kernel, plan, entries), out_shap...  14.1 us
    all_to_all x3, starting transfers between devices, exchange(): lax.all_to_all(array, ('grp', 'ctx'), split_axis=0, concat_axis=0, tiled=...  9.93 us
    pallas_call x1, Pallas kernels, local(): pl.pallas_call(functools.partial(expert_kernel, plan, entries), out_shape...  9.71 us
    unnamed x62, local copies, waits for them, and re-layouts  9.64 us
    ppermute x3, waiting for transfers between devices, local(): lax.ppermute(totals[i - 1], 'ctx', plan.outer_turn(i))  9.32 us
    pallas_call x2, Pallas kernels, near_part(): pl.pallas_call(functools.partial(near_kernel, scaling, cut * (heads // cu...  8.7 us
  transfers between devices with their start and end apart: 36, of which 11 were waited for; matrix products, arithmetic and copies ran while one was open for 0% of the time, Pallas kernels for 27%

profile of v4, /device:TPU:0, one launch (start us, length us, event | category | flops | bytes accessed | tf_op | source)
XLA Modules:
  0.0 158.1 jit_solution(11476087806053301083)
XLA Ops:
  1.3 2.5 %states.3 = bf16[2,512,128]{2,1,0:T(8,128)(2,1)S(1)} custom-call(s32[4]{0:T(128)S(1)} %pad_add_fusion.pos_ref, bf16[512,1024]{1,0:T(8,128)(2,1)S(1)} %bitcast.34, bf16[512,1024]{1,0:T(8,128)(2,1)} %bitcast.19, bf16[512,1024]{1,0:T(8,128)(2,1)} %bitcast.24, bf16[512,1024]{1,0:T(8,128)(2,1)} %bitcast.29), custom_call_target="tpu_custom_call" | custom-call | flops 1 | bytes 1 | tf_op jit(solution)/shard_map/states/pallas_call | solution.py:538
  3.8 3.0 %collective-permute-start = (bf16[2,512,128]{2,1,0:T(8,128)(2,1)S(1)}, bf16[2,512,128]{2,1,0:T(8,128)(2,1)S(1)}, u32[]{:S(2)}, u32[]{:S(2)}) collective-permute-start(bf16[2,512,128]{2,1,0:T(8,128)(2,1)S(1)} %states.3), channel_id=1, source_target_pairs={{0,1},{1,0},{2,3},{3,2},{4,5},{5,4},{6,7},{7,6},{8,9},{9,8},{10,11... | collective-permute-start | bytes 786440 | tf_op jit(solution)/shard_map/ppermute | solution.py:549
  9.9 2.5 %states.2.refs_0_ = bf16[2,512,128]{2,1,0:T(8,128)(2,1)S(1)} custom-call(s32[4]{0:T(128)S(1)} %pad_add_fusion.pos_ref, bf16[512,1024]{1,0:T(8,128)(2,1)S(1)} %bitcast.35, bf16[512,1024]{1,0:T(8,128)(2,1)} %bitcast.20, bf16[512,1024]{1,0:T(8,128)(2,1)} %bitcast.25, bf16[512,1024]{1,0:T(8,128)(2,1)} %bitcast.30), custom_call_target="tpu_custom_call" | custom-call | flops 1 | bytes 1 | tf_op jit(solution)/shard_map/states/pallas_call | solution.py:538
  14.2 3.3 %input_rows.1 = (bf16[512,384]{1,0:T(8,128)(2,1)}, bf16[64,512]{1,0:T(8,128)(2,1)S(1)}) custom-call(s32[1,1,32,2]{3,2,1,0:T(8,128)S(1)} %copy.13.chosen_ref, s32[1,1,32]{2,1,0:T(1,128)S(1)} %copy-done.20, f32[1,1,32,2]{3,2,1,0:T(8,128)S(1)} %copy.14.combine_ref, bf16[512,2048]{1,0:T(8,128)(2,1)S(1)} %bitcast.40), custom_call_target="tpu_custom_call" | custom-call | flops 1 | bytes 1 | tf_op jit(solution)/shard_map/input_rows/pallas_call | solution.py:554
  22.3 4.3 %near.2.refs_2_ = bf16[3,512,512]{2,1,0:T(8,128)(2,1)S(1)} custom-call(s32[4]{0:T(128)S(1)} %pad_add_fusion.pos_ref, bf16[512,1024]{1,0:T(8,128)(2,1)S(1)} %bitcast.36, bf16[512,1024]{1,0:T(8,128)(2,1)S(1)} %bitcast.21, bf16[512,1024]{1,0:T(8,128)(2,1)S(1)} %bitcast.26, bf16[512,1024]{1,0:T(8,128)(2,1)S(1)} %bitcast.31), custom_call_target="tpu_custom_call" | custom-call | flops 1 | bytes 1 | tf_op jit(solution)/shard_map/near/pallas_call | solution.py:591
  31.2 2.0 %collective-permute-start.4 = (bf16[512,128]{1,0:T(8,128)(2,1)S(1)}, bf16[512,128]{1,0:T(8,128)(2,1)S(1)}, u32[]{:S(2)}, u32[]{:S(2)}) collective-permute-start(bf16[512,128]{1,0:T(8,128)(2,1)S(1)} %get-tuple-element.75), channel_id=1, source_target_pairs={{0,6},{1,7},{2,0},{3,1},{4,2},{5,3},{6,4},{7,5},{8,14},{9,15},{10,... | collective-permute-start | bytes 393224 | tf_op jit(solution)/shard_map/ppermute | solution.py:581
  33.2 4.4 %near.3.refs_3_ = bf16[3,512,512]{2,1,0:T(8,128)(2,1)S(1)} custom-call(s32[4]{0:T(128)S(1)} %pad_add_fusion.pos_ref, bf16[512,1024]{1,0:T(8,128)(2,1)S(1)} %bitcast.37, bf16[512,1024]{1,0:T(8,128)(2,1)S(1)} %bitcast.22, bf16[512,1024]{1,0:T(8,128)(2,1)S(1)} %bitcast.27, bf16[512,1024]{1,0:T(8,128)(2,1)S(1)} %bitcast.32), custom_call_target="tpu_custom_call" | custom-call | flops 1 | bytes 1 | tf_op jit(solution)/shard_map/near/pallas_call | solution.py:591
  40.1 8.2 %collective-permute-done.3.refs_3_ = bf16[512,128]{1,0:T(8,128)(2,1)S(1)} collective-permute-done((bf16[512,128]{1,0:T(8,128)(2,1)S(1)}, bf16[512,128]{1,0:T(8,128)(2,1)S(1)}, u32[]{:S(2)}, u32[]{:S(2)}) %collective-permute-start.3) | collective-permute-done | bytes 131104 | tf_op jit(solution)/shard_map/ppermute | solution.py:581
  51.2 1.8 %collective-permute-start.11 = (bf16[768,256]{1,0:T(8,128)(2,1)S(1)}, bf16[768,256]{1,0:T(8,128)(2,1)S(1)}, u32[]{:S(2)}, u32[]{:S(2)}) collective-permute-start(bf16[768,256]{1,0:T(8,128)(2,1)S(1)} %collective-permute-done.7.refs_3_.refs_5_.refs_17_.refs_19_), channel_id=1, source_target_pairs={{0,2},{1,3},{2,4},{3,5},{4,6},{5,7},{6,0},{7,1},{8,10},{9,11},{10,... | collective-permute-start | bytes 1179656 | tf_op jit(solution)/shard_map/ppermute | solution.py:642
  53.7 2.3 %collective-permute-done.10.refs_7_.refs_9_ = bf16[768,256]{1,0:T(8,128)(2,1)S(1)} collective-permute-done((bf16[768,256]{1,0:T(8,128)(2,1)S(1)}, bf16[768,256]{1,0:T(8,128)(2,1)S(1)}, u32[]{:S(2)}, u32[]{:S(2)}) %collective-permute-start.10) | collective-permute-done | bytes 393248 | tf_op jit(solution)/shard_map/ppermute | solution.py:84
  56.0 6.3 %collective-permute-done.9.refs_1_ = bf16[2,512,128]{2,1,0:T(8,128)(2,1)S(1)} collective-permute-done((bf16[2,512,128]{2,1,0:T(8,128)(2,1)S(1)}, bf16[2,512,128]{2,1,0:T(8,128)(2,1)S(1)}, u32[]{:S(2)}, u32[]{:S(2)}) %collective-permute-start.9) | collective-permute-done | bytes 262176 | tf_op jit(solution)/shard_map/ppermute | solution.py:631
  62.3 2.3 %collective-permute-done.11.refs_19_.refs_21_.refs_37_.refs_39_ = bf16[768,256]{1,0:T(8,128)(2,1)S(1)} collective-permute-done((bf16[768,256]{1,0:T(8,128)(2,1)S(1)}, bf16[768,256]{1,0:T(8,128)(2,1)S(1)}, u32[]{:S(2)}, u32[]{:S(2)}) %collective-permute-start.11) | collective-permute-done | bytes 393248 | tf_op jit(solution)/shard_map/ppermute | solution.py:642
  64.6 3.7 %far.1 = (bf16[512,3072]{1,0:T(8,128)(2,1)S(1)}, bf16[512,384]{1,0:T(8,128)(2,1)}) custom-call(s32[4]{0:T(128)S(1)} %pad_add_fusion.pos_ref, bf16[64,512]{1,0:T(8,128)(2,1)S(1)} %get-tuple-element.63.picks_ref, bf16[512,1024]{1,0:T(8,128)(2,1)S(1)} %bitcast.23, bf16[512,1024]{1,0:T(8,128)(2,1)S(1)} %bitcast.28, bf16[512,1024]{1,0:T(8,128)(2,1)S(1)} %bitcast.33, ...), custom_call_target="tpu_custom_call" | custom-call | flops 1 | bytes 1 | tf_op jit(solution)/shard_map/far/pallas_call | solution.py:657
  71.5 4.0 %all-to-all-start = ((bf16[32,16,384]{2,1,0:T(8,128)(2,1)}), bf16[32,16,384]{2,1,0:T(8,128)(2,1)S(1)}, u32[]{:S(2)}, u32[]{:S(2)}) async-start(bf16[32,16,384]{2,1,0:T(8,128)(2,1)} %bitcast.9), calls=%async_computation | async-start | bytes 786432 | tf_op jit(solution)/shard_map/all_to_all | solution.py:616
  75.4 1.8 %collective-permute-start.15 = (bf16[768,256]{1,0:T(8,128)(2,1)S(1)}, bf16[768,256]{1,0:T(8,128)(2,1)}, u32[]{:S(2)}, u32[]{:S(2)}) collective-permute-start(bf16[768,256]{1,0:T(8,128)(2,1)S(1)} %collective-permute-done.10.refs_7_.refs_9_), channel_id=1, source_target_pairs={{0,1},{1,0},{2,3},{3,2},{4,5},{5,4},{6,7},{7,6},{8,24},{9,25},{10,... | collective-permute-start | bytes 1179656 | tf_op jit(solution)/shard_map/ppermute | solution.py:84
  80.8 10.0 %collective-permute-done.15.refs_13_.refs_15_ = bf16[768,256]{1,0:T(8,128)(2,1)} collective-permute-done((bf16[768,256]{1,0:T(8,128)(2,1)S(1)}, bf16[768,256]{1,0:T(8,128)(2,1)}, u32[]{:S(2)}, u32[]{:S(2)}) %collective-permute-start.15) | collective-permute-done | bytes 393248 | tf_op jit(solution)/shard_map/ppermute | solution.py:84
  95.0 11.1 %collective-permute-start.18 = (bf16[768,256]{1,0:T(8,128)(2,1)S(1)}, bf16[768,256]{1,0:T(8,128)(2,1)S(1)}, u32[]{:S(2)}, u32[]{:S(2)}) collective-permute-start(bf16[768,256]{1,0:T(8,128)(2,1)S(1)} %collective-permute-done.8.refs_5_.refs_11_), channel_id=1, source_target_pairs={{0,8},{1,9},{2,10},{3,11},{4,12},{5,13},{6,14},{7,15},{8,0},{9,1},... | collective-permute-start | bytes 1179656 | tf_op jit(solution)/shard_map/ppermute | solution.py:84
  109.5 3.2 %all-to-all-start.1 = ((bf16[32,16,384]{2,1,0:T(8,128)(2,1)}), bf16[32,16,384]{2,1,0:T(8,128)(2,1)S(1)}, u32[]{:S(2)}, u32[]{:S(2)}) async-start(bf16[32,16,384]{2,1,0:T(8,128)(2,1)} %bitcast.11), calls=%async_computation.1 | async-start | bytes 786432 | tf_op jit(solution)/shard_map/all_to_all | solution.py:616
  113.3 5.5 %reach.1.back_ref = f32[768,64]{1,0:T(8,128)S(1)} custom-call(s32[4]{0:T(128)S(1)} %pad_add_fusion.pos_ref, bf16[512,384]{1,0:T(8,128)(2,1)S(1)} %bitcast.38, bf16[768,2048]{1,0:T(8,128)(2,1)} %bitcast.44, bf16[3072,256]{1,0:T(8,128)(2,1)} %copy-done.6, bf16[768,256]{1,0:T(8,128)(2,1)S(1)} %collective-permute-done.1.refs_1_.refs_3_, ...), custom_call_target="tpu_custom_call" | custom-call | flops 1 | bytes 1 | tf_op jit(solution)/shard_map/reach/pallas_call | solution.py:718
  119.0 4.4 %collective-permute-done.27.refs_15_.refs_17_.refs_29_.refs_31_ = bf16[768,256]{1,0:T(8,128)(2,1)} collective-permute-done((bf16[768,256]{1,0:T(8,128)(2,1)}, bf16[768,256]{1,0:T(8,128)(2,1)}, u32[]{:S(2)}, u32[]{:S(2)}) %collective-permute-start.27) | collective-permute-done | bytes 393248 | tf_op jit(solution)/shard_map/ppermute | solution.py:84
  126.3 9.7 %expert.1 = bf16[512,256]{1,0:T(8,128)(2,1)S(1)} custom-call(s32[4]{0:T(128)S(1)} %pad_add_fusion.pos_ref, bf16[512,384]{1,0:T(8,128)(2,1)S(1)} %bitcast.39, bf16[512,384]{1,0:T(8,128)(2,1)S(1)} %bitcast.41, f32[768,64]{1,0:T(8,128)S(1)} %reach.1.back_ref, bf16[2048,768]{1,0:T(8,128)(2,1)} %bitcast.46, bf16[2048,768]{1,0:T(8,128)(2,1)} %bitcast.47, ...), custom_call_target="tpu_custom_call" | custom-call | flops 1 | bytes 1 | tf_op jit(solution)/shard_map/expert/pallas_call | solution.py:740
  136.7 2.7 %all-to-all-start.2 = ((bf16[32,16,256]{2,1,0:T(8,128)(2,1)}), bf16[32,16,256]{2,1,0:T(8,128)(2,1)S(1)}, u32[]{:S(2)}, u32[]{:S(2)}) async-start(bf16[32,16,256]{2,1,0:T(8,128)(2,1)} %bitcast.42), calls=%async_computation.2 | async-start | bytes 524288 | tf_op jit(solution)/shard_map/all_to_all | solution.py:616
  139.5 14.1 %project.1.token_ref = bf16[512,2048]{1,0:T(8,128)(2,1)} custom-call(s32[4]{0:T(128)S(1)} %pad_add_fusion.pos_ref, bf16[512,3072]{1,0:T(8,128)(2,1)} %copy-done.13, bf16[3072,256]{1,0:T(8,128)(2,1)} %copy-done.6, bf16[768,256]{1,0:T(8,128)(2,1)S(1)} %collective-permute-done.1.refs_1_.refs_3_, bf16[768,256]{1,0:T(8,128)(2,1)S(1)} %collective-permute-done.5.refs_2_.refs_4_, ...), custom_call_target="tpu_custom_call" | custom-call | flops 1 | bytes 1 | tf_op jit(solution)/shard_map/project/pallas_call | solution.py:760
  155.2 2.8 %join.1 = bf16[512,2048]{1,0:T(8,128)(2,1)} custom-call(bf16[64,512]{1,0:T(8,128)(2,1)S(1)} %copy-done.19, bf16[512,256]{1,0:T(8,128)(2,1)S(1)} %bitcast.43, bf16[512,2048]{1,0:T(8,128)(2,1)S(1)} %copy-done.7), custom_call_target="tpu_custom_call" | custom-call | flops 1 | bytes 1 | tf_op jit(solution)/shard_map/join/pallas_call | solution.py:771
  (126 shorter events, 41.8 us)
Async XLA Ops:
  3.8 13.7 %collective-permute-start = (bf16[2,512,128]{2,1,0:T(8,128)(2,1)S(1)}, bf16[2,512,128]{2,1,0:T(8,128)(2,1)S(1)}, u32[]{:S(2)}, u32[]{:S(2)}) collective-permute-start(bf16[2,512,128]{2,1,0:T(8,128)(2,1)S(1)} %states.3), channel_id=1, source_target_pairs={{0,1},{1,0},{2,3},{3,2},{4,5},{5,4},{6,7},{7,6},{8,9},{9,8},{10,11... | collective-permute-start | bytes 786440 | tf_op jit(solution)/shard_map/ppermute | solution.py:549
  8.3 19.5 %collective-permute-start.1 = (bf16[768,256]{1,0:T(8,128)(2,1)}, bf16[768,256]{1,0:T(8,128)(2,1)S(1)}, u32[]{:S(2)}, u32[]{:S(2)}) collective-permute-start(bf16[768,256]{1,0:T(8,128)(2,1)} %turned.3), channel_id=1, source_target_pairs={{0,2},{1,3},{2,4},{3,5},{4,6},{5,7},{6,0},{7,1},{8,10},{9,11},{10,... | collective-permute-start | bytes 1179656 | tf_op jit(solution)/shard_map/ppermute | solution.py:552
  19.2 29.8 %collective-permute-start.6 = (bf16[1536,256]{1,0:T(8,128)(2,1)S(1)}, bf16[1536,256]{1,0:T(8,128)(2,1)}, u32[]{:S(2)}, u32[]{:S(2)}) collective-permute-start(bf16[1536,256]{1,0:T(8,128)(2,1)S(1)} %turned.5), channel_id=1, source_target_pairs={{8,9},{9,8},{10,11},{11,10},{12,13},{13,12},{14,15},{15,14},{24,25... | collective-permute-start | bytes 2359304 | tf_op jit(solution)/shard_map/ppermute | solution.py:84
  27.9 22.0 %collective-permute-start.8 = (bf16[768,256]{1,0:T(8,128)(2,1)S(1)}, bf16[768,256]{1,0:T(8,128)(2,1)S(1)}, u32[]{:S(2)}, u32[]{:S(2)}) collective-permute-start(bf16[768,256]{1,0:T(8,128)(2,1)S(1)} %collective-permute-done.1.refs_1_.refs_3_), channel_id=1, source_target_pairs={{0,16},{1,17},{2,18},{3,19},{4,20},{5,21},{6,22},{7,23},{8,9},{9,8... | collective-permute-start | bytes 1179656 | tf_op jit(solution)/shard_map/ppermute | solution.py:84
  29.4 20.5 %collective-permute-start.7 = (bf16[768,256]{1,0:T(8,128)(2,1)S(1)}, bf16[768,256]{1,0:T(8,128)(2,1)S(1)}, u32[]{:S(2)}, u32[]{:S(2)}) collective-permute-start(bf16[768,256]{1,0:T(8,128)(2,1)S(1)} %collective-permute-done.1.refs_1_.refs_3_), channel_id=1, source_target_pairs={{0,2},{1,3},{2,4},{3,5},{4,6},{5,7},{6,0},{7,1},{8,10},{9,11},{10,... | collective-permute-start | bytes 1179656 | tf_op jit(solution)/shard_map/ppermute | solution.py:609
  29.9 18.3 %collective-permute-start.3 = (bf16[512,128]{1,0:T(8,128)(2,1)S(1)}, bf16[512,128]{1,0:T(8,128)(2,1)S(1)}, u32[]{:S(2)}, u32[]{:S(2)}) collective-permute-start(bf16[512,128]{1,0:T(8,128)(2,1)S(1)} %get-tuple-element.74), channel_id=1, source_target_pairs={{0,4},{1,5},{2,6},{3,7},{4,0},{5,1},{6,2},{7,3},{8,12},{9,13},{10,... | collective-permute-start | bytes 393224 | tf_op jit(solution)/shard_map/ppermute | solution.py:581
  31.2 17.8 %collective-permute-start.4 = (bf16[512,128]{1,0:T(8,128)(2,1)S(1)}, bf16[512,128]{1,0:T(8,128)(2,1)S(1)}, u32[]{:S(2)}, u32[]{:S(2)}) collective-permute-start(bf16[512,128]{1,0:T(8,128)(2,1)S(1)} %get-tuple-element.75), channel_id=1, source_target_pairs={{0,6},{1,7},{2,0},{3,1},{4,2},{5,3},{6,4},{7,5},{8,14},{9,15},{10,... | collective-permute-start | bytes 393224 | tf_op jit(solution)/shard_map/ppermute | solution.py:581
  49.9 12.3 %collective-permute-start.13 = (bf16[768,256]{1,0:T(8,128)(2,1)S(1)}, bf16[768,256]{1,0:T(8,128)(2,1)S(1)}, u32[]{:S(2)}, u32[]{:S(2)}) collective-permute-start(bf16[768,256]{1,0:T(8,128)(2,1)S(1)} %collective-permute-done.7.refs_3_.refs_5_.refs_17_.refs_19_), channel_id=1, source_target_pairs={{0,16},{1,17},{2,18},{3,19},{4,20},{5,21},{6,22},{7,23},{8,9},{9,8... | collective-permute-start | bytes 1179656 | tf_op jit(solution)/shard_map/ppermute | solution.py:84
  51.2 13.3 %collective-permute-start.11 = (bf16[768,256]{1,0:T(8,128)(2,1)S(1)}, bf16[768,256]{1,0:T(8,128)(2,1)S(1)}, u32[]{:S(2)}, u32[]{:S(2)}) collective-permute-start(bf16[768,256]{1,0:T(8,128)(2,1)S(1)} %collective-permute-done.7.refs_3_.refs_5_.refs_17_.refs_19_), channel_id=1, source_target_pairs={{0,2},{1,3},{2,4},{3,5},{4,6},{5,7},{6,0},{7,1},{8,10},{9,11},{10,... | collective-permute-start | bytes 1179656 | tf_op jit(solution)/shard_map/ppermute | solution.py:642
  69.9 22.5 %collective-permute-start.17 = (bf16[1536,256]{1,0:T(8,128)(2,1)}, bf16[1536,256]{1,0:T(8,128)(2,1)}, u32[]{:S(2)}, u32[]{:S(2)}) collective-permute-start(bf16[1536,256]{1,0:T(8,128)(2,1)} %collective-permute-done.6.refs_17_.refs_33_), channel_id=1, source_target_pairs={{8,24},{9,25},{10,26},{11,27},{12,28},{13,29},{14,30},{15,31},{24,... | collective-permute-start | bytes 2359304 | tf_op jit(solution)/shard_map/ppermute | solution.py:84
  71.5 20.9 %all-to-all-start = ((bf16[32,16,384]{2,1,0:T(8,128)(2,1)}), bf16[32,16,384]{2,1,0:T(8,128)(2,1)S(1)}, u32[]{:S(2)}, u32[]{:S(2)}) async-start(bf16[32,16,384]{2,1,0:T(8,128)(2,1)} %bitcast.9), calls=%async_computation | async-start | bytes 786432 | tf_op jit(solution)/shard_map/all_to_all | solution.py:616
  75.4 15.3 %collective-permute-start.15 = (bf16[768,256]{1,0:T(8,128)(2,1)S(1)}, bf16[768,256]{1,0:T(8,128)(2,1)}, u32[]{:S(2)}, u32[]{:S(2)}) collective-permute-start(bf16[768,256]{1,0:T(8,128)(2,1)S(1)} %collective-permute-done.10.refs_7_.refs_9_), channel_id=1, source_target_pairs={{0,1},{1,0},{2,3},{3,2},{4,5},{5,4},{6,7},{7,6},{8,24},{9,25},{10,... | collective-permute-start | bytes 1179656 | tf_op jit(solution)/shard_map/ppermute | solution.py:84
  77.3 14.3 %collective-permute-start.16 = (bf16[768,256]{1,0:T(8,128)(2,1)S(1)}, bf16[768,256]{1,0:T(8,128)(2,1)S(1)}, u32[]{:S(2)}, u32[]{:S(2)}) collective-permute-start(bf16[768,256]{1,0:T(8,128)(2,1)S(1)} %collective-permute-done.12.refs_4_.refs_6_.refs_18_.refs_20_), channel_id=1, source_target_pairs={{0,16},{1,17},{2,18},{3,19},{4,20},{5,21},{6,22},{7,23},{8,9},{9,8... | collective-permute-start | bytes 1179656 | tf_op jit(solution)/shard_map/ppermute | solution.py:84
  78.7 27.3 %collective-permute-start.29 = (bf16[768,256]{1,0:T(8,128)(2,1)}, bf16[768,256]{1,0:T(8,128)(2,1)}, u32[]{:S(2)}, u32[]{:S(2)}) collective-permute-start(bf16[768,256]{1,0:T(8,128)(2,1)} %copy-done.23), channel_id=1, source_target_pairs={{0,16},{1,17},{2,18},{3,19},{4,20},{5,21},{6,22},{7,23},{8,9},{9,8... | collective-permute-start | bytes 1179656 | tf_op jit(solution)/shard_map/ppermute | solution.py:84
  79.3 26.9 %collective-permute-start.23 = (bf16[768,256]{1,0:T(8,128)(2,1)}, bf16[768,256]{1,0:T(8,128)(2,1)}, u32[]{:S(2)}, u32[]{:S(2)}) collective-permute-start(bf16[768,256]{1,0:T(8,128)(2,1)} %collective-permute-done.14.refs_20_.refs_22_.refs_38_.refs_40_), channel_id=1, source_target_pairs={{0,16},{1,17},{2,18},{3,19},{4,20},{5,21},{6,22},{7,23},{8,9},{9,8... | collective-permute-start | bytes 1179656 | tf_op jit(solution)/shard_map/ppermute | solution.py:84
  92.4 20.4 %collective-permute-start.21 = (bf16[1536,256]{1,0:T(8,128)(2,1)}, bf16[1536,256]{1,0:T(8,128)(2,1)}, u32[]{:S(2)}, u32[]{:S(2)}) collective-permute-start(bf16[1536,256]{1,0:T(8,128)(2,1)} %collective-permute-done.6.refs_17_.refs_33_), channel_id=1, source_target_pairs={{8,0},{9,1},{10,2},{11,3},{12,4},{13,5},{14,6},{15,7},{24,16},{25,... | collective-permute-start | bytes 2359304 | tf_op jit(solution)/shard_map/ppermute | solution.py:84
  93.7 19.4 %collective-permute-start.22 = (bf16[1536,256]{1,0:T(8,128)(2,1)}, bf16[1536,256]{1,0:T(8,128)(2,1)}, u32[]{:S(2)}, u32[]{:S(2)}) collective-permute-start(bf16[1536,256]{1,0:T(8,128)(2,1)} %collective-permute-done.17.refs_19_.refs_35_), channel_id=1, source_target_pairs={{8,0},{9,1},{10,2},{11,3},{12,4},{13,5},{14,6},{15,7},{24,16},{25,... | collective-permute-start | bytes 2359304 | tf_op jit(solution)/shard_map/ppermute | solution.py:84
  95.0 12.5 %collective-permute-start.18 = (bf16[768,256]{1,0:T(8,128)(2,1)S(1)}, bf16[768,256]{1,0:T(8,128)(2,1)S(1)}, u32[]{:S(2)}, u32[]{:S(2)}) collective-permute-start(bf16[768,256]{1,0:T(8,128)(2,1)S(1)} %collective-permute-done.8.refs_5_.refs_11_), channel_id=1, source_target_pairs={{0,8},{1,9},{2,10},{3,11},{4,12},{5,13},{6,14},{7,15},{8,0},{9,1},... | collective-permute-start | bytes 1179656 | tf_op jit(solution)/shard_map/ppermute | solution.py:84
  107.4 11.3 %collective-permute-start.24 = (bf16[768,256]{1,0:T(8,128)(2,1)}, bf16[768,256]{1,0:T(8,128)(2,1)}, u32[]{:S(2)}, u32[]{:S(2)}) collective-permute-start(bf16[768,256]{1,0:T(8,128)(2,1)} %collective-permute-done.23.refs_25_.refs_27_.refs_43_.refs_45_), channel_id=1, source_target_pairs={{0,1},{1,0},{2,3},{3,2},{4,5},{5,4},{6,7},{7,6},{8,24},{9,25},{10,... | collective-permute-start | bytes 1179656 | tf_op jit(solution)/shard_map/ppermute | solution.py:84
  108.6 14.9 %collective-permute-start.27 = (bf16[768,256]{1,0:T(8,128)(2,1)}, bf16[768,256]{1,0:T(8,128)(2,1)}, u32[]{:S(2)}, u32[]{:S(2)}) collective-permute-start(bf16[768,256]{1,0:T(8,128)(2,1)} %copy-done.24), channel_id=1, source_target_pairs={{0,1},{1,0},{2,3},{3,2},{4,5},{5,4},{6,7},{7,6},{8,24},{9,25},{10,... | collective-permute-start | bytes 1179656 | tf_op jit(solution)/shard_map/ppermute | solution.py:84
  109.5 14.0 %collective-permute-start.30 = (bf16[768,256]{1,0:T(8,128)(2,1)}, bf16[768,256]{1,0:T(8,128)(2,1)}, u32[]{:S(2)}, u32[]{:S(2)}) collective-permute-start(bf16[768,256]{1,0:T(8,128)(2,1)} %collective-permute-done.29.refs_23_.refs_29_.refs_41_.refs_47_), channel_id=1, source_target_pairs={{0,8},{1,9},{2,10},{3,11},{4,12},{5,13},{6,14},{7,15},{8,0},{9,1},... | collective-permute-start | bytes 1179656 | tf_op jit(solution)/shard_map/ppermute | solution.py:84
  109.5 16.8 %all-to-all-start.1 = ((bf16[32,16,384]{2,1,0:T(8,128)(2,1)}), bf16[32,16,384]{2,1,0:T(8,128)(2,1)S(1)}, u32[]{:S(2)}, u32[]{:S(2)}) async-start(bf16[32,16,384]{2,1,0:T(8,128)(2,1)} %bitcast.11), calls=%async_computation.1 | async-start | bytes 786432 | tf_op jit(solution)/shard_map/all_to_all | solution.py:616
  113.1 11.7 %collective-permute-start.26 = (bf16[768,256]{1,0:T(8,128)(2,1)}, bf16[768,256]{1,0:T(8,128)(2,1)}, u32[]{:S(2)}, u32[]{:S(2)}) collective-permute-start(bf16[768,256]{1,0:T(8,128)(2,1)} %copy-done.24), channel_id=1, source_target_pairs={{0,8},{1,9},{2,10},{3,11},{4,12},{5,13},{6,14},{7,15},{8,0},{9,1},... | collective-permute-start | bytes 1179656 | tf_op jit(solution)/shard_map/ppermute | solution.py:84
  136.7 16.9 %all-to-all-start.2 = ((bf16[32,16,256]{2,1,0:T(8,128)(2,1)}), bf16[32,16,256]{2,1,0:T(8,128)(2,1)S(1)}, u32[]{:S(2)}, u32[]{:S(2)}) async-start(bf16[32,16,256]{2,1,0:T(8,128)(2,1)} %bitcast.42), calls=%async_computation.2 | async-start | bytes 524288 | tf_op jit(solution)/shard_map/all_to_all | solution.py:616
  (42 other events, 455.4 us)
